TPU v7x, 32 devices: a whole 2x2x4 slice. The times are simulated.
32 devices in a mesh: dp: 16 (over z, y, x), tensor: 2 (over core).
Axes of the slice: x: 2, y: 2, z: 4, core: 2. Of those that a mesh axis runs over, the one named last changes fastest.
Arguments:
- layer_input: bfloat16 [32768, 1024], P(('dp', 'tensor')), may hold values from -6 to 6
- segment_ids: int32 [32768], P('dp'), may hold values from 0 to 2, as said below
- out_grad: bfloat16 [32768, 1024], P(('dp', 'tensor')), may hold values from -6 to 6
- norm_gain: float32 [1024], replicated, may hold values from 0.5 to 1.5
- query_w: bfloat16 [1024, 512], P('dp', 'tensor'), may hold values from -0.1875 to 0.1875
- key_w: bfloat16 [1024, 128], P('dp'), may hold values from -0.1875 to 0.1875
- value_w: bfloat16 [1024, 128], P('dp'), may hold values from -0.1875 to 0.1875
- out_w: bfloat16 [512, 1024], P('tensor', 'dp'), may hold values from -0.75 to 0.75
- mamba_gate_w: bfloat16 [1024, 1536], P('dp', 'tensor'), may hold values from -0.1875 to 0.1875
- mamba_in_w: bfloat16 [1024, 1536], P('dp', 'tensor'), may hold values from -0.1875 to 0.1875
- state_in_w: bfloat16 [1024, 256], P('dp'), may hold values from -0.1875 to 0.1875
- step_w: bfloat16 [1024, 24], P('dp', 'tensor'), may hold values from -0.1875 to 0.1875
- channel_conv: float32 [4, 1536], P(None, 'tensor'), may hold values from -3 to 3
- state_conv: float32 [4, 256], replicated, may hold values from -3 to 3
- step_bias: float32 [24], P('tensor'), may hold values from -4 to -1
- decay_log: float32 [24], P('tensor'), may hold values from -3 to 1
- skip_gain: float32 [24], P('tensor'), may hold values from 0.5 to 2
- mamba_out_w: bfloat16 [1536, 1024], P('tensor', 'dp'), may hold values from -0.0390625 to 0.0390625
- ffn_gain: float32 [1024], replicated, may hold values from 0.5 to 1.5
- ffn_gate_w: bfloat16 [1024, 2048], P('dp', 'tensor'), may hold values from -0.1875 to 0.1875
- ffn_up_w: bfloat16 [1024, 2048], P('dp', 'tensor'), may hold values from -0.1875 to 0.1875
- ffn_down_w: bfloat16 [2048, 1024], P('tensor', 'dp'), may hold values from -0.125 to 0.125
Outputs:
- block_out: bfloat16 [32768, 1024], P(('dp', 'tensor'))
- input_grad: float32 [32768, 1024], P(('dp', 'tensor'))
- norm_gain_grad: float32 [1024], replicated
- query_w_grad: float32 [1024, 512], P('dp', 'tensor')
- key_w_grad: float32 [1024, 128], P('dp')
- value_w_grad: float32 [1024, 128], P('dp')
- out_w_grad: float32 [512, 1024], P('tensor', 'dp')
- mamba_gate_w_grad: float32 [1024, 1536], P('dp', 'tensor')
- mamba_in_w_grad: float32 [1024, 1536], P('dp', 'tensor')
- state_in_w_grad: float32 [1024, 256], P('dp')
- step_w_grad: float32 [1024, 24], P('dp', 'tensor')
- channel_conv_grad: float32 [4, 1536], P(None, 'tensor')
- state_conv_grad: float32 [4, 256], replicated
- step_bias_grad: float32 [24], P('tensor')
- decay_log_grad: float32 [24], P('tensor')
- skip_gain_grad: float32 [24], P('tensor')
- mamba_out_w_grad: float32 [1536, 1024], P('tensor', 'dp')
- ffn_gain_grad: float32 [1024], replicated
- ffn_gate_w_grad: float32 [1024, 2048], P('dp', 'tensor')
- ffn_up_w_grad: float32 [1024, 2048], P('dp', 'tensor')
- ffn_down_w_grad: float32 [2048, 1024], P('tensor', 'dp')
Inputs may be any that keep to these rules, and one draw needn't show every extreme that they name: `segment_ids`: within each sequence of 2048 tokens the segment numbers start at 0, never fall, and rise by one at each of 2 document starts.
All inputs are finite; a program needn't handle non-finite values.
Results may differ from a plain program's by a relative error of at most 0.024.
Values may be sent and summed in bfloat16 or wider, within the bound.
No kernel may reach another device: no remote copies, remote signals or barrier semaphores. Data moves between devices by JAX's collectives and lax.ppermute only.
A program may use at most 512 MiB of HBM per device.

v0:
```python
import functools
import math

import jax
import jax.numpy as jnp
from jax import lax
from jax.experimental import pallas as pl
from jax.experimental.pallas import tpu as pltpu
from jax.sharding import PartitionSpec as P

HEAD_DIM = 64
STATE = 128
LEN = 2048
BQ = 512
Q = 128
HALO = 8
NEG = -1e30
PRECISE = lax.Precision.HIGHEST
F32 = jnp.float32
BF16 = jnp.bfloat16
VMEM_BYTES = 48 * 1024 * 1024


def dot_nn(left, right):
    return lax.dot_general(left, right, (((1,), (0,)), ((), ())), preferred_element_type=F32)


def dot_nt(left, right):
    return lax.dot_general(left, right, (((1,), (1,)), ((), ())), preferred_element_type=F32)


def dot_tn(left, right):
    return lax.dot_general(left, right, (((0,), (0,)), ((), ())), preferred_element_type=F32)


def pieces(a, count):
    parts = []
    for _ in range(count):
        parts.append(a.astype(BF16))
        a = a - parts[-1].astype(F32)
    return parts


def rope_kernel(heads, qkv_ref, cos_ref, sin_ref, q_ref, k_ref, v_ref):
    half = HEAD_DIM // 2
    cos, sin = cos_ref[...], sin_ref[...]

    def turn(x):
        return x * cos + jnp.concatenate([-x[:, half:], x[:, :half]], axis=1) * sin

    for h in range(heads):
        lanes = slice(h * HEAD_DIM, (h + 1) * HEAD_DIM)
        q_ref[:, lanes] = (turn(qkv_ref[:, lanes]).astype(BF16) * HEAD_DIM ** -0.5).astype(BF16)
    edge = heads * HEAD_DIM
    k_ref[...] = turn(qkv_ref[:, edge:edge + HEAD_DIM]).astype(BF16)
    v_ref[:, :HEAD_DIM] = qkv_ref[:, edge + HEAD_DIM:].astype(BF16)
    v_ref[:, HEAD_DIM:] = jnp.ones((v_ref.shape[0], HEAD_DIM), BF16)


def rope(qkv, cos, sin):
    rows, width = qkv.shape
    heads = width // HEAD_DIM - 2
    per = LEN // BQ
    blk = lambda w: pl.BlockSpec((BQ, w), lambda i: (i, 0))
    table = pl.BlockSpec((BQ, HEAD_DIM), lambda i: (lax.rem(i, per), 0))
    return pl.pallas_call(
        functools.partial(rope_kernel, heads),
        grid=(rows // BQ,),
        in_specs=[blk(width), table, table],
        out_specs=[blk(heads * HEAD_DIM), blk(HEAD_DIM), blk(2 * HEAD_DIM)],
        out_shape=[
            jax.ShapeDtypeStruct((rows, heads * HEAD_DIM), BF16),
            jax.ShapeDtypeStruct((rows, HEAD_DIM), BF16),
            jax.ShapeDtypeStruct((rows, 2 * HEAD_DIM), BF16),
        ],
        compiler_params=pltpu.CompilerParams(vmem_limit_bytes=VMEM_BYTES),
        cost_estimate=pl.CostEstimate(
            flops=rows * width * 8, bytes_accessed=rows * width * 6, transcendentals=0),
        name="rope",
    )(qkv, cos, sin)


def attend_fwd_kernel(heads, first_ref, q_ref, k_ref, v_ref, seg_ref, segrow_ref, out_ref, lse_ref,
                      top_ref, acc_ref):
    seq = pl.program_id(0)
    block = pl.program_id(1)
    top_ref[...] = jnp.full_like(top_ref, NEG)
    acc_ref[...] = jnp.zeros_like(acc_ref)
    key_pos = lax.broadcasted_iota(jnp.int32, (BQ, BQ), 0)
    row_pos = lax.broadcasted_iota(jnp.int32, (BQ, BQ), 1)

    def step(j, carry):
        at = pl.ds(pl.multiple_of(j * BQ, BQ), BQ)
        k = k_ref[at, :]
        v = v_ref[at, :]
        allowed = (segrow_ref[0] == seg_ref[at, :]) & (key_pos + (j - block) * BQ <= row_pos)
        bias = jnp.where(allowed, 0.0, NEG)
        for h in range(heads):
            s = dot_nt(k, q_ref[:, h * HEAD_DIM:(h + 1) * HEAD_DIM]) + bias
            old = top_ref[h]
            new = jnp.maximum(old, jnp.max(s, axis=0, keepdims=True))
            shrink = jnp.broadcast_to(jnp.exp(old - new), (2 * HEAD_DIM, BQ)).T
            p = jnp.exp(s - new).astype(BF16)
            acc_ref[h] = acc_ref[h] * shrink + dot_tn(p, v)
            top_ref[h] = new
        return carry

    lax.fori_loop(first_ref[seq * (LEN // BQ) + block], block + 1, step, 0)
    for h in range(heads):
        acc = acc_ref[h]
        out_ref[:, h * HEAD_DIM:(h + 1) * HEAD_DIM] = (
            acc[:, :HEAD_DIM] / acc[:, HEAD_DIM:]).astype(BF16)
        lse_ref[0, h:h + 1, :] = top_ref[h] + jnp.log(acc.T[HEAD_DIM:HEAD_DIM + 1, :])


def attend_fwd(first, q, k, v, seg_col, seg_rows):
    rows, width = q.shape
    heads = width // HEAD_DIM
    seqs = rows // LEN
    per = LEN // BQ
    return pl.pallas_call(
        functools.partial(attend_fwd_kernel, heads),
        grid_spec=pltpu.PrefetchScalarGridSpec(
            num_scalar_prefetch=1,
            grid=(seqs, per),
            in_specs=[
                pl.BlockSpec((BQ, width), lambda s, i, f: (s * per + i, 0)),
                pl.BlockSpec((LEN, HEAD_DIM), lambda s, i, f: (s, 0)),
                pl.BlockSpec((LEN, 2 * HEAD_DIM), lambda s, i, f: (s, 0)),
                pl.BlockSpec((LEN, 1), lambda s, i, f: (s, 0)),
                pl.BlockSpec((1, 1, BQ), lambda s, i, f: (s * per + i, 0, 0)),
            ],
            out_specs=[
                pl.BlockSpec((BQ, width), lambda s, i, f: (s * per + i, 0)),
                pl.BlockSpec((1, heads, BQ), lambda s, i, f: (s * per + i, 0, 0)),
            ],
            scratch_shapes=[
                pltpu.VMEM((heads, 1, BQ), F32),
                pltpu.VMEM((heads, BQ, 2 * HEAD_DIM), F32),
            ],
        ),
        out_shape=[
            jax.ShapeDtypeStruct((rows, width), BF16),
            jax.ShapeDtypeStruct((seqs * per, heads, BQ), F32),
        ],
        compiler_params=pltpu.CompilerParams(vmem_limit_bytes=VMEM_BYTES),
        cost_estimate=pl.CostEstimate(
            flops=2 * rows * LEN * width, bytes_accessed=4 * rows * width,
            transcendentals=rows * LEN * heads // 2),
        name="attend_fwd",
    )(first, q, k, v, seg_col, seg_rows)


def attend_bwd_kernel(heads, first_ref, q_ref, k_ref, v_ref, g_ref, seg_ref, segrow_ref, lse_ref,
                      out_ref, cos_ref, sin_ref, cosk_ref, sink_ref, dq_ref, dk_ref, dv_ref,
                      dqs_ref, dks_ref, dvs_ref, delta_ref):
    seq = pl.program_id(0)
    block = pl.program_id(1)
    half = HEAD_DIM // 2
    scale = HEAD_DIM ** -0.5

    @pl.when(block == 0)
    def _():
        dks_ref[...] = jnp.zeros_like(dks_ref)
        dvs_ref[...] = jnp.zeros_like(dvs_ref)

    dqs_ref[...] = jnp.zeros_like(dqs_ref)
    ones = jnp.ones((16, HEAD_DIM), BF16)
    high, less = pieces(g_ref[...].astype(F32) * out_ref[...].astype(F32), 2)
    for h in range(heads):
        lanes = slice(h * HEAD_DIM, (h + 1) * HEAD_DIM)
        delta_ref[h] = (dot_nt(ones, high[:, lanes]) + dot_nt(ones, less[:, lanes]))[0:1, :]
    key_pos = lax.broadcasted_iota(jnp.int32, (BQ, BQ), 0)
    row_pos = lax.broadcasted_iota(jnp.int32, (BQ, BQ), 1)

    def step(j, carry):
        at = pl.ds(pl.multiple_of(j * BQ, BQ), BQ)
        k = k_ref[at, :]
        v = v_ref[at, :HEAD_DIM]
        allowed = (segrow_ref[0] == seg_ref[at, :]) & (key_pos + (j - block) * BQ <= row_pos)
        bias = jnp.where(allowed, 0.0, NEG)
        dk = jnp.zeros((BQ, HEAD_DIM), F32)
        dv = jnp.zeros((BQ, HEAD_DIM), F32)
        for h in range(heads):
            lanes = slice(h * HEAD_DIM, (h + 1) * HEAD_DIM)
            q = q_ref[:, lanes]
            g = g_ref[:, lanes]
            s = dot_nt(k, q) + bias
            p = jnp.exp(s - lse_ref[0, h:h + 1, :])
            dp = dot_nt(v, g)
            ds = (p * (dp - delta_ref[h])).astype(BF16)
            dv = dv + dot_nn(p.astype(BF16), g)
            dk = dk + dot_nn(ds, q)
            dqs_ref[h] = dqs_ref[h] + dot_tn(ds, k)
        dks_ref[at, :] = dks_ref[at, :] + dk
        dvs_ref[at, :] = dvs_ref[at, :] + dv
        return carry

    lax.fori_loop(first_ref[seq * (LEN // BQ) + block], block + 1, step, 0)

    def turn_back(x, cos, sin):
        swapped = jnp.concatenate([x[:, half:], -x[:, :half]], axis=1)
        return x * cos + swapped * sin

    for h in range(heads):
        dq = turn_back(dqs_ref[h] * scale, cos_ref[...], sin_ref[...])
        dq_ref[:, h * HEAD_DIM:(h + 1) * HEAD_DIM] = dq.astype(BF16)

    @pl.when(block == pl.num_programs(1) - 1)
    def _():
        dk_ref[...] = turn_back(dks_ref[...], cosk_ref[...], sink_ref[...]).astype(BF16)
        dv_ref[...] = dvs_ref[...].astype(BF16)


def attend_bwd(first, q, k, v, g, seg_col, seg_rows, lse_rows, attended, cos, sin):
    rows, width = q.shape
    heads = width // HEAD_DIM
    seqs = rows // LEN
    per = LEN // BQ
    return pl.pallas_call(
        functools.partial(attend_bwd_kernel, heads),
        grid_spec=pltpu.PrefetchScalarGridSpec(
            num_scalar_prefetch=1,
            grid=(seqs, per),
            in_specs=[
                pl.BlockSpec((BQ, width), lambda s, i, f: (s * per + i, 0)),
                pl.BlockSpec((LEN, HEAD_DIM), lambda s, i, f: (s, 0)),
                pl.BlockSpec((LEN, 2 * HEAD_DIM), lambda s, i, f: (s, 0)),
                pl.BlockSpec((BQ, width), lambda s, i, f: (s * per + i, 0)),
                pl.BlockSpec((LEN, 1), lambda s, i, f: (s, 0)),
                pl.BlockSpec((1, 1, BQ), lambda s, i, f: (s * per + i, 0, 0)),
                pl.BlockSpec((1, heads, BQ), lambda s, i, f: (s * per + i, 0, 0)),
                pl.BlockSpec((BQ, width), lambda s, i, f: (s * per + i, 0)),
                pl.BlockSpec((BQ, HEAD_DIM), lambda s, i, f: (i, 0)),
                pl.BlockSpec((BQ, HEAD_DIM), lambda s, i, f: (i, 0)),
                pl.BlockSpec((LEN, HEAD_DIM), lambda s, i, f: (0, 0)),
                pl.BlockSpec((LEN, HEAD_DIM), lambda s, i, f: (0, 0)),
            ],
            out_specs=[
                pl.BlockSpec((BQ, width), lambda s, i, f: (s * per + i, 0)),
                pl.BlockSpec((LEN, HEAD_DIM), lambda s, i, f: (s, 0)),
                pl.BlockSpec((LEN, HEAD_DIM), lambda s, i, f: (s, 0)),
            ],
            scratch_shapes=[
                pltpu.VMEM((heads, BQ, HEAD_DIM), F32),
                pltpu.VMEM((LEN, HEAD_DIM), F32),
                pltpu.VMEM((LEN, HEAD_DIM), F32),
                pltpu.VMEM((heads, 1, BQ), F32),
            ],
        ),
        out_shape=[
            jax.ShapeDtypeStruct((rows, width), BF16),
            jax.ShapeDtypeStruct((rows, HEAD_DIM), BF16),
            jax.ShapeDtypeStruct((rows, HEAD_DIM), BF16),
        ],
        compiler_params=pltpu.CompilerParams(vmem_limit_bytes=VMEM_BYTES),
        cost_estimate=pl.CostEstimate(
            flops=5 * rows * LEN * width, bytes_accessed=8 * rows * width,
            transcendentals=rows * LEN * heads // 2),
        name="attend_bwd",
    )(first, q, k, v, g, seg_col, seg_rows, lse_rows, attended, cos, sin, cos, sin)


LAG, LEAD, CARRIED, ENDING = 0, 3, 6, 7


def token_masks(seg):
    seqs = seg.shape[0]
    padded = jnp.pad(seg, ((0, 0), (3, 3)), constant_values=-1)
    columns = [padded[:, 3 - k:3 - k + LEN] == seg for k in (1, 2, 3)]
    columns += [padded[:, 3 + k:3 + k + LEN] == seg for k in (1, 2, 3)]
    chunks = seg.reshape(seqs, LEN // Q, Q)
    prior = jnp.pad(chunks[:, :-1, -1:], ((0, 0), (1, 0), (0, 0)), constant_values=-1)
    columns.append((chunks == prior).reshape(seqs, LEN))
    columns.append((chunks == chunks[:, :, -1:]).reshape(seqs, LEN))
    return jnp.stack(columns, axis=-1).astype(F32).reshape(seqs * LEN, 8)


def shifted_conv(buf_ref, width, masks, taps):
    rows = [buf_ref[HALO - k:HALO - k + Q, :width] for k in range(4)]
    rows = [rows[0]] + [rows[k] * masks[:, LAG + k - 1:LAG + k] for k in (1, 2, 3)]
    total = rows[0] * taps[3:4, :]
    for k in (1, 2, 3):
        total = total + rows[k] * taps[3 - k:4 - k, :]
    return total, rows


def softplus(x):
    return jnp.maximum(x, 0.0) + jnp.log1p(jnp.exp(-jnp.abs(x)))


def spread_heads(columns, spread):
    stack = jnp.concatenate(columns, axis=0)
    high, less = pieces(stack, 2)
    wide = dot_nn(high, spread) + dot_nn(less, spread)
    return [wide[k * Q:(k + 1) * Q] for k in range(len(columns))]


def ones_times(ones, a, count):
    width = a.shape[1]
    total = dot_nn(ones, jnp.concatenate(pieces(a, count), axis=1))
    parts = [total[:, k * width:(k + 1) * width] for k in range(count)]
    return functools.reduce(jnp.add, parts)


def chunk_masks(seg_ref, segrow_ref):
    row = lax.broadcasted_iota(jnp.int32, (Q, Q), 0)
    col = lax.broadcasted_iota(jnp.int32, (Q, Q), 1)
    same = seg_ref[...] == segrow_ref[0]
    return row, col, same


def split_pre(ref, width):
    return (ref.at[:, pl.ds(0, width)], ref.at[:, pl.ds(width, width)],
            ref.at[:, pl.ds(2 * width, 3 * STATE)])


def mix_fwd_kernel(heads, seg_ref, segrow_ref, mask_ref, pre_ref, cw_ref,
                   sw_ref, bias_ref, rate_ref, skip_ref, spread_ref, gated_ref, y_ref, states_ref,
                   carry_ref, buf_ref, sbuf_ref):
    width = y_ref.shape[1]
    gate_ref, inner_ref, ss_ref = split_pre(pre_ref, width)

    @pl.when(pl.program_id(1) == 0)
    def _():
        carry_ref[...] = jnp.zeros_like(carry_ref)
        buf_ref[0:HALO, :] = jnp.zeros((HALO, buf_ref.shape[1]), F32)
        sbuf_ref[0:HALO, :] = jnp.zeros((HALO, sbuf_ref.shape[1]), F32)

    masks = mask_ref[...]
    buf_ref[HALO:HALO + Q, :] = inner_ref[...]
    sbuf_ref[HALO:HALO + Q, :] = ss_ref[:, :2 * STATE]
    z, _ = shifted_conv(buf_ref, buf_ref.shape[1], masks, cw_ref[...])
    zs, _ = shifted_conv(sbuf_ref, 2 * STATE, masks, sw_ref[...])
    buf_ref[0:HALO, :] = buf_ref[Q:Q + HALO, :]
    sbuf_ref[0:HALO, :] = sbuf_ref[Q:Q + HALO, :]
    x = z * jax.nn.sigmoid(z)
    states = (zs * jax.nn.sigmoid(zs)).astype(BF16)
    entry = states[:, :STATE]
    readout = states[:, STATE:]
    size = softplus(ss_ref[:, 2 * STATE:] + bias_ref[...])
    decay = -size * jnp.exp(rate_ref[...])
    row, col, same = chunk_masks(seg_ref, segrow_ref)
    cum = ones_times(jnp.where(row >= col, 1.0, 0.0).astype(BF16), decay, 3)
    cum_rows = cum.T
    bias = jnp.where((row >= col) & same, 0.0, NEG)
    spread = spread_ref[...]
    into = jnp.exp(cum) * masks[:, CARRIED:CARRIED + 1]
    tail = jnp.exp(cum[Q - 1:Q, :] - cum) * masks[:, ENDING:ENDING + 1]
    size_wide, into_wide, tail_wide = spread_heads([size, into, tail], spread)
    xs = (x * size_wide)
    xs_low = xs.astype(BF16)
    pair = dot_nt(readout, entry)
    prior = carry_ref[...]
    states_ref[0] = prior
    y = dot_nn(readout, prior.astype(BF16)) * into_wide
    for h in range(heads):
        lanes = slice(h * HEAD_DIM, (h + 1) * HEAD_DIM)
        mix = (pair * jnp.exp(cum[:, h:h + 1] - cum_rows[h:h + 1, :] + bias)).astype(BF16)
        y_ref[:, lanes] = dot_nn(mix, xs_low[:, lanes])
    y = y + y_ref[...]
    y_ref[...] = y
    fresh = dot_tn(entry, (xs * tail_wide).astype(BF16))
    carry_ref[...] = prior * into_wide[Q - 1:Q, :] + fresh
    gate = gate_ref[...]
    gated_ref[...] = ((y + skip_ref[...] * x) * (gate * jax.nn.sigmoid(gate))).astype(BF16)


def mix_fwd(seg_col, seg_rows, masks, pre, cw, sw, bias, rate, skip, spread,
            heads):
    rows, width = pre.shape[0], cw.shape[1]
    seqs = rows // LEN
    per = LEN // Q
    pre_width = pre.shape[1]
    blk = lambda w: pl.BlockSpec((Q, w), lambda s, c: (s * per + c, 0))
    whole = lambda a: pl.BlockSpec(a.shape, lambda s, c: (0, 0))
    return pl.pallas_call(
        functools.partial(mix_fwd_kernel, heads),
        grid=(seqs, per),
        in_specs=[
            blk(1),
            pl.BlockSpec((1, 1, Q), lambda s, c: (s * per + c, 0, 0)),
            blk(8), blk(pre_width),
            whole(cw), whole(sw), whole(bias), whole(rate), whole(skip), whole(spread),
        ],
        out_specs=[
            blk(width), blk(width),
            pl.BlockSpec((1, STATE, width), lambda s, c: (s * per + c, 0, 0)),
        ],
        out_shape=[
            jax.ShapeDtypeStruct((rows, width), BF16),
            jax.ShapeDtypeStruct((rows, width), F32),
            jax.ShapeDtypeStruct((seqs * per, STATE, width), F32),
        ],
        scratch_shapes=[
            pltpu.VMEM((STATE, width), F32),
            pltpu.VMEM((Q + HALO, width), F32),
            pltpu.VMEM((Q + HALO, 2 * STATE), F32),
        ],
        compiler_params=pltpu.CompilerParams(vmem_limit_bytes=VMEM_BYTES),
        cost_estimate=pl.CostEstimate(
            flops=rows * width * 1200, bytes_accessed=rows * width * 22,
            transcendentals=rows * width * 4),
        name="mix_fwd",
    )(seg_col, seg_rows, masks, pre, cw, sw, bias, rate, skip, spread)


def lead_sum(buf_ref, masks, taps):
    total = buf_ref[0:Q, :] * taps[3:4, :]
    for k in (1, 2, 3):
        total = total + buf_ref[k:k + Q, :] * masks[:, LEAD + k - 1:LEAD + k] * taps[3 - k:4 - k, :]
    return total


def column_sum(a):
    return jnp.sum(a, axis=0, keepdims=True)


def silu_slope(v, sig):
    return sig * (1.0 + v * (1.0 - sig))


def mix_bwd_kernel(heads, seg_ref, segrow_ref, mask_ref, pre_ref, pre_prev_ref, y_ref, states_ref, dout_ref, cw_ref, sw_ref, bias_ref, rate_ref,
                   skip_ref, spread_ref, dpre_ref, dcw_ref, dsw_ref, dhead_ref,
                   dskip_ref, carry_ref, buf_ref, sbuf_ref, dxs_ref, dz_ref, dzs_ref):
    width = y_ref.shape[1]
    gate_ref, inner_ref, ss_ref = split_pre(pre_ref, width)
    _, inner_prev_ref, ss_prev_ref = split_pre(pre_prev_ref, width)
    dgate_ref, dinner_ref, dss_ref = split_pre(dpre_ref, width)

    @pl.when((pl.program_id(0) == 0) & (pl.program_id(1) == 0))
    def _():
        dcw_ref[...] = jnp.zeros_like(dcw_ref)
        dsw_ref[...] = jnp.zeros_like(dsw_ref)
        dhead_ref[...] = jnp.zeros_like(dhead_ref)
        dskip_ref[...] = jnp.zeros_like(dskip_ref)

    @pl.when(pl.program_id(1) == 0)
    def _():
        carry_ref[...] = jnp.zeros_like(carry_ref)
        dz_ref[Q:Q + HALO, :] = jnp.zeros((HALO, width), F32)
        dzs_ref[Q:Q + HALO, :] = jnp.zeros((HALO, 2 * STATE), F32)

    masks = mask_ref[...]
    buf_ref[0:HALO, :] = inner_prev_ref[...]
    buf_ref[HALO:HALO + Q, :] = inner_ref[...]
    sbuf_ref[0:HALO, :] = ss_prev_ref[:, :2 * STATE]
    sbuf_ref[HALO:HALO + Q, :] = ss_ref[:, :2 * STATE]
    z, z_rows = shifted_conv(buf_ref, width, masks, cw_ref[...])
    zs, zs_rows = shifted_conv(sbuf_ref, 2 * STATE, masks, sw_ref[...])
    sig_z = jax.nn.sigmoid(z)
    sig_zs = jax.nn.sigmoid(zs)
    x = z * sig_z
    states = (zs * sig_zs).astype(BF16)
    entry = states[:, :STATE]
    readout = states[:, STATE:]
    raw = ss_ref[:, 2 * STATE:] + bias_ref[...]
    size = softplus(raw)
    rate = jnp.exp(rate_ref[...])
    decay = -size * rate
    row, col, same = chunk_masks(seg_ref, segrow_ref)
    cum = ones_times(jnp.where(row >= col, 1.0, 0.0).astype(BF16), decay, 3)
    cum_rows = cum.T
    bias = jnp.where((row <= col) & same, 0.0, NEG)
    spread = spread_ref[...]
    into = jnp.exp(cum) * masks[:, CARRIED:CARRIED + 1]
    tail = jnp.exp(cum[Q - 1:Q, :] - cum) * masks[:, ENDING:ENDING + 1]
    size_wide, into_wide, tail_wide = spread_heads([size, into, tail], spread)
    xs = x * size_wide
    xs_low = xs.astype(BF16)
    gate = gate_ref[...]
    sig = jax.nn.sigmoid(gate)
    dout = dout_ref[...]
    y = y_ref[...]
    skip = skip_ref[...]
    dgate_ref[...] = (dout * (y + skip * x) * silu_slope(gate, sig)).astype(BF16)
    g = dout * (gate * sig)
    g_low = g.astype(BF16)
    dskip_ref[...] += column_sum(g * x)
    pair = dot_nt(entry, readout)
    dpair = jnp.zeros((Q, Q), F32)
    for h in range(heads):
        lanes = slice(h * HEAD_DIM, (h + 1) * HEAD_DIM)
        fade = jnp.exp(cum_rows[h:h + 1, :] - cum[:, h:h + 1] + bias)
        dxs_ref[:, lanes] = dot_nn((pair * fade).astype(BF16), g_low[:, lanes])
        dpair = dpair + dot_nt(xs_low[:, lanes], g_low[:, lanes]) * fade
    prior = states_ref[0]
    after = carry_ref[...]
    after_low = after.astype(BF16)
    from_tail = dot_nn(entry, after_low) * tail_wide
    dxs = dxs_ref[...] + from_tail
    g_into = (g * into_wide).astype(BF16)
    dpair_low = dpair.astype(BF16)
    dreadout = dot_tn(dpair_low, entry) + dot_nt(g_into, prior.astype(BF16))
    dentry = dot_nn(dpair_low, readout) + dot_nt((xs * tail_wide).astype(BF16), after_low)
    keep = into_wide[Q - 1:Q, :]
    carry_ref[...] = after * keep + dot_tn(readout, g_into)
    xs_round = xs_low.astype(F32)
    end_sum = column_sum(xs_round * from_tail) + keep * column_sum(after * prior)
    terms = jnp.concatenate([
        g_low.astype(F32) * y - xs_round * dxs, x * dxs, jnp.broadcast_to(end_sum, (16, width))], axis=0)
    high, less = pieces(terms, 2)
    sums = dot_nt(high, spread) + dot_nt(less, spread)
    end_heads = sums[2 * Q:2 * Q + 1]
    last_row = lax.broadcasted_iota(jnp.int32, (Q, STATE), 0) == Q - 1
    dcum = sums[:Q] + jnp.where(last_row, end_heads, 0.0)
    ddecay = ones_times(jnp.where(row <= col, 1.0, 0.0).astype(BF16), dcum, 3)
    dsize = sums[Q:2 * Q] - ddecay * rate
    draw = dsize * jax.nn.sigmoid(raw)
    dhead_ref[0:1, :] += column_sum(draw)
    dhead_ref[1:2, :] += column_sum(ddecay * decay)
    dz = (size_wide * dxs + skip * g) * silu_slope(z, sig_z)
    dz_ref[0:Q, :] = dz
    for k in range(4):
        dcw_ref[3 - k:4 - k, :] += column_sum(dz * z_rows[k])
    dinner_ref[...] = lead_sum(dz_ref, masks, cw_ref[...]).astype(BF16)
    dz_ref[Q:Q + HALO, :] = dz_ref[0:HALO, :]
    dzs = jnp.concatenate([dentry, dreadout], axis=1) * silu_slope(zs, sig_zs)
    dzs_ref[0:Q, :] = dzs
    for k in range(4):
        dsw_ref[3 - k:4 - k, :] += column_sum(dzs * zs_rows[k])
    dss_ref[:, :2 * STATE] = lead_sum(dzs_ref, masks, sw_ref[...]).astype(BF16)
    dzs_ref[Q:Q + HALO, :] = dzs_ref[0:HALO, :]
    dss_ref[:, 2 * STATE:] = draw.astype(BF16)


def mix_bwd(seg_col, seg_rows, masks, pre, y, states, dout, cw, sw, bias, rate, skip, spread, heads):
    rows, width = pre.shape[0], cw.shape[1]
    seqs = rows // LEN
    per = LEN // Q
    pre_width = pre.shape[1]
    at = lambda s, c: s * per + per - 1 - c
    blk = lambda w: pl.BlockSpec((Q, w), lambda s, c: (at(s, c), 0))
    prev = lambda w: pl.BlockSpec(
        (HALO, w), lambda s, c: (jnp.maximum(at(s, c) * (Q // HALO) - 1, 0), 0))
    whole = lambda shape: pl.BlockSpec(shape, lambda s, c: (0, 0))
    return pl.pallas_call(
        functools.partial(mix_bwd_kernel, heads),
        grid=(seqs, per),
        in_specs=[
            blk(1),
            pl.BlockSpec((1, 1, Q), lambda s, c: (at(s, c), 0, 0)),
            blk(8), blk(pre_width), prev(pre_width), blk(width),
            pl.BlockSpec((1, STATE, width), lambda s, c: (at(s, c), 0, 0)),
            blk(width),
            whole(cw.shape), whole(sw.shape), whole(bias.shape), whole(rate.shape),
            whole(skip.shape), whole(spread.shape),
        ],
        out_specs=[
            blk(pre_width),
            whole((4, width)), whole((4, 2 * STATE)), whole((8, STATE)), whole((1, width)),
        ],
        out_shape=[
            jax.ShapeDtypeStruct((rows, pre_width), BF16),
            jax.ShapeDtypeStruct((4, width), F32),
            jax.ShapeDtypeStruct((4, 2 * STATE), F32),
            jax.ShapeDtypeStruct((8, STATE), F32),
            jax.ShapeDtypeStruct((1, width), F32),
        ],
        scratch_shapes=[
            pltpu.VMEM((STATE, width), F32),
            pltpu.VMEM((Q + HALO, width), F32),
            pltpu.VMEM((Q + HALO, 2 * STATE), F32),
            pltpu.VMEM((Q, width), F32),
            pltpu.VMEM((Q + HALO, width), F32),
            pltpu.VMEM((Q + HALO, 2 * STATE), F32),
        ],
        compiler_params=pltpu.CompilerParams(vmem_limit_bytes=VMEM_BYTES),
        cost_estimate=pl.CostEstimate(
            flops=rows * width * 3000, bytes_accessed=rows * width * 28,
            transcendentals=rows * width * 4),
        name="mix_bwd",
    )(seg_col, seg_rows, masks, pre, pre, y, states, dout, cw, sw, bias,
      rate, skip, spread)


NORM_EPS = 1e-05
ROPE_THETA = 100000000000.0
KV_HEADS = 2
HEADS = 8
LANES = 128


def permute_bit(x, axis, bit):
    n = lax.axis_size(axis)
    return lax.ppermute(x, axis, [(i, i ^ bit) for i in range(n)])


def bit_orders(axis):
    n = lax.axis_size(axis)
    bits = [n >> (k + 1) for k in range(n.bit_length() - 1)]
    rest = bits[1:]
    turn = lambda j: rest[j % len(rest):] + rest[:j % len(rest)] if rest else []
    return [bits[:1] + turn(j) for j in range(3)]


def gather_rel(piece, axis, order):
    held = piece[None]
    places = [0]
    for bit in order:
        before = held
        held = jnp.concatenate([held, permute_bit(held, axis, bit)], axis=0)
        places = places + [p ^ bit for p in places]
    return held, places, before


def assemble_kernel(plan, count, me_ref, *refs):
    sources = refs[:len(plan)]
    dests = refs[len(plan):len(plan) + count]
    sems = refs[-1]
    copies = []
    for j, (places, dest, row_off, lane_off, block_rows) in enumerate(plan):
        rows, width = sources[j].shape[1:]
        for p, place in enumerate(places):
            start = pl.multiple_of((me_ref[0] ^ place) * block_rows + row_off, 16)
            copies.append(pltpu.make_async_copy(
                sources[j].at[p],
                dests[dest].at[pl.ds(start, rows), pl.ds(lane_off, width)],
                sems.at[j, p]))
    for copy in copies:
        copy.start()
    for copy in copies:
        copy.wait()


def assemble(me, rels, plan, shapes):
    hbm = pl.BlockSpec(memory_space=pl.ANY)
    return pl.pallas_call(
        functools.partial(assemble_kernel, plan, len(shapes)),
        grid_spec=pltpu.PrefetchScalarGridSpec(
            num_scalar_prefetch=1,
            grid=(1,),
            in_specs=[hbm] * len(rels),
            out_specs=[hbm] * len(shapes),
            scratch_shapes=[pltpu.SemaphoreType.DMA((len(rels), rels[0].shape[0]))],
        ),
        out_shape=[jax.ShapeDtypeStruct(s, BF16) for s in shapes],
        compiler_params=pltpu.CompilerParams(vmem_limit_bytes=4 * 1024 * 1024),
        cost_estimate=pl.CostEstimate(
            flops=0, bytes_accessed=sum(4 * s[0] * s[1] for s in shapes), transcendentals=0),
        name="assemble",
    )(me, *rels)


def thirds(width):
    cuts = [0] + [min(width, -(-width * k // (3 * LANES)) * LANES) for k in (1, 2)] + [width]
    return [(a, b) for a, b in zip(cuts, cuts[1:]) if b > a]


def reduce_open(part, axis, row_off, row_count):
    n = lax.axis_size(axis)
    levels = n.bit_length() - 1
    own = part.shape[0] // n
    cur = part.reshape((2,) * levels + (own, part.shape[1]))
    if (row_off, row_count) != (0, own):
        cur = lax.slice_in_dim(cur, row_off, row_off + row_count, axis=levels)
    return cur


def reduce_halves(cur, axis, bit):
    mine = (lax.axis_index(axis) // bit) % 2
    dim = cur.ndim - 2 - bit.bit_length()
    return lax.dynamic_slice_in_dim(cur, mine, 1, dim), lax.dynamic_slice_in_dim(cur, 1 - mine, 1, dim)


def reduce_step(halves, axis, bit, last):
    keep, send = halves
    total = keep.astype(F32) + permute_bit(send, axis, bit).astype(F32)
    return total if last else total.astype(BF16)


def reduce_rest(cur, axis, order):
    for bit in reversed(order):
        cur = reduce_step(reduce_halves(cur, axis, bit), axis, bit, bit == order[0])
    return cur.reshape(cur.shape[-2:])


def sum_cube(x, axis):
    n = lax.axis_size(axis)
    bit = 1
    while bit < n:
        x = (x.astype(F32) + permute_bit(x, axis, bit).astype(F32)).astype(x.dtype)
        bit *= 2
    return x


def tensor_gather(x, natural):
    n = lax.axis_size("tensor")
    rank = lax.axis_index("tensor")
    bit = 1
    while bit < n:
        other = permute_bit(x, "tensor", bit)
        if natural:
            low = (rank // bit) % 2 == 0
            x = jnp.concatenate([jnp.where(low, x, other), jnp.where(low, other, x)], axis=0)
        else:
            x = jnp.concatenate([x, other], axis=0)
        bit *= 2
    return x


def tensor_scatter(product, arrays, natural):
    n = lax.axis_size("tensor")
    rank = lax.axis_index("tensor")
    if n == 2:
        half = arrays[0].shape[0] // 2
        cut = lambda a, k: lax.dynamic_slice_in_dim(a, k * half, half, 0) if natural else (
            lax.slice_in_dim(a, k * half, (k + 1) * half, axis=0))
        mine, other = (rank, 1 - rank) if natural else (0, 1)
        send = product(*[cut(a, other) for a in arrays]).astype(BF16)
        arrived = permute_bit(send, "tensor", 1)
        return product(*[cut(a, mine) for a in arrays]) + arrived.astype(F32)
    x = product(*arrays)
    bit = n // 2
    while bit >= 1:
        half = x.shape[0] // 2
        if natural:
            mine = (rank // bit) % 2
            keep = lax.dynamic_slice_in_dim(x, mine * half, half, 0)
            send = lax.dynamic_slice_in_dim(x, (1 - mine) * half, half, 0)
        else:
            keep, send = x[:half], x[half:]
        x = keep.astype(F32) + permute_bit(send.astype(BF16), "tensor", bit).astype(F32)
        bit //= 2
    return x


def inverse_rms(v):
    return lax.rsqrt(jnp.mean(v * v, axis=-1, keepdims=True) + NORM_EPS)


def norm_back(v, inverse, gain, grad):
    u = grad * gain
    into = inverse * u - inverse ** 3 * v * jnp.mean(u * v, axis=-1, keepdims=True)
    return into, jnp.sum(grad * v * inverse, axis=0)


def rope_tables():
    half = HEAD_DIM // 2
    index = (jnp.arange(HEAD_DIM, dtype=jnp.int32) % half).astype(F32)
    frequency = jnp.exp(index * (-2.0 * math.log(ROPE_THETA) / HEAD_DIM))
    angles = jnp.arange(LEN, dtype=jnp.int32).astype(F32)[:, None] * frequency[None, :]
    return jnp.cos(angles), jnp.sin(angles)


def per_device(
    layer_input, segment_ids, out_grad, norm_gain, query_w, key_w, value_w, out_w, mamba_gate_w,
    mamba_in_w, state_in_w, step_w, channel_conv, state_conv, step_bias, decay_log, skip_gain,
    mamba_out_w, ffn_gain, ffn_gate_w, ffn_up_w, ffn_down_w,
):
    dp = lax.axis_size("dp")
    rank = lax.axis_index("tensor")
    me = lax.axis_index("dp").astype(jnp.int32).reshape(1)
    heads = query_w.shape[1] // HEAD_DIM
    ssm = step_w.shape[1]
    width = mamba_in_w.shape[1]
    q_width = query_w.shape[1]
    units = ffn_gate_w.shape[1]
    kv_index = rank * heads // (HEADS // KV_HEADS)
    features = layer_input.shape[1]
    block_rows = query_w.shape[0]
    half_rows = block_rows // 2
    orders = bit_orders("dp")

    key_own = lax.dynamic_slice_in_dim(key_w, kv_index * HEAD_DIM, HEAD_DIM, 1)
    value_own = lax.dynamic_slice_in_dim(value_w, kv_index * HEAD_DIM, HEAD_DIM, 1)
    qkv_shard = jnp.concatenate([query_w, key_own, value_own], axis=1)
    mix_shard = jnp.concatenate(
        [mamba_gate_w, mamba_in_w, state_in_w, jnp.pad(step_w, ((0, 0), (0, STATE - ssm)))], axis=1)
    total_cols = mix_shard.shape[1] + qkv_shard.shape[1]
    mix_cols = thirds(total_cols)
    mix_cols = [(a, min(b, mix_shard.shape[1])) for a, b in mix_cols if a < mix_shard.shape[1]]
    rels, plan, befores = [], [], []
    for j, (a, b) in enumerate(mix_cols):
        rel, places, before = gather_rel(mix_shard[:, a:b], "dp", orders[j])
        rels.append(rel)
        befores.append(before)
        plan.append((places, 0, 0, a, block_rows))
    rel, places, before = gather_rel(qkv_shard, "dp", orders[2])
    rels.append(rel)
    befores.append(before)
    plan.append((places, 1, 0, 0, block_rows))
    mix_w, qkv_w = assemble(me, rels, plan, [(features, mix_shard.shape[1]),
                                            (features, qkv_shard.shape[1])])

    later = jnp.concatenate([ffn_gate_w, ffn_up_w, ffn_down_w.T], axis=1)
    later, _ = lax.optimization_barrier((later, tuple(befores)))
    later = lax.all_gather(later, "dp", axis=0, tiled=True)
    ffn_gate, ffn_up, ffn_down_t = (later[:, k * units:(k + 1) * units] for k in range(3))

    (out_shard, mout_shard), rels = lax.optimization_barrier(((out_w.T, mamba_out_w.T), tuple(rels)))
    rels2, plan2 = [], []
    for piece, dest, row_off, order in (
        (mout_shard[:half_rows], 1, 0, 0), (mout_shard[half_rows:], 1, half_rows, 1),
        (out_shard, 0, 0, 2),
    ):
        rel, places, _ = gather_rel(piece, "dp", orders[order])
        rels2.append(rel)
        plan2.append((places, dest, row_off, 0, block_rows))
    out_t, mout_t = assemble(me, rels2, plan2, [(features, q_width), (features, width)])

    tokens = layer_input.astype(F32)
    inverse = inverse_rms(tokens)
    normed = tensor_gather((tokens * inverse * norm_gain).astype(BF16), True)
    top_grad = tensor_gather(out_grad, False)
    rows = normed.shape[0]
    seqs = rows // LEN

    seg = segment_ids.reshape(seqs, LEN)
    seg_col = segment_ids[:, None]
    masks = token_masks(seg)
    starts = jnp.sum(seg[:, None, :] < seg[:, ::BQ, None], axis=-1, dtype=jnp.int32)
    first = (starts // BQ).reshape(-1)
    cos, sin = rope_tables()

    queries, key_rows, value_rows = rope(dot_nn(normed, qkv_w), cos, sin)
    seg_blocks = segment_ids.reshape(-1, 1, BQ)
    attended, lse = attend_fwd(first, queries, key_rows, value_rows, seg_col, seg_blocks)

    pre = dot_nn(normed, mix_w)
    pad_heads = lambda a: jnp.pad(a[None], ((0, 0), (0, STATE - ssm)))
    bias, rate = pad_heads(step_bias), pad_heads(decay_log)
    skip = jnp.repeat(skip_gain, HEAD_DIM)[None]
    spread = jnp.pad(jnp.repeat(jnp.eye(ssm, dtype=BF16), HEAD_DIM, axis=1), ((0, STATE - ssm), (0, 0)))
    chunk_rows = segment_ids.reshape(-1, 1, Q)
    gated, scanned, states = mix_fwd(
        seg_col, chunk_rows, masks, pre, channel_conv, state_conv, bias, rate, skip, spread, ssm)

    branch = tensor_scatter(
        lambda a, b: dot_nt(a, out_t) + dot_nt(b, mout_t), (attended, gated), True)
    middle = tokens + branch
    mid_inverse = inverse_rms(middle)
    mid = tensor_gather((middle * mid_inverse * ffn_gain).astype(BF16), False)
    gate_vals = dot_nn(mid, ffn_gate).astype(BF16).astype(F32)
    up_vals = dot_nn(mid, ffn_up).astype(BF16).astype(F32)
    act = (jax.nn.silu(gate_vals) * up_vals).astype(BF16)
    block_out = (middle + tensor_scatter(lambda a: dot_nt(a, ffn_down_t), (act,), False)).astype(BF16)

    act_grad = dot_nn(top_grad, ffn_down_t)
    gate_sig = jax.nn.sigmoid(gate_vals)
    gate_grad = (act_grad * up_vals * silu_slope(gate_vals, gate_sig)).astype(BF16)
    up_grad = (act_grad * (gate_vals * gate_sig)).astype(BF16)
    mid_norm_grad = tensor_scatter(
        lambda a, b: dot_nt(a, ffn_gate) + dot_nt(b, ffn_up), (gate_grad, up_grad), False)
    down_part = dot_tn(top_grad, act).astype(BF16)
    gate_part = dot_tn(mid, gate_grad).astype(BF16)
    up_part = dot_tn(mid, up_grad).astype(BF16)
    by_owner = lambda a: a.reshape(dp, block_rows, units)
    ffn_sum = lax.psum_scatter(
        jnp.concatenate([by_owner(gate_part), by_owner(up_part), by_owner(down_part)], axis=1),
        "dp", scatter_dimension=0, tiled=True)[0]
    ffn_gate_w_grad, ffn_up_w_grad, ffn_down_w_grad = (
        ffn_sum[k * block_rows:(k + 1) * block_rows].astype(F32) for k in range(3))

    mid_into, ffn_gain_part = norm_back(middle, mid_inverse, ffn_gain, mid_norm_grad)
    middle_grad = out_grad.astype(F32) + mid_into
    branch_grad = tensor_gather(middle_grad.astype(BF16), True)
    attended_grad = dot_nn(branch_grad, out_t).astype(BF16)
    gated_grad = dot_nn(branch_grad, mout_t)
    out_part = dot_tn(branch_grad, attended).astype(BF16)
    mout_part = dot_tn(branch_grad, gated).astype(BF16)
    pieces2 = [(mout_part, 0, half_rows, 0), (mout_part, half_rows, half_rows, 1),
               (out_part, 0, block_rows, 2)]
    halves2 = [
        reduce_halves(reduce_open(p, "dp", off, count), "dp", orders[j][-1]) for p, off, count, j in pieces2]
    attended_grad, halves2 = lax.optimization_barrier((attended_grad, halves2))
    held2 = [reduce_step(h, "dp", orders[p[3]][-1], False) for h, p in zip(halves2, pieces2)]
    query_grad, key_grad, value_grad = attend_bwd(
        first, queries, key_rows, value_rows, attended_grad, seg_col, seg_blocks, lse, attended, cos, sin)
    qkv_grad = jnp.concatenate([query_grad, key_grad, value_grad], axis=1)
    halves2 = [reduce_halves(c, "dp", orders[p[3]][-2]) for c, p in zip(held2, pieces2)]
    gated_grad, qkv_grad, halves2 = lax.optimization_barrier((gated_grad, qkv_grad, halves2))
    held2 = [reduce_step(h, "dp", orders[p[3]][-2], False) for h, p in zip(halves2, pieces2)]
    mix_grad, conv_part, state_conv_part, head_part, skip_part = mix_bwd(
        seg_col, chunk_rows, masks, pre, scanned, states, gated_grad, channel_conv, state_conv, bias,
        rate, skip, spread, ssm)

    pieces1 = [(dot_tn(normed, mix_grad[:, a:b]).astype(BF16), j) for j, (a, b) in enumerate(mix_cols)]
    pieces1.append((dot_tn(normed, qkv_grad).astype(BF16), 2))
    halves1 = [reduce_halves(reduce_open(p, "dp", 0, block_rows), "dp", orders[j][-1]) for p, j in pieces1]
    mix_grad_late, halves1 = lax.optimization_barrier((mix_grad, halves1))
    held1 = [reduce_step(h, "dp", orders[p[1]][-1], False) for h, p in zip(halves1, pieces1)]
    sums = [reduce_rest(c, "dp", orders[p[1]][:-1]) for c, p in zip(held1, pieces1)]
    mix_sum = jnp.concatenate(sums[:-1], axis=1)
    qkv_sum = sums[-1]
    mout_a, mout_b, out_sum = (
        reduce_rest(c, "dp", orders[p[3]][:-2]) for c, p in zip(held2, pieces2))
    mamba_out_w_grad = jnp.concatenate([mout_a, mout_b], axis=0).T
    out_w_grad = out_sum.T
    normed_grad = tensor_scatter(
        lambda a, b: dot_nt(a, qkv_w) + dot_nt(b, mix_w), (qkv_grad, mix_grad_late), True)
    norm_into, norm_gain_part = norm_back(tokens, inverse, norm_gain, normed_grad)
    input_grad = middle_grad + norm_into

    place = lambda a, whole: lax.dynamic_update_slice_in_dim(
        jnp.zeros((block_rows, whole.shape[1]), BF16), a.astype(BF16), kv_index * HEAD_DIM, 1)
    shared = sum_cube(jnp.concatenate([
        place(qkv_sum[:, q_width:q_width + HEAD_DIM], key_w),
        place(qkv_sum[:, q_width + HEAD_DIM:], value_w),
        mix_sum[:, 2 * width:2 * width + 2 * STATE].astype(BF16)], axis=1), "tensor").astype(F32)
    kv_cols = key_w.shape[1]

    heads_part = jnp.concatenate([
        head_part[0, :ssm], head_part[1, :ssm],
        jnp.sum(skip_part.reshape(ssm, HEAD_DIM), axis=1)])
    own = 4 * width + 3 * ssm
    small = sum_cube(jnp.concatenate([
        conv_part.reshape(-1), heads_part, state_conv_part.reshape(-1), ffn_gain_part,
        norm_gain_part]), "dp")
    conv_grad = small[:4 * width].reshape(4, width)
    bias_grad, decay_grad, skip_grad = (
        small[4 * width + k * ssm:4 * width + (k + 1) * ssm] for k in range(3))
    both = sum_cube(small[own:], "tensor")
    state_conv_grad = both[:8 * STATE].reshape(4, 2 * STATE)
    ffn_gain_grad = both[8 * STATE:8 * STATE + features]
    gain = both[8 * STATE + features:]
    return (
        block_out,
        input_grad,
        gain,
        qkv_sum[:, :q_width],
        shared[:, :kv_cols],
        shared[:, kv_cols:2 * kv_cols],
        out_w_grad,
        mix_sum[:, :width],
        mix_sum[:, width:2 * width],
        shared[:, 2 * kv_cols:],
        mix_sum[:, 2 * width + 2 * STATE:2 * width + 2 * STATE + ssm],
        conv_grad,
        state_conv_grad,
        bias_grad,
        decay_grad,
        skip_grad,
        mamba_out_w_grad,
        ffn_gain_grad,
        ffn_gate_w_grad,
        ffn_up_w_grad,
        ffn_down_w_grad.T,
    )


def solution(mesh):
    in_specs = (
        P(("dp", "tensor"), None),
        P("dp"),
        P(("dp", "tensor"), None),
        P(),
        P("dp", "tensor"),
        P("dp", None),
        P("dp", None),
        P("tensor", "dp"),
        P("dp", "tensor"),
        P("dp", "tensor"),
        P("dp", None),
        P("dp", "tensor"),
        P(None, "tensor"),
        P(),
        P("tensor"),
        P("tensor"),
        P("tensor"),
        P("tensor", "dp"),
        P(),
        P("dp", "tensor"),
        P("dp", "tensor"),
        P("tensor", "dp"),
    )
    out_specs = (
        P(("dp", "tensor"), None),
        P(("dp", "tensor"), None),
        P(),
        P("dp", "tensor"),
        P("dp", None),
        P("dp", None),
        P("tensor", "dp"),
        P("dp", "tensor"),
        P("dp", "tensor"),
        P("dp", None),
        P("dp", "tensor"),
        P(None, "tensor"),
        P(),
        P("tensor"),
        P("tensor"),
        P("tensor"),
        P("tensor", "dp"),
        P(),
        P("dp", "tensor"),
        P("dp", "tensor"),
        P("tensor", "dp"),
    )
    return jax.shard_map(
        per_device, mesh=mesh, in_specs=in_specs, out_specs=out_specs, check_vma=False
    )
```

profile of v0, /device:TPU:0, one launch (start us, length us, event | category | flops | bytes accessed | tf_op | source)
XLA Modules:
  0.0 609.3 jit_solution(1801371872333063776)
XLA Ops:
  9.6 4.0 collective-permute-start.13
  21.0 3.5 fusion.10
  27.3 5.3 multiply_sine_fusion
  81.1 4.1 collective-permute-done.12
  114.0 4.7 collective-permute-done.18
  126.7 3.3 collective-permute-done.28
  132.7 13.5 %fusion.98.pre_ref.pre_prev_ref = f32[2048,1920]{1,0:T(8,128)} fusion(bf16[1024,1920]{1,0:T(8,128)(2,1)S(1)} %get-tuple-element.76, bf16[1024,1024]{1,0:T(8,128)(2,1)S(1)} %get-tuple-element.239, bf16[1024,1024]{1,0:T(8,128)(2,1)S(1)} %get-tuple-element.238), kind=kOutput, calls=%fused_computation.289 | convolution fusion | flops 8061452288 | bytes 23855104 | tf_op jit(solution)/shard_map/dot_general | solution.py:25
  146.3 4.1 fusion.99.qkv_ref
  150.3 23.2 %mix_fwd.1 = (bf16[2048,768]{1,0:T(8,128)(2,1)S(1)}, f32[2048,768]{1,0:T(8,128)}, f32[16,128,768]{2,1,0:T(8,128)}) custom-call(s32[2048,1]{1,0:T(8,128)S(1)} %copy.102.seg_ref, s32[16,1,128]{2,1,0:T(1,128)S(1)} %bitcast.123, f32[2048,8]{1,0:T(8,128)S(1)} %convert_element_type.421.mask_ref, f32[2048,1920]{1,0:T(8,128)} %fusion.98.pre_ref.pre_prev_ref, ...), custom_call_target="tpu_custom_call" | custom-call | flops 1887436800 | bytes 34603008 | tf_op jit(solution)/shard_map/mix_fwd/pallas_call | solution.py:377
  173.6 6.1 %rope.1 = (bf16[2048,256]{1,0:T(8,128)(2,1)S(1)}, bf16[2048,64]{1,0:T(8,128)(2,1)S(1)}, bf16[2048,128]{1,0:T(8,128)(2,1)S(1)}) custom-call(f32[2048,384]{1,0:T(8,128)} %fusion.99.qkv_ref, f32[2048,64]{1,0:T(8,128)S(1)} %copy-done.3, f32[2048,64]{1,0:T(8,128)S(1)} %get-tuple-element.281.sin_ref.sink_ref), custom_call_target="tpu_custom_call" | custom-call | flops 6291456 | bytes 4718592 | tf_op jit(solution)/shard_map/rope/pallas_call | solution.py:66
  179.8 29.6 %attend_fwd.1 = (bf16[2048,256]{1,0:T(8,128)(2,1)S(1)}, f32[4,4,512]{2,1,0:T(4,128)S(1)}) custom-call(s32[4]{0:T(128)S(1)} %and_select_fusion.1.first_ref, bf16[2048,256]{1,0:T(8,128)(2,1)S(1)} %get-tuple-element.69.q_ref, bf16[2048,64]{1,0:T(8,128)(2,1)S(1)} %get-tuple-element.70.k_ref, bf16[2048,128]{1,0:T(8,128)(2,1)S(1)} %get-tuple-element.71.v_ref, ...), custom_call_target="tpu_custom_call" | custom-call | flops 2147483648 | bytes 2097152 | tf_op jit(solution)/shard_map/attend_fwd/pallas_call | solution.py:121
  209.5 3.9 assemble.3
  228.4 3.1 constant_dynamic-update-slice_fusion.36
  231.5 3.1 constant_dynamic-update-slice_fusion.35
  234.6 9.5 %convolution_convert_fusion.1 = bf16[2048,1024]{1,0:T(8,128)(2,1)} fusion(bf16[1024,3072]{1,0:T(8,128)(2,1)} %all-gather.2.cloned.1.call-done, bf16[1024,1024]{1,0:T(8,128)(2,1)} %collective-permute-done.30, bf16[1024,1024]{1,0:T(8,128)(2,1)} %multiply_convert_fusion.1), kind=kOutput, calls=%fused_computation.49 | convolution fusion | flops 4305453056 | bytes 10485760 | tf_op jit(solution)/shard_map/dot_general | solution.py:25
  244.1 8.5 %convolution_convert_fusion = bf16[2048,1024]{1,0:T(8,128)(2,1)} fusion(bf16[1024,3072]{1,0:T(8,128)(2,1)S(1)} %copy-done.57, bf16[1024,1024]{1,0:T(8,128)(2,1)} %collective-permute-done.30, bf16[1024,1024]{1,0:T(8,128)(2,1)} %multiply_convert_fusion.1), kind=kOutput, calls=%fused_computation.48 | convolution fusion | flops 4305453056 | bytes 10485760 | tf_op jit(solution)/shard_map/dot_general | solution.py:25
  252.6 13.8 %fusion.2 = (bf16[2048,1024]{1,0:T(8,128)(2,1)S(1)}, bf16[2048,1024]{1,0:T(8,128)(2,1)}, bf16[2048,1024]{1,0:T(8,128)(2,1)S(1)}) fusion(bf16[2048,1024]{1,0:T(8,128)(2,1)} %convolution_convert_fusion, bf16[2048,1024]{1,0:T(8,128)(2,1)} %convolution_convert_fusion.1, bf16[2048,1024]{1,0:T(8,128)(2,1)} %constant_dynamic-update-slice_fusion.35, ...), kind=kOutput, calls=%fused_computation.13 | convolution fusion | flops 4330618880 | bytes 27262976 | tf_op jit(solution)/shard_map/dot_general | solution.py:25
  266.4 5.5 fusion.25
  274.8 3.7 fusion.37
  278.7 4.4 fusion.29
  283.0 7.2 %convolution_convert_fusion.5 = bf16[1024,1024]{1,0:T(8,128)(2,1)S(1)} fusion(bf16[2048,1024]{1,0:T(8,128)(2,1)S(1)} %get-tuple-element.233, bf16[1024,1024]{1,0:T(8,128)(2,1)} %collective-permute-done.30, bf16[1024,1024]{1,0:T(8,128)(2,1)} %multiply_convert_fusion.1), kind=kOutput, calls=%fused_computation.74 | convolution fusion | flops 4304404480 | bytes 10485760 | tf_op jit(solution)/shard_map/dot_general | solution.py:33
  290.2 7.2 %convolution_convert_fusion.3 = bf16[1024,1024]{1,0:T(8,128)(2,1)S(1)} fusion(bf16[2048,1024]{1,0:T(8,128)(2,1)} %constant_dynamic-update-slice_fusion.35, bf16[2048,1024]{1,0:T(8,128)(2,1)S(1)} %copy-done.61), kind=kOutput, calls=%fused_computation.72 | convolution fusion | flops 4296015872 | bytes 10485760 | tf_op jit(solution)/shard_map/dot_general | solution.py:33
  297.4 5.7 multiply_reduce_fusion
  303.1 4.7 fusion.101
  308.2 7.0 %convolution_convert_fusion.4 = bf16[1024,1024]{1,0:T(8,128)(2,1)S(1)} fusion(bf16[2048,1024]{1,0:T(8,128)(2,1)S(1)} %copy-done.63, bf16[1024,1024]{1,0:T(8,128)(2,1)} %collective-permute-done.30, bf16[1024,1024]{1,0:T(8,128)(2,1)} %multiply_convert_fusion.1), kind=kOutput, calls=%fused_computation.73 | convolution fusion | flops 4304404480 | bytes 10485760 | tf_op jit(solution)/shard_map/dot_general | solution.py:33
  315.3 6.4 %pad_maximum_fusion = bf16[16,192,1024]{2,1,0:T(8,128)(2,1)} fusion(bf16[16,64,1024]{2,1,0:T(8,128)(2,1)S(1)} %bitcast.129, bf16[16,64,1024]{2,1,0:T(8,128)(2,1)S(1)} %bitcast.130, bf16[16,64,1024]{2,1,0:T(8,128)(2,1)S(1)} %bitcast.128), kind=kLoop, calls=%fused_computation.20 | loop fusion | flops 18874368 | bytes 12582912 | tf_op jit(solution)/shard_map/concatenate | solution.py:850
  321.7 7.8 %add_convert_fusion.2 = bf16[1024,1024]{1,0:T(8,128)(2,1)} fusion(f32[1024,1024]{1,0:T(8,128)} %copy-done.29, bf16[1024,1024]{1,0:T(8,128)(2,1)} %collective-permute-done.31, bf16[1024,3072]{1,0:T(8,128)(2,1)} %all-gather.2.cloned.1.call-done, bf16[2048,1024]{1,0:T(8,128)(2,1)} %copy-done.60), kind=kOutput, calls=%fused_computation.40 | convolution fusion | flops 2151677952 | bytes 12582912 | tf_op jit(solution)/shard_map/dot_general | solution.py:29
  334.0 3.7 convolution_convert_fusion.6
  339.0 7.0 %fusion.97.dout_ref = f32[2048,768]{1,0:T(8,128)} fusion(bf16[1024,768]{1,0:T(8,128)(2,1)S(1)} %get-tuple-element.78, bf16[1024,1024]{1,0:T(8,128)(2,1)S(1)} %get-tuple-element.237, bf16[1024,1024]{1,0:T(8,128)(2,1)S(1)} %get-tuple-element.236), kind=kOutput, calls=%fused_computation.288 | convolution fusion | flops 3229614080 | bytes 12058624 | tf_op jit(solution)/shard_map/dot_general | solution.py:25
  347.5 42.9 %attend_bwd.1 = (bf16[2048,256]{1,0:T(8,128)(2,1)S(1)}, bf16[2048,64]{1,0:T(8,128)(2,1)S(1)}, bf16[2048,64]{1,0:T(8,128)(2,1)S(1)}) custom-call(s32[4]{0:T(128)S(1)} %and_select_fusion.1.first_ref, bf16[2048,256]{1,0:T(8,128)(2,1)S(1)} %copy-done.21, bf16[2048,64]{1,0:T(8,128)(2,1)S(1)} %copy-done.23, bf16[2048,128]{1,0:T(8,128)(2,1)S(1)} %copy-done.25, ...), custom_call_target="tpu_custom_call" | custom-call | flops 5368709120 | bytes 4194304 | tf_op jit(solution)/shard_map/attend_bwd/pallas_call | solution.py:220
  392.7 55.9 %mix_bwd.1 = (bf16[2048,1920]{1,0:T(8,128)(2,1)}, f32[4,768]{1,0:T(4,128)S(1)}, f32[4,256]{1,0:T(4,128)S(1)}, f32[8,128]{1,0:T(8,128)S(1)}, f32[1,768]{1,0:T(1,128)S(1)}) custom-call(s32[2048,1]{1,0:T(8,128)S(1)} %copy-done.1, s32[16,1,128]{2,1,0:T(1,128)S(1)} %bitcast.126, f32[2048,8]{1,0:T(8,128)S(1)} %convert_element_type.421.mask_ref, ...), custom_call_target="tpu_custom_call" | custom-call | flops 4718592000 | bytes 44040192 | tf_op jit(solution)/shard_map/mix_bwd/pallas_call | solution.py:537
  448.6 4.0 fusion.66
  452.6 3.6 fusion.43
  456.3 3.7 fusion.40
  469.6 4.8 fusion.17
  477.0 6.1 %fusion.19 = f32[1024,1024]{1,0:T(8,128)} fusion(bf16[1024,1920]{1,0:T(8,128)(2,1)S(1)} %copy-done.16, bf16[2048,1920]{1,0:T(8,128)(2,1)S(1)} %copy-done.56, s32[]{:T(128)S(6)} %select_n.259), kind=kOutput, calls=%fused_computation.46 | convolution fusion | flops 4026531840 | bytes 12058628 | tf_op jit(solution)/shard_map/dot_general | solution.py:29
  483.1 3.3 fusion.74
  486.4 3.1 collective-permute-done.53
  490.9 3.0 collective-permute-done.54
  502.6 4.0 collective-permute-done.65
  507.1 7.4 %collective-permute-done.68 = bf16[2,1,1,1,32,768]{5,4,3,2,1,0:T(8,128)(2,1)S(1)} collective-permute-done((bf16[2,1,1,1,32,768]{5,4,3,2,1,0:T(8,128)(2,1)S(1)}, bf16[2,1,1,1,32,768]{5,4,3,2,1,0:T(8,128)(2,1)S(1)}, u32[]{:S(2)}, u32[]{:S(2)}) %collective-permute-start.68) | collective-permute-done | bytes 98336 | tf_op jit(solution)/shard_map/ppermute | solution.py:586
  515.9 3.6 collective-permute-done.66
  521.2 3.3 collective-permute-done.69
  527.7 5.5 collective-permute-done.45
  555.5 7.0 %collective-permute-done.61 = bf16[2,1,2,1,64,768]{5,4,3,2,1,0:T(8,128)(2,1)S(1)} collective-permute-done((bf16[2,1,2,1,64,768]{5,4,3,2,1,0:T(8,128)(2,1)S(1)}, bf16[2,1,2,1,64,768]{5,4,3,2,1,0:T(8,128)(2,1)S(1)}, u32[]{:S(2)}, u32[]{:S(2)}) %collective-permute-start.61) | collective-permute-done | bytes 393248 | tf_op jit(solution)/shard_map/ppermute | solution.py:586
  566.0 3.6 collective-permute-done.62
  572.9 4.9 fusion.16
  591.6 5.4 fusion.13
  (455 shorter events, 204.7 us)
Async XLA Ops:
  7.2 227.4 %all-gather.2.cloned.1.call-start = ((), (), s32[]{:S(2)}) async-start(), calls=%async_computation.1 | async-start | bytes 6684672 | tf_op jit(solution)/shard_map/all_gather | solution.py:788
  9.6 25.4 %collective-permute-start.13 = (bf16[1,64,384]{2,1,0:T(8,128)(2,1)}, bf16[1,64,384]{2,1,0:T(8,128)(2,1)}, u32[]{:S(2)}, u32[]{:S(2)}) collective-permute-start(bf16[1,64,384]{2,1,0:T(8,128)(2,1)} %get-tuple-element.232), channel_id=1, source_target_pairs={{0,16},{2,18},{4,20},{6,22},{8,24},{10,26},{12,28},{14,30},{16,0},... | collective-permute-start | bytes 147464 | tf_op jit(solution)/shard_map/ppermute | solution.py:586
  15.2 22.4 %collective-permute-start.9 = (bf16[1,64,384]{2,1,0:T(8,128)(2,1)S(1)}, bf16[1,64,384]{2,1,0:T(8,128)(2,1)}, u32[]{:S(2)}, u32[]{:S(2)}) collective-permute-start(bf16[1,64,384]{2,1,0:T(8,128)(2,1)S(1)} %fusion.84), channel_id=1, source_target_pairs={{0,16},{2,18},{4,20},{6,22},{8,24},{10,26},{12,28},{14,30},{16,0},... | collective-permute-start | bytes 147464 | tf_op jit(solution)/shard_map/ppermute | solution.py:586
  15.2 26.5 %collective-permute-start.5 = (bf16[1,64,768]{2,1,0:T(8,128)(2,1)}, bf16[1,64,768]{2,1,0:T(8,128)(2,1)}, u32[]{:S(2)}, u32[]{:S(2)}) collective-permute-start(bf16[1,64,768]{2,1,0:T(8,128)(2,1)} %bitcast.134), channel_id=1, source_target_pairs={{0,16},{2,18},{4,20},{6,22},{8,24},{10,26},{12,28},{14,30},{16,0},... | collective-permute-start | bytes 294920 | tf_op jit(solution)/shard_map/ppermute | solution.py:586
  18.1 26.3 %collective-permute-start.1 = (bf16[1,64,768]{2,1,0:T(8,128)(2,1)}, bf16[1,64,768]{2,1,0:T(8,128)(2,1)}, u32[]{:S(2)}, u32[]{:S(2)}) collective-permute-start(bf16[1,64,768]{2,1,0:T(8,128)(2,1)} %bitcast.138), channel_id=1, source_target_pairs={{0,16},{2,18},{4,20},{6,22},{8,24},{10,26},{12,28},{14,30},{16,0},... | collective-permute-start | bytes 294920 | tf_op jit(solution)/shard_map/ppermute | solution.py:586
  24.5 105.6 %collective-permute-start = (bf16[1024,1024]{1,0:T(8,128)(2,1)}, bf16[1024,1024]{1,0:T(8,128)(2,1)}, u32[]{:S(2)}, u32[]{:S(2)}) collective-permute-start(bf16[1024,1024]{1,0:T(8,128)(2,1)} %fusion.10), channel_id=1, source_target_pairs={{0,1},{1,0},{2,3},{3,2},{4,5},{5,4},{6,7},{7,6},{8,9},{9,8},{10,11... | collective-permute-start | bytes 6291464 | tf_op jit(solution)/shard_map/ppermute | solution.py:586
  35.9 14.2 %collective-permute-start.14 = (bf16[2,64,384]{2,1,0:T(8,128)(2,1)S(1)}, bf16[2,64,384]{2,1,0:T(8,128)(2,1)S(1)}, u32[]{:S(2)}, u32[]{:S(2)}) collective-permute-start(bf16[2,64,384]{2,1,0:T(8,128)(2,1)S(1)} %pad_maximum_fusion.23), channel_id=1, source_target_pairs={{0,2},{2,0},{4,6},{6,4},{8,10},{10,8},{12,14},{14,12},{16,18},{18,... | collective-permute-start | bytes 294920 | tf_op jit(solution)/shard_map/ppermute | solution.py:586
  38.5 13.0 %collective-permute-start.10 = (bf16[2,64,384]{2,1,0:T(8,128)(2,1)S(1)}, bf16[2,64,384]{2,1,0:T(8,128)(2,1)S(1)}, u32[]{:S(2)}, u32[]{:S(2)}) collective-permute-start(bf16[2,64,384]{2,1,0:T(8,128)(2,1)S(1)} %pad_maximum_fusion.22), channel_id=1, source_target_pairs={{0,2},{2,0},{4,6},{6,4},{8,10},{10,8},{12,14},{14,12},{16,18},{18,... | collective-permute-start | bytes 294920 | tf_op jit(solution)/shard_map/ppermute | solution.py:586
  42.7 12.6 %collective-permute-start.6 = (bf16[2,64,768]{2,1,0:T(8,128)(2,1)S(1)}, bf16[2,64,768]{2,1,0:T(8,128)(2,1)S(1)}, u32[]{:S(2)}, u32[]{:S(2)}) collective-permute-start(bf16[2,64,768]{2,1,0:T(8,128)(2,1)S(1)} %pad_maximum_fusion.16), channel_id=1, source_target_pairs={{0,4},{2,6},{4,0},{6,2},{8,12},{10,14},{12,8},{14,10},{16,20},{18,... | collective-permute-start | bytes 589832 | tf_op jit(solution)/shard_map/ppermute | solution.py:586
  45.4 12.4 %collective-permute-start.2 = (bf16[2,64,768]{2,1,0:T(8,128)(2,1)S(1)}, bf16[2,64,768]{2,1,0:T(8,128)(2,1)S(1)}, u32[]{:S(2)}, u32[]{:S(2)}) collective-permute-start(bf16[2,64,768]{2,1,0:T(8,128)(2,1)S(1)} %pad_maximum_fusion.15), channel_id=1, source_target_pairs={{0,8},{2,10},{4,12},{6,14},{8,0},{10,2},{12,4},{14,6},{16,24},{18,... | collective-permute-start | bytes 589832 | tf_op jit(solution)/shard_map/ppermute | solution.py:586
  50.9 9.7 %collective-permute-start.15 = (bf16[4,64,384]{2,1,0:T(8,128)(2,1)S(1)}, bf16[4,64,384]{2,1,0:T(8,128)(2,1)S(1)}, u32[]{:S(2)}, u32[]{:S(2)}) collective-permute-start(bf16[4,64,384]{2,1,0:T(8,128)(2,1)S(1)} %pad_maximum_fusion.18), channel_id=1, source_target_pairs={{0,8},{2,10},{4,12},{6,14},{8,0},{10,2},{12,4},{14,6},{16,24},{18,... | collective-permute-start | bytes 589832 | tf_op jit(solution)/shard_map/ppermute | solution.py:586
  52.3 11.5 %collective-permute-start.11 = (bf16[4,64,384]{2,1,0:T(8,128)(2,1)S(1)}, bf16[4,64,384]{2,1,0:T(8,128)(2,1)S(1)}, u32[]{:S(2)}, u32[]{:S(2)}) collective-permute-start(bf16[4,64,384]{2,1,0:T(8,128)(2,1)S(1)} %pad_maximum_fusion.17), channel_id=1, source_target_pairs={{0,8},{2,10},{4,12},{6,14},{8,0},{10,2},{12,4},{14,6},{16,24},{18,... | collective-permute-start | bytes 589832 | tf_op jit(solution)/shard_map/ppermute | solution.py:586
  56.2 9.9 %collective-permute-start.7 = (bf16[4,64,768]{2,1,0:T(8,128)(2,1)S(1)}, bf16[4,64,768]{2,1,0:T(8,128)(2,1)S(1)}, u32[]{:S(2)}, u32[]{:S(2)}) collective-permute-start(bf16[4,64,768]{2,1,0:T(8,128)(2,1)S(1)} %pad_maximum_fusion.8), channel_id=1, source_target_pairs={{0,2},{2,0},{4,6},{6,4},{8,10},{10,8},{12,14},{14,12},{16,18},{18,... | collective-permute-start | bytes 1179656 | tf_op jit(solution)/shard_map/ppermute | solution.py:586
  58.7 12.1 %collective-permute-start.3 = (bf16[4,64,768]{2,1,0:T(8,128)(2,1)S(1)}, bf16[4,64,768]{2,1,0:T(8,128)(2,1)S(1)}, u32[]{:S(2)}, u32[]{:S(2)}) collective-permute-start(bf16[4,64,768]{2,1,0:T(8,128)(2,1)S(1)} %pad_maximum_fusion.7), channel_id=1, source_target_pairs={{0,4},{2,6},{4,0},{6,2},{8,12},{10,14},{12,8},{14,10},{16,20},{18,... | collective-permute-start | bytes 1179656 | tf_op jit(solution)/shard_map/ppermute | solution.py:586
  62.3 17.1 %collective-permute-start.16 = (bf16[8,64,384]{2,1,0:T(8,128)(2,1)}, bf16[8,64,384]{2,1,0:T(8,128)(2,1)}, u32[]{:S(2)}, u32[]{:S(2)}) collective-permute-start(bf16[8,64,384]{2,1,0:T(8,128)(2,1)} %pad_maximum_fusion.10), channel_id=1, source_target_pairs={{0,4},{2,6},{4,0},{6,2},{8,12},{10,14},{12,8},{14,10},{16,20},{18,... | collective-permute-start | bytes 1179656 | tf_op jit(solution)/shard_map/ppermute | solution.py:586
  65.4 19.9 %collective-permute-start.12 = (bf16[8,64,384]{2,1,0:T(8,128)(2,1)}, bf16[8,64,384]{2,1,0:T(8,128)(2,1)}, u32[]{:S(2)}, u32[]{:S(2)}) collective-permute-start(bf16[8,64,384]{2,1,0:T(8,128)(2,1)} %pad_maximum_fusion.9), channel_id=1, source_target_pairs={{0,4},{2,6},{4,0},{6,2},{8,12},{10,14},{12,8},{14,10},{16,20},{18,... | collective-permute-start | bytes 1179656 | tf_op jit(solution)/shard_map/ppermute | solution.py:586
  68.0 19.1 %collective-permute-start.8 = (bf16[8,64,768]{2,1,0:T(8,128)(2,1)}, bf16[8,64,768]{2,1,0:T(8,128)(2,1)}, u32[]{:S(2)}, u32[]{:S(2)}) collective-permute-start(bf16[8,64,768]{2,1,0:T(8,128)(2,1)} %pad_maximum_fusion.6), channel_id=1, source_target_pairs={{0,8},{2,10},{4,12},{6,14},{8,0},{10,2},{12,4},{14,6},{16,24},{18,... | collective-permute-start | bytes 2359304 | tf_op jit(solution)/shard_map/ppermute | solution.py:586
  72.8 17.8 %collective-permute-start.4 = (bf16[8,64,768]{2,1,0:T(8,128)(2,1)}, bf16[8,64,768]{2,1,0:T(8,128)(2,1)}, u32[]{:S(2)}, u32[]{:S(2)}) collective-permute-start(bf16[8,64,768]{2,1,0:T(8,128)(2,1)} %pad_maximum_fusion.5), channel_id=1, source_target_pairs={{0,2},{2,0},{4,6},{6,4},{8,10},{10,8},{12,14},{14,12},{16,18},{18,... | collective-permute-start | bytes 2359304 | tf_op jit(solution)/shard_map/ppermute | solution.py:586
  74.7 525.4 %reduce-scatter.2.cloned.1.call-start = ((), (), s32[]{:S(2)}) async-start(), calls=%async_computation.2 | async-start | bytes 6684672 | tf_op jit(solution)/shard_map/reduce_scatter | solution.py:849
  92.7 11.1 %collective-permute-start.25 = (bf16[1,64,256]{2,1,0:T(8,128)(2,1)S(1)}, bf16[1,64,256]{2,1,0:T(8,128)(2,1)S(1)}, u32[]{:S(2)}, u32[]{:S(2)}) collective-permute-start(bf16[1,64,256]{2,1,0:T(8,128)(2,1)S(1)} %bitcast.145), channel_id=1, source_target_pairs={{0,16},{2,18},{4,20},{6,22},{8,24},{10,26},{12,28},{14,30},{16,0},... | collective-permute-start | bytes 98312 | tf_op jit(solution)/shard_map/ppermute | solution.py:586
  101.1 8.0 %collective-permute-start.17 = (bf16[1,32,768]{2,1,0:T(8,128)(2,1)S(1)}, bf16[1,32,768]{2,1,0:T(8,128)(2,1)S(1)}, u32[]{:S(2)}, u32[]{:S(2)}) collective-permute-start(bf16[1,32,768]{2,1,0:T(8,128)(2,1)S(1)} %get-tuple-element.268), channel_id=1, source_target_pairs={{0,16},{2,18},{4,20},{6,22},{8,24},{10,26},{12,28},{14,30},{16,0},... | collective-permute-start | bytes 147464 | tf_op jit(solution)/shard_map/ppermute | solution.py:586
  109.1 9.6 %collective-permute-start.18 = (bf16[2,32,768]{2,1,0:T(8,128)(2,1)S(1)}, bf16[2,32,768]{2,1,0:T(8,128)(2,1)S(1)}, u32[]{:S(2)}, u32[]{:S(2)}) collective-permute-start(bf16[2,32,768]{2,1,0:T(8,128)(2,1)S(1)} %pad_maximum_fusion.24), channel_id=1, source_target_pairs={{0,8},{2,10},{4,12},{6,14},{8,0},{10,2},{12,4},{14,6},{16,24},{18,... | collective-permute-start | bytes 294920 | tf_op jit(solution)/shard_map/ppermute | solution.py:586
  110.8 11.3 %collective-permute-start.27 = (bf16[4,64,256]{2,1,0:T(8,128)(2,1)S(1)}, bf16[4,64,256]{2,1,0:T(8,128)(2,1)S(1)}, u32[]{:S(2)}, u32[]{:S(2)}) collective-permute-start(bf16[4,64,256]{2,1,0:T(8,128)(2,1)S(1)} %pad_maximum_fusion.21), channel_id=1, source_target_pairs={{0,8},{2,10},{4,12},{6,14},{8,0},{10,2},{12,4},{14,6},{16,24},{18,... | collective-permute-start | bytes 393224 | tf_op jit(solution)/shard_map/ppermute | solution.py:586
  112.1 11.4 %collective-permute-start.23 = (bf16[4,32,768]{2,1,0:T(8,128)(2,1)S(1)}, bf16[4,32,768]{2,1,0:T(8,128)(2,1)S(1)}, u32[]{:S(2)}, u32[]{:S(2)}) collective-permute-start(bf16[4,32,768]{2,1,0:T(8,128)(2,1)S(1)} %pad_maximum_fusion.20), channel_id=1, source_target_pairs={{0,2},{2,0},{4,6},{6,4},{8,10},{10,8},{12,14},{14,12},{16,18},{18,... | collective-permute-start | bytes 589832 | tf_op jit(solution)/shard_map/ppermute | solution.py:586
  118.7 7.8 %collective-permute-start.19 = (bf16[4,32,768]{2,1,0:T(8,128)(2,1)S(1)}, bf16[4,32,768]{2,1,0:T(8,128)(2,1)S(1)}, u32[]{:S(2)}, u32[]{:S(2)}) collective-permute-start(bf16[4,32,768]{2,1,0:T(8,128)(2,1)S(1)} %pad_maximum_fusion.19), channel_id=1, source_target_pairs={{0,4},{2,6},{4,0},{6,2},{8,12},{10,14},{12,8},{14,10},{16,20},{18,... | collective-permute-start | bytes 589832 | tf_op jit(solution)/shard_map/ppermute | solution.py:586
  122.1 7.9 %collective-permute-start.28 = (bf16[8,64,256]{2,1,0:T(8,128)(2,1)S(1)}, bf16[8,64,256]{2,1,0:T(8,128)(2,1)S(1)}, u32[]{:S(2)}, u32[]{:S(2)}) collective-permute-start(bf16[8,64,256]{2,1,0:T(8,128)(2,1)S(1)} %pad_maximum_fusion.14), channel_id=1, source_target_pairs={{0,4},{2,6},{4,0},{6,2},{8,12},{10,14},{12,8},{14,10},{16,20},{18,... | collective-permute-start | bytes 786440 | tf_op jit(solution)/shard_map/ppermute | solution.py:586
  123.5 85.9 %collective-permute-start.24 = (bf16[8,32,768]{2,1,0:T(8,128)(2,1)S(1)}, bf16[8,32,768]{2,1,0:T(8,128)(2,1)S(1)}, u32[]{:S(2)}, u32[]{:S(2)}) collective-permute-start(bf16[8,32,768]{2,1,0:T(8,128)(2,1)S(1)} %pad_maximum_fusion.12), channel_id=1, source_target_pairs={{0,8},{2,10},{4,12},{6,14},{8,0},{10,2},{12,4},{14,6},{16,24},{18,... | collective-permute-start | bytes 1179656 | tf_op jit(solution)/shard_map/ppermute | solution.py:586
  126.6 82.9 %collective-permute-start.20 = (bf16[8,32,768]{2,1,0:T(8,128)(2,1)S(1)}, bf16[8,32,768]{2,1,0:T(8,128)(2,1)S(1)}, u32[]{:S(2)}, u32[]{:S(2)}) collective-permute-start(bf16[8,32,768]{2,1,0:T(8,128)(2,1)S(1)} %pad_maximum_fusion.11), channel_id=1, source_target_pairs={{0,2},{2,0},{4,6},{6,4},{8,10},{10,8},{12,14},{14,12},{16,18},{18,... | collective-permute-start | bytes 1179656 | tf_op jit(solution)/shard_map/ppermute | solution.py:586
  217.3 14.2 %collective-permute-start.32 = (bf16[1024,1024]{1,0:T(8,128)(2,1)}, bf16[1024,1024]{1,0:T(8,128)(2,1)}, u32[]{:S(2)}, u32[]{:S(2)}) collective-permute-start(bf16[1024,1024]{1,0:T(8,128)(2,1)} %param.24), channel_id=1, source_target_pairs={{0,1},{1,0},{2,3},{3,2},{4,5},{5,4},{6,7},{7,6},{8,9},{9,8},{10,11... | collective-permute-start | bytes 6291464 | tf_op jit(solution)/shard_map/ppermute | solution.py:586
  274.3 23.1 %collective-permute-start.33 = (bf16[1024,1024]{1,0:T(8,128)(2,1)S(1)}, bf16[1024,1024]{1,0:T(8,128)(2,1)S(1)}, u32[]{:S(2)}, u32[]{:S(2)}) collective-permute-start(bf16[1024,1024]{1,0:T(8,128)(2,1)S(1)} %add_convert_fusion.1), channel_id=1, source_target_pairs={{0,1},{1,0},{2,3},{3,2},{4,5},{5,4},{6,7},{7,6},{8,9},{9,8},{10,11... | collective-permute-start | bytes 6291464 | tf_op jit(solution)/shard_map/ppermute | solution.py:586
  278.5 43.2 %collective-permute-start.31 = (bf16[1024,1024]{1,0:T(8,128)(2,1)}, bf16[1024,1024]{1,0:T(8,128)(2,1)}, u32[]{:S(2)}, u32[]{:S(2)}) collective-permute-start(bf16[1024,1024]{1,0:T(8,128)(2,1)} %fusion.37), channel_id=1, source_target_pairs={{0,1},{1,0},{2,3},{3,2},{4,5},{5,4},{6,7},{7,6},{8,9},{9,8},{10,11... | collective-permute-start | bytes 6291464 | tf_op jit(solution)/shard_map/ppermute | solution.py:586
  307.8 21.7 %collective-permute-start.34 = (bf16[1024,1024]{1,0:T(8,128)(2,1)}, bf16[1024,1024]{1,0:T(8,128)(2,1)}, u32[]{:S(2)}, u32[]{:S(2)}) collective-permute-start(bf16[1024,1024]{1,0:T(8,128)(2,1)} %get-tuple-element.227), channel_id=1, source_target_pairs={{0,1},{1,0},{2,3},{3,2},{4,5},{5,4},{6,7},{7,6},{8,9},{9,8},{10,11... | collective-permute-start | bytes 6291464 | tf_op jit(solution)/shard_map/ppermute | solution.py:586
  346.3 44.5 %collective-permute-start.37 = (bf16[2,2,1,2,64,256]{5,4,3,2,1,0:T(8,128)(2,1)S(1)}, bf16[2,2,1,2,64,256]{5,4,3,2,1,0:T(8,128)(2,1)S(1)}, u32[]{:S(2)}, u32[]{:S(2)}) collective-permute-start(bf16[2,2,1,2,64,256]{5,4,3,2,1,0:T(8,128)(2,1)S(1)} %get-tuple-element.90), channel_id=1, source_target_pairs={{0,4},{2,6},{4,0},{6,2},{8,12},{10,14},{12,8},{14,10},{16,20},{18,... | collective-permute-start | bytes 786440 | tf_op jit(solution)/shard_map/ppermute | solution.py:586
  346.4 44.5 %collective-permute-start.36 = (bf16[2,1,2,2,32,768]{5,4,3,2,1,0:T(8,128)(2,1)S(1)}, bf16[2,1,2,2,32,768]{5,4,3,2,1,0:T(8,128)(2,1)S(1)}, u32[]{:S(2)}, u32[]{:S(2)}) collective-permute-start(bf16[2,1,2,2,32,768]{5,4,3,2,1,0:T(8,128)(2,1)S(1)} %get-tuple-element.88), channel_id=1, source_target_pairs={{0,8},{2,10},{4,12},{6,14},{8,0},{10,2},{12,4},{14,6},{16,24},{18,... | collective-permute-start | bytes 1179656 | tf_op jit(solution)/shard_map/ppermute | solution.py:586
  346.5 45.3 %collective-permute-start.35 = (bf16[2,2,2,1,32,768]{5,4,3,2,1,0:T(8,128)(2,1)S(1)}, bf16[2,2,2,1,32,768]{5,4,3,2,1,0:T(8,128)(2,1)S(1)}, u32[]{:S(2)}, u32[]{:S(2)}) collective-permute-start(bf16[2,2,2,1,32,768]{5,4,3,2,1,0:T(8,128)(2,1)S(1)} %get-tuple-element.86), channel_id=1, source_target_pairs={{0,2},{2,0},{4,6},{6,4},{8,10},{10,8},{12,14},{14,12},{16,18},{18,... | collective-permute-start | bytes 1179656 | tf_op jit(solution)/shard_map/ppermute | solution.py:586
  459.9 37.2 %collective-permute-start.67 = (bf16[2,1,2,1,32,768]{5,4,3,2,1,0:T(8,128)(2,1)}, bf16[2,1,2,1,32,768]{5,4,3,2,1,0:T(8,128)(2,1)}, u32[]{:S(2)}, u32[]{:S(2)}) collective-permute-start(bf16[2,1,2,1,32,768]{5,4,3,2,1,0:T(8,128)(2,1)} %get-tuple-element.114), channel_id=1, source_target_pairs={{0,2},{2,0},{4,6},{6,4},{8,10},{10,8},{12,14},{14,12},{16,18},{18,... | collective-permute-start | bytes 589832 | tf_op jit(solution)/shard_map/ppermute | solution.py:586
  465.5 83.3 %collective-permute-start.60 = (bf16[2,1,2,2,64,768]{5,4,3,2,1,0:T(8,128)(2,1)S(1)}, bf16[2,1,2,2,64,768]{5,4,3,2,1,0:T(8,128)(2,1)}, u32[]{:S(2)}, u32[]{:S(2)}) collective-permute-start(bf16[2,1,2,2,64,768]{5,4,3,2,1,0:T(8,128)(2,1)S(1)} %get-tuple-element.110), channel_id=1, source_target_pairs={{0,8},{2,10},{4,12},{6,14},{8,0},{10,2},{12,4},{14,6},{16,24},{18,... | collective-permute-start | bytes 2359304 | tf_op jit(solution)/shard_map/ppermute | solution.py:586
  465.6 87.2 %collective-permute-start.56 = (bf16[2,2,2,1,64,768]{5,4,3,2,1,0:T(8,128)(2,1)}, bf16[2,2,2,1,64,768]{5,4,3,2,1,0:T(8,128)(2,1)}, u32[]{:S(2)}, u32[]{:S(2)}) collective-permute-start(bf16[2,2,2,1,64,768]{5,4,3,2,1,0:T(8,128)(2,1)} %get-tuple-element.108), channel_id=1, source_target_pairs={{0,2},{2,0},{4,6},{6,4},{8,10},{10,8},{12,14},{14,12},{16,18},{18,... | collective-permute-start | bytes 2359304 | tf_op jit(solution)/shard_map/ppermute | solution.py:586
  467.6 22.0 %collective-permute-start.53 = (bf16[2,1,1,2,64,256]{5,4,3,2,1,0:T(8,128)(2,1)S(1)}, bf16[2,1,1,2,64,256]{5,4,3,2,1,0:T(8,128)(2,1)S(1)}, u32[]{:S(2)}, u32[]{:S(2)}) collective-permute-start(bf16[2,1,1,2,64,256]{5,4,3,2,1,0:T(8,128)(2,1)S(1)} %get-tuple-element.106), channel_id=1, source_target_pairs={{0,8},{2,10},{4,12},{6,14},{8,0},{10,2},{12,4},{14,6},{16,24},{18,... | collective-permute-start | bytes 393224 | tf_op jit(solution)/shard_map/ppermute | solution.py:586
  493.9 32.8 %collective-permute-start.48 = (bf16[2,2,1,2,64,384]{5,4,3,2,1,0:T(8,128)(2,1)}, bf16[2,2,1,2,64,384]{5,4,3,2,1,0:T(8,128)(2,1)S(1)}, u32[]{:S(2)}, u32[]{:S(2)}) collective-permute-start(bf16[2,2,1,2,64,384]{5,4,3,2,1,0:T(8,128)(2,1)} %get-tuple-element.104), channel_id=1, source_target_pairs={{0,4},{2,6},{4,0},{6,2},{8,12},{10,14},{12,8},{14,10},{16,20},{18,... | collective-permute-start | bytes 1179656 | tf_op jit(solution)/shard_map/ppermute | solution.py:586
  494.0 31.2 %collective-permute-start.44 = (bf16[2,2,1,2,64,384]{5,4,3,2,1,0:T(8,128)(2,1)}, bf16[2,2,1,2,64,384]{5,4,3,2,1,0:T(8,128)(2,1)S(1)}, u32[]{:S(2)}, u32[]{:S(2)}) collective-permute-start(bf16[2,2,1,2,64,384]{5,4,3,2,1,0:T(8,128)(2,1)} %get-tuple-element.102), channel_id=1, source_target_pairs={{0,4},{2,6},{4,0},{6,2},{8,12},{10,14},{12,8},{14,10},{16,20},{18,... | collective-permute-start | bytes 1179656 | tf_op jit(solution)/shard_map/ppermute | solution.py:586
  506.6 7.9 %collective-permute-start.68 = (bf16[2,1,1,1,32,768]{5,4,3,2,1,0:T(8,128)(2,1)S(1)}, bf16[2,1,1,1,32,768]{5,4,3,2,1,0:T(8,128)(2,1)S(1)}, u32[]{:S(2)}, u32[]{:S(2)}) collective-permute-start(bf16[2,1,1,1,32,768]{5,4,3,2,1,0:T(8,128)(2,1)S(1)} %constant_dynamic-slice_fusion.1), channel_id=1, source_target_pairs={{0,4},{2,6},{4,0},{6,2},{8,12},{10,14},{12,8},{14,10},{16,20},{18,... | collective-permute-start | bytes 294920 | tf_op jit(solution)/shard_map/ppermute | solution.py:586
  524.5 48.4 %collective-permute-start.38 = (bf16[1024,1024]{1,0:T(8,128)(2,1)}, bf16[1024,1024]{1,0:T(8,128)(2,1)}, u32[]{:S(2)}, u32[]{:S(2)}) collective-permute-start(bf16[1024,1024]{1,0:T(8,128)(2,1)} %add_convert_fusion), channel_id=1, source_target_pairs={{0,1},{1,0},{2,3},{3,2},{4,5},{5,4},{6,7},{7,6},{8,9},{9,8},{10,11... | collective-permute-start | bytes 6291464 | tf_op jit(solution)/shard_map/ppermute | solution.py:586
  526.9 10.1 %collective-permute-start.49 = (bf16[2,1,1,2,64,384]{5,4,3,2,1,0:T(8,128)(2,1)S(1)}, bf16[2,1,1,2,64,384]{5,4,3,2,1,0:T(8,128)(2,1)S(1)}, u32[]{:S(2)}, u32[]{:S(2)}) collective-permute-start(bf16[2,1,1,2,64,384]{5,4,3,2,1,0:T(8,128)(2,1)S(1)} %constant_dynamic-slice_fusion.14), channel_id=1, source_target_pairs={{0,8},{2,10},{4,12},{6,14},{8,0},{10,2},{12,4},{14,6},{16,24},{18,... | collective-permute-start | bytes 589832 | tf_op jit(solution)/shard_map/ppermute | solution.py:586
  550.5 12.0 %collective-permute-start.61 = (bf16[2,1,2,1,64,768]{5,4,3,2,1,0:T(8,128)(2,1)S(1)}, bf16[2,1,2,1,64,768]{5,4,3,2,1,0:T(8,128)(2,1)S(1)}, u32[]{:S(2)}, u32[]{:S(2)}) collective-permute-start(bf16[2,1,2,1,64,768]{5,4,3,2,1,0:T(8,128)(2,1)S(1)} %constant_dynamic-slice_fusion.6), channel_id=1, source_target_pairs={{0,2},{2,0},{4,6},{6,4},{8,10},{10,8},{12,14},{14,12},{16,18},{18,... | collective-permute-start | bytes 1179656 | tf_op jit(solution)/shard_map/ppermute | solution.py:586
  554.1 11.4 %collective-permute-start.57 = (bf16[2,2,1,1,64,768]{5,4,3,2,1,0:T(8,128)(2,1)S(1)}, bf16[2,2,1,1,64,768]{5,4,3,2,1,0:T(8,128)(2,1)S(1)}, u32[]{:S(2)}, u32[]{:S(2)}) collective-permute-start(bf16[2,2,1,1,64,768]{5,4,3,2,1,0:T(8,128)(2,1)S(1)} %constant_dynamic-slice_fusion.9), channel_id=1, source_target_pairs={{0,4},{2,6},{4,0},{6,2},{8,12},{10,14},{12,8},{14,10},{16,20},{18,... | collective-permute-start | bytes 1179656 | tf_op jit(solution)/shard_map/ppermute | solution.py:586
  569.7 10.6 %collective-permute-start.63 = (bf16[1,1,1,1,64,768]{5,4,3,2,1,0:T(8,128)(2,1)S(1)}, bf16[1,1,1,1,64,768]{5,4,3,2,1,0:T(8,128)(2,1)S(1)}, u32[]{:S(2)}, u32[]{:S(2)}) collective-permute-start(bf16[1,1,1,1,64,768]{5,4,3,2,1,0:T(8,128)(2,1)S(1)} %constant_dynamic-slice_fusion.4), channel_id=1, source_target_pairs={{0,16},{2,18},{4,20},{6,22},{8,24},{10,26},{12,28},{14,30},{16,0},... | collective-permute-start | bytes 294920 | tf_op jit(solution)/shard_map/ppermute | solution.py:586
  571.9 10.6 %collective-permute-start.59 = (bf16[1,1,1,1,64,768]{5,4,3,2,1,0:T(8,128)(2,1)S(1)}, bf16[1,1,1,1,64,768]{5,4,3,2,1,0:T(8,128)(2,1)S(1)}, u32[]{:S(2)}, u32[]{:S(2)}) collective-permute-start(bf16[1,1,1,1,64,768]{5,4,3,2,1,0:T(8,128)(2,1)S(1)} %constant_dynamic-slice_fusion.7), channel_id=1, source_target_pairs={{0,16},{2,18},{4,20},{6,22},{8,24},{10,26},{12,28},{14,30},{16,0},... | collective-permute-start | bytes 294920 | tf_op jit(solution)/shard_map/ppermute | solution.py:586
  (88 other events, 1453.5 us)
Sparse Core Ops, SparseCore 0:
  74.8 102.4 all-gather.1
  321.8 150.7 reduce-scatter.1
where the time goes:
time: 615 us; the launch traced here: 609 us
  Pallas kernels  164 us (27%)
  matrix products  152 us (25%)
  waiting for transfers between devices  83.4 us (14%)
  other arithmetic  72.5 us (12%)
  starting transfers between devices  71.6 us (12%)
  local copies, waits for them, and re-layouts  49.9 us (8%)
  between operations  16.1 us (3%)
    ppermute x70, waiting for transfers between devices, permute_bit(): return lax.ppermute(x, axis, [(i, i ^ bit) for i in range(n)])  83.3 us
    ppermute x70, starting transfers between devices, permute_bit(): return lax.ppermute(x, axis, [(i, i ^ bit) for i in range(n)])  71.3 us
    dot_general x7, matrix products, dot_nn(): lax.dot_general(left, right, (((1,), (0,)), ((), ())), preferred_element_...  57.7 us
    pallas_call x1, Pallas kernels, mix_bwd(): pl.pallas_call(functools.partial(mix_bwd_kernel, heads), grid=(seqs, per)...  55.9 us
    dot_general x14, matrix products, dot_nt(): lax.dot_general(left, right, (((1,), (1,)), ((), ())), preferred_element_...  53.9 us
    pallas_call x1, Pallas kernels, attend_bwd(): pl.pallas_call(functools.partial(attend_bwd_kernel, heads), grid_spec=plt...  42.9 us
    dot_general x9, matrix products, dot_tn(): lax.dot_general(left, right, (((0,), (0,)), ((), ())), preferred_element_...  40 us
    pallas_call x1, Pallas kernels, attend_fwd(): pl.pallas_call(functools.partial(attend_fwd_kernel, heads), grid_spec=plt...  29.6 us
  transfers between devices with their start and end apart: 72, of which 33 were waited for; matrix products, arithmetic and copies ran while one was open for 37% of the time, Pallas kernels for 27%

commit v1 on v0

--- a/solution.py
+++ b/solution.py
@@ -594,14 +594,15 @@
     return [bits[:1] + turn(j) for j in range(3)]
 
 
-def gather_rel(piece, axis, order):
-    held = piece[None]
+def gather_step(held, axis, bit):
+    return jnp.concatenate([held, permute_bit(held, axis, bit)], axis=0)
+
+
+def gather_last(held, axis, order):
     places = [0]
-    for bit in order:
-        before = held
-        held = jnp.concatenate([held, permute_bit(held, axis, bit)], axis=0)
+    for bit in order[:-1]:
         places = places + [p ^ bit for p in places]
-    return held, places, before
+    return (held, places), (permute_bit(held, axis, order[-1]), [p ^ order[-1] for p in places])
 
 
 def assemble_kernel(plan, count, me_ref, *refs):
@@ -632,7 +633,7 @@
             grid=(1,),
             in_specs=[hbm] * len(rels),
             out_specs=[hbm] * len(shapes),
-            scratch_shapes=[pltpu.SemaphoreType.DMA((len(rels), rels[0].shape[0]))],
+            scratch_shapes=[pltpu.SemaphoreType.DMA((len(rels), max(r.shape[0] for r in rels)))],
         ),
         out_shape=[jax.ShapeDtypeStruct(s, BF16) for s in shapes],
         compiler_params=pltpu.CompilerParams(vmem_limit_bytes=4 * 1024 * 1024),
@@ -770,34 +771,33 @@
     total_cols = mix_shard.shape[1] + qkv_shard.shape[1]
     mix_cols = thirds(total_cols)
     mix_cols = [(a, min(b, mix_shard.shape[1])) for a, b in mix_cols if a < mix_shard.shape[1]]
-    rels, plan, befores = [], [], []
-    for j, (a, b) in enumerate(mix_cols):
-        rel, places, before = gather_rel(mix_shard[:, a:b], "dp", orders[j])
-        rels.append(rel)
-        befores.append(before)
-        plan.append((places, 0, 0, a, block_rows))
-    rel, places, before = gather_rel(qkv_shard, "dp", orders[2])
-    rels.append(rel)
-    befores.append(before)
-    plan.append((places, 1, 0, 0, block_rows))
+    steps = len(orders[0])
+    shards = [(mix_shard[:, a:b], 0, a, j) for j, (a, b) in enumerate(mix_cols)]
+    shards.append((qkv_shard, 1, 0, 2))
+    held = [p[0][None] for p in shards]
+    for k in range(steps - 1):
+        held = [gather_step(h, "dp", orders[p[3]][k]) for h, p in zip(held, shards)]
+
+    later = jnp.concatenate([ffn_gate_w, ffn_up_w, ffn_down_w.T], axis=1)
+    later, held = lax.optimization_barrier((later, held))
+    later = lax.all_gather(later, "dp", axis=0, tiled=True)
+    ffn_gate, ffn_up, ffn_down_t = (later[:, k * units:(k + 1) * units] for k in range(3))
+
+    rels, plan = [], []
+    for h, (_, dest, lane_off, j) in zip(held, shards):
+        for rel, places in gather_last(h, "dp", orders[j]):
+            rels.append(rel)
+            plan.append((places, dest, 0, lane_off, block_rows))
+
+    (out_shard, mout_shard), rels = lax.optimization_barrier(((out_w.T, mamba_out_w.T), rels))
     mix_w, qkv_w = assemble(me, rels, plan, [(features, mix_shard.shape[1]),
                                             (features, qkv_shard.shape[1])])
-
-    later = jnp.concatenate([ffn_gate_w, ffn_up_w, ffn_down_w.T], axis=1)
-    later, _ = lax.optimization_barrier((later, tuple(befores)))
-    later = lax.all_gather(later, "dp", axis=0, tiled=True)
-    ffn_gate, ffn_up, ffn_down_t = (later[:, k * units:(k + 1) * units] for k in range(3))
-
-    (out_shard, mout_shard), rels = lax.optimization_barrier(((out_w.T, mamba_out_w.T), tuple(rels)))
-    rels2, plan2 = [], []
-    for piece, dest, row_off, order in (
-        (mout_shard[:half_rows], 1, 0, 0), (mout_shard[half_rows:], 1, half_rows, 1),
-        (out_shard, 0, 0, 2),
-    ):
-        rel, places, _ = gather_rel(piece, "dp", orders[order])
-        rels2.append(rel)
-        plan2.append((places, dest, row_off, 0, block_rows))
-    out_t, mout_t = assemble(me, rels2, plan2, [(features, q_width), (features, width)])
+    shards2 = [(mout_shard[:half_rows], 1, 0, 0), (mout_shard[half_rows:], 1, half_rows, 1),
+               (out_shard, 0, 0, 2)]
+    held2 = [p[0][None] for p in shards2]
+
+    def output_step(held, k):
+        return [gather_step(h, "dp", orders[p[3]][k]) for h, p in zip(held, shards2)]
 
     tokens = layer_input.astype(F32)
     inverse = inverse_rms(tokens)
@@ -813,11 +813,13 @@
     first = (starts // BQ).reshape(-1)
     cos, sin = rope_tables()
 
-    queries, key_rows, value_rows = rope(dot_nn(normed, qkv_w), cos, sin)
-    seg_blocks = segment_ids.reshape(-1, 1, BQ)
-    attended, lse = attend_fwd(first, queries, key_rows, value_rows, seg_col, seg_blocks)
-
-    pre = dot_nn(normed, mix_w)
+    qkv = dot_nn(normed, qkv_w)
+    for k in range(steps - 3):
+        held2 = output_step(held2, k)
+    normed_late, held2, qkv = lax.optimization_barrier((normed, held2, qkv))
+    pre = dot_nn(normed_late, mix_w)
+    held2 = output_step(held2, steps - 3)
+    pre, held2 = lax.optimization_barrier((pre, held2))
     pad_heads = lambda a: jnp.pad(a[None], ((0, 0), (0, STATE - ssm)))
     bias, rate = pad_heads(step_bias), pad_heads(decay_log)
     skip = jnp.repeat(skip_gain, HEAD_DIM)[None]
@@ -825,6 +827,18 @@
     chunk_rows = segment_ids.reshape(-1, 1, Q)
     gated, scanned, states = mix_fwd(
         seg_col, chunk_rows, masks, pre, channel_conv, state_conv, bias, rate, skip, spread, ssm)
+
+    held2 = output_step(held2, steps - 2)
+    qkv, gated, held2 = lax.optimization_barrier((qkv, gated, held2))
+    queries, key_rows, value_rows = rope(qkv, cos, sin)
+    seg_blocks = segment_ids.reshape(-1, 1, BQ)
+    attended, lse = attend_fwd(first, queries, key_rows, value_rows, seg_col, seg_blocks)
+    rels2, plan2 = [], []
+    for h, (_, dest, row_off, j) in zip(held2, shards2):
+        for rel, places in gather_last(h, "dp", orders[j]):
+            rels2.append(rel)
+            plan2.append((places, dest, row_off, 0, block_rows))
+    out_t, mout_t = assemble(me, rels2, plan2, [(features, q_width), (features, width)])
 
     branch = tensor_scatter(
         lambda a, b: dot_nt(a, out_t) + dot_nt(b, mout_t), (attended, gated), True)
@@ -880,17 +894,36 @@
     halves1 = [reduce_halves(reduce_open(p, "dp", 0, block_rows), "dp", orders[j][-1]) for p, j in pieces1]
     mix_grad_late, halves1 = lax.optimization_barrier((mix_grad, halves1))
     held1 = [reduce_step(h, "dp", orders[p[1]][-1], False) for h, p in zip(halves1, pieces1)]
-    sums = [reduce_rest(c, "dp", orders[p[1]][:-1]) for c, p in zip(held1, pieces1)]
-    mix_sum = jnp.concatenate(sums[:-1], axis=1)
-    qkv_sum = sums[-1]
-    mout_a, mout_b, out_sum = (
-        reduce_rest(c, "dp", orders[p[3]][:-2]) for c, p in zip(held2, pieces2))
-    mamba_out_w_grad = jnp.concatenate([mout_a, mout_b], axis=0).T
-    out_w_grad = out_sum.T
     normed_grad = tensor_scatter(
         lambda a, b: dot_nt(a, qkv_w) + dot_nt(b, mix_w), (qkv_grad, mix_grad_late), True)
     norm_into, norm_gain_part = norm_back(tokens, inverse, norm_gain, normed_grad)
     input_grad = middle_grad + norm_into
+
+    heads_part = jnp.concatenate([
+        head_part[0, :ssm], head_part[1, :ssm],
+        jnp.sum(skip_part.reshape(ssm, HEAD_DIM), axis=1)])
+    small = jnp.concatenate([
+        conv_part.reshape(-1), heads_part, state_conv_part.reshape(-1), ffn_gain_part,
+        norm_gain_part])
+    small_bits = list(bit_orders("dp")[0])
+    tail = [(c, list(reversed(orders[p[1]][:-1]))) for c, p in zip(held1, pieces1)]
+    tail += [(c, list(reversed(orders[p[3]][:-2]))) for c, p in zip(held2, pieces2)]
+    cur = [c for c, _ in tail]
+    for k in range(steps - 1):
+        cur, small = lax.optimization_barrier((cur, small))
+        bit = small_bits.pop()
+        small = small + permute_bit(small, "dp", bit)
+        cur = [
+            reduce_step(reduce_halves(c, "dp", bits[k]), "dp", bits[k], k == len(bits) - 1)
+            if k < len(bits) else c for c, (_, bits) in zip(cur, tail)]
+    while small_bits:
+        small = small + permute_bit(small, "dp", small_bits.pop())
+    sums = [c.reshape(c.shape[-2:]) for c in cur]
+    mix_sum = jnp.concatenate(sums[:len(mix_cols)], axis=1)
+    qkv_sum = sums[len(mix_cols)]
+    mout_a, mout_b, out_sum = sums[len(mix_cols) + 1:]
+    mamba_out_w_grad = jnp.concatenate([mout_a, mout_b], axis=0).T
+    out_w_grad = out_sum.T
 
     place = lambda a, whole: lax.dynamic_update_slice_in_dim(
         jnp.zeros((block_rows, whole.shape[1]), BF16), a.astype(BF16), kv_index * HEAD_DIM, 1)
@@ -900,13 +933,7 @@
         mix_sum[:, 2 * width:2 * width + 2 * STATE].astype(BF16)], axis=1), "tensor").astype(F32)
     kv_cols = key_w.shape[1]
 
-    heads_part = jnp.concatenate([
-        head_part[0, :ssm], head_part[1, :ssm],
-        jnp.sum(skip_part.reshape(ssm, HEAD_DIM), axis=1)])
     own = 4 * width + 3 * ssm
-    small = sum_cube(jnp.concatenate([
-        conv_part.reshape(-1), heads_part, state_conv_part.reshape(-1), ffn_gain_part,
-        norm_gain_part]), "dp")
     conv_grad = small[:4 * width].reshape(4, width)
     bias_grad, decay_grad, skip_grad = (
         small[4 * width + k * ssm:4 * width + (k + 1) * ssm] for k in range(3))

time: 615 us -> 572 us (0.930)
  waiting for transfers between devices: 83.4 us -> 57.9 us
  local copies, waits for them, and re-layouts: 49.9 us -> 34.8 us
    ppermute x70, waiting for transfers between devices: 83.3 us -> 57.8 us  [permute_bit(): return lax.ppermute(x, axis, [(i, i ^ bit) for i in range(n)])]
    unnamed x157 -> x136, local copies, waits for them, and re-layouts: 26.1 us -> 13.5 us
    concatenate x7 -> x0, local copies, waits for them, and re-layouts: 7.83 us -> none  [gather_rel(): held = jnp.concatenate([held, permute_bit(held, axis, bit)], axis=0)]
    concatenate x21 -> x22, other arithmetic: 14.4 us -> 13.4 us  [the longest x21 13 us: gather_step(): return jnp.concatenate([held, permute_bit(held, axis, bit)], axis=0)]
  transfers between devices with their start and end apart: 72 -> 72, of which waited for: 33 -> 18; matrix products, arithmetic and copies ran while one was open for 37% -> 36% of each run, Pallas kernels for 27% -> 29%
where the time goes in v1:
time: 572 us; the launch traced here: 567 us
  Pallas kernels  162 us (28%)
  matrix products  152 us (27%)
  starting transfers between devices  73.2 us (13%)
  other arithmetic  71.1 us (12%)
  waiting for transfers between devices  57.9 us (10%)
  local copies, waits for them, and re-layouts  34.8 us (6%)
  between operations  16.1 us (3%)
    ppermute x70, starting transfers between devices, permute_bit(): return lax.ppermute(x, axis, [(i, i ^ bit) for i in range(n)])  72.9 us
    ppermute x70, waiting for transfers between devices, permute_bit(): return lax.ppermute(x, axis, [(i, i ^ bit) for i in range(n)])  57.8 us
    dot_general x14, matrix products, dot_nt(): lax.dot_general(left, right, (((1,), (1,)), ((), ())), preferred_element_...  56.4 us
    dot_general x7, matrix products, dot_nn(): lax.dot_general(left, right, (((1,), (0,)), ((), ())), preferred_element_...  56 us
    pallas_call x1, Pallas kernels, mix_bwd(): pl.pallas_call(functools.partial(mix_bwd_kernel, heads), grid=(seqs, per)...  55.7 us
    pallas_call x1, Pallas kernels, attend_bwd(): pl.pallas_call(functools.partial(attend_bwd_kernel, heads), grid_spec=plt...  43 us
    dot_general x9, matrix products, dot_tn(): lax.dot_general(left, right, (((0,), (0,)), ((), ())), preferred_element_...  40 us
    pallas_call x1, Pallas kernels, attend_fwd(): pl.pallas_call(functools.partial(attend_fwd_kernel, heads), grid_spec=plt...  29.5 us
  transfers between devices with their start and end apart: 72, of which 18 were waited for; matrix products, arithmetic and copies ran while one was open for 36% of the time, Pallas kernels for 29%

profile of v1, /device:TPU:0, one launch (start us, length us, event | category | flops | bytes accessed | tf_op | source)
XLA Modules:
  0.0 567.3 jit_solution(11017105325629877394)
XLA Ops:
  9.2 4.0 collective-permute-start.10
  20.4 3.5 fusion.10
  55.5 5.3 multiply_sine_fusion
  60.9 4.7 collective-permute-done.15.refs_5_
  65.6 7.8 %collective-permute-done.16.refs_7_ = bf16[8,64,384]{2,1,0:T(8,128)(2,1)} collective-permute-done((bf16[8,64,384]{2,1,0:T(8,128)(2,1)}, bf16[8,64,384]{2,1,0:T(8,128)(2,1)}, u32[]{:S(2)}, u32[]{:S(2)}) %collective-permute-start.16) | collective-permute-done | bytes 393248 | tf_op jit(solution)/shard_map/ppermute | solution.py:586
  73.3 5.1 collective-permute-done.14.refs_3_
  83.8 2.9 assemble.2
  87.6 3.3 broadcast_select_fusion.3
  92.9 4.1 fusion.97.qkv_ref
  99.7 11.5 %fusion.107.pre_ref.pre_prev_ref = f32[2048,1920]{1,0:T(8,128)} fusion(bf16[2048,1024]{1,0:T(8,128)(2,1)S(1)} %pad_maximum_fusion.1, bf16[1024,1920]{1,0:T(8,128)(2,1)S(1)} %get-tuple-element.135), kind=kOutput, calls=%fused_computation.263 | convolution fusion | flops 8053063680 | bytes 23855104 | tf_op jit(solution)/shard_map/dot_general | solution.py:25
  114.8 23.1 %mix_fwd.1 = (bf16[2048,768]{1,0:T(8,128)(2,1)S(1)}, f32[2048,768]{1,0:T(8,128)}, f32[16,128,768]{2,1,0:T(8,128)}) custom-call(s32[2048,1]{1,0:T(8,128)S(1)} %copy.103.seg_ref, s32[16,1,128]{2,1,0:T(1,128)S(1)} %bitcast.111, f32[2048,8]{1,0:T(8,128)S(1)} %convert_element_type.419.mask_ref, f32[2048,1920]{1,0:T(8,128)} %fusion.107.pre_ref.pre_prev_ref, ...), custom_call_target="tpu_custom_call" | custom-call | flops 1887436800 | bytes 34603008 | tf_op jit(solution)/shard_map/mix_fwd/pallas_call | solution.py:377
  146.0 5.6 rope.1
  151.6 29.5 %attend_fwd.1 = (bf16[2048,256]{1,0:T(8,128)(2,1)S(1)}, f32[4,4,512]{2,1,0:T(4,128)S(1)}) custom-call(s32[4]{0:T(128)S(1)} %and_select_fusion.1.first_ref, bf16[2048,256]{1,0:T(8,128)(2,1)S(1)} %get-tuple-element.145.q_ref, bf16[2048,64]{1,0:T(8,128)(2,1)S(1)} %get-tuple-element.146.k_ref, bf16[2048,128]{1,0:T(8,128)(2,1)S(1)} %get-tuple-element.147.v_ref, ...), custom_call_target="tpu_custom_call" | custom-call | flops 2147483648 | bytes 2097152 | tf_op jit(solution)/shard_map/attend_fwd/pallas_call | solution.py:121
  190.2 3.8 fusion.64
  194.0 4.0 multiply_reduce_fusion.2
  201.8 3.1 constant_dynamic-update-slice_fusion.1
  204.9 3.1 constant_dynamic-update-slice_fusion
  208.0 9.5 %convolution_convert_fusion.1 = bf16[2048,1024]{1,0:T(8,128)(2,1)} fusion(bf16[1024,3072]{1,0:T(8,128)(2,1)} %all-gather.2.cloned.1.call-done, bf16[1024,1024]{1,0:T(8,128)(2,1)} %collective-permute-done.30, bf16[1024,1024]{1,0:T(8,128)(2,1)} %multiply_convert_fusion.1), kind=kOutput, calls=%fused_computation.49 | convolution fusion | flops 4305453056 | bytes 10485760 | tf_op jit(solution)/shard_map/dot_general | solution.py:25
  217.5 8.8 %convolution_convert_fusion = bf16[2048,1024]{1,0:T(8,128)(2,1)} fusion(bf16[1024,3072]{1,0:T(8,128)(2,1)S(1)} %copy-done.59, bf16[1024,1024]{1,0:T(8,128)(2,1)} %collective-permute-done.30, bf16[1024,1024]{1,0:T(8,128)(2,1)} %multiply_convert_fusion.1), kind=kOutput, calls=%fused_computation.48 | convolution fusion | flops 4305453056 | bytes 10485760 | tf_op jit(solution)/shard_map/dot_general | solution.py:25
  226.3 13.8 %fusion.2 = (bf16[2048,1024]{1,0:T(8,128)(2,1)S(1)}, bf16[2048,1024]{1,0:T(8,128)(2,1)}, bf16[2048,1024]{1,0:T(8,128)(2,1)S(1)}) fusion(bf16[2048,1024]{1,0:T(8,128)(2,1)} %convolution_convert_fusion, bf16[2048,1024]{1,0:T(8,128)(2,1)} %convolution_convert_fusion.1, bf16[2048,1024]{1,0:T(8,128)(2,1)} %constant_dynamic-update-slice_fusion, ...), kind=kOutput, calls=%fused_computation.13 | convolution fusion | flops 4330618880 | bytes 27262976 | tf_op jit(solution)/shard_map/dot_general | solution.py:25
  240.1 5.5 fusion.25
  248.6 3.7 fusion.37
  252.4 4.4 fusion.29
  256.7 7.2 %convolution_convert_fusion.5 = bf16[1024,1024]{1,0:T(8,128)(2,1)S(1)} fusion(bf16[2048,1024]{1,0:T(8,128)(2,1)S(1)} %get-tuple-element.330, bf16[1024,1024]{1,0:T(8,128)(2,1)} %collective-permute-done.30, bf16[1024,1024]{1,0:T(8,128)(2,1)} %multiply_convert_fusion.1), kind=kOutput, calls=%fused_computation.74 | convolution fusion | flops 4304404480 | bytes 10485760 | tf_op jit(solution)/shard_map/dot_general | solution.py:33
  263.9 7.2 %convolution_convert_fusion.3 = bf16[1024,1024]{1,0:T(8,128)(2,1)S(1)} fusion(bf16[2048,1024]{1,0:T(8,128)(2,1)} %constant_dynamic-update-slice_fusion, bf16[2048,1024]{1,0:T(8,128)(2,1)S(1)} %copy-done.63), kind=kOutput, calls=%fused_computation.72 | convolution fusion | flops 4296015872 | bytes 10485760 | tf_op jit(solution)/shard_map/dot_general | solution.py:33
  271.1 5.7 multiply_reduce_fusion
  276.8 4.7 fusion.99
  282.0 7.0 %convolution_convert_fusion.4 = bf16[1024,1024]{1,0:T(8,128)(2,1)S(1)} fusion(bf16[2048,1024]{1,0:T(8,128)(2,1)S(1)} %copy-done.65, bf16[1024,1024]{1,0:T(8,128)(2,1)} %collective-permute-done.30, bf16[1024,1024]{1,0:T(8,128)(2,1)} %multiply_convert_fusion.1), kind=kOutput, calls=%fused_computation.73 | convolution fusion | flops 4304404480 | bytes 10485760 | tf_op jit(solution)/shard_map/dot_general | solution.py:33
  289.0 6.5 %pad_maximum_fusion = bf16[16,192,1024]{2,1,0:T(8,128)(2,1)} fusion(bf16[16,64,1024]{2,1,0:T(8,128)(2,1)S(1)} %bitcast.117, bf16[16,64,1024]{2,1,0:T(8,128)(2,1)S(1)} %bitcast.118, bf16[16,64,1024]{2,1,0:T(8,128)(2,1)S(1)} %bitcast.116), kind=kLoop, calls=%fused_computation.20 | loop fusion | flops 18874368 | bytes 12582912 | tf_op jit(solution)/shard_map/concatenate | solution.py:864
  295.5 7.8 %add_convert_fusion.2 = bf16[1024,1024]{1,0:T(8,128)(2,1)} fusion(f32[1024,1024]{1,0:T(8,128)} %copy-done.30, bf16[1024,1024]{1,0:T(8,128)(2,1)} %collective-permute-done.31, bf16[1024,3072]{1,0:T(8,128)(2,1)} %all-gather.2.cloned.1.call-done, bf16[2048,1024]{1,0:T(8,128)(2,1)} %copy-done.62), kind=kOutput, calls=%fused_computation.40 | convolution fusion | flops 2151677952 | bytes 12582912 | tf_op jit(solution)/shard_map/dot_general | solution.py:29
  307.7 3.7 convolution_convert_fusion.6
  312.8 7.0 %fusion.96.dout_ref = f32[2048,768]{1,0:T(8,128)} fusion(bf16[1024,768]{1,0:T(8,128)(2,1)S(1)} %copy-done.20, bf16[1024,1024]{1,0:T(8,128)(2,1)S(1)} %get-tuple-element.334, bf16[1024,1024]{1,0:T(8,128)(2,1)S(1)} %get-tuple-element.333), kind=kOutput, calls=%fused_computation.252 | convolution fusion | flops 3229614080 | bytes 12058624 | tf_op jit(solution)/shard_map/dot_general | solution.py:25
  320.3 3.2 collective-permute-start.35
  323.5 43.0 %attend_bwd.1 = (bf16[2048,256]{1,0:T(8,128)(2,1)S(1)}, bf16[2048,64]{1,0:T(8,128)(2,1)S(1)}, bf16[2048,64]{1,0:T(8,128)(2,1)S(1)}) custom-call(s32[4]{0:T(128)S(1)} %and_select_fusion.1.first_ref, bf16[2048,256]{1,0:T(8,128)(2,1)S(1)} %copy-done.22, bf16[2048,64]{1,0:T(8,128)(2,1)S(1)} %copy-done.24, bf16[2048,128]{1,0:T(8,128)(2,1)S(1)} %copy-done.26, ...), custom_call_target="tpu_custom_call" | custom-call | flops 5368709120 | bytes 4194304 | tf_op jit(solution)/shard_map/attend_bwd/pallas_call | solution.py:220
  368.0 55.7 %mix_bwd.1 = (bf16[2048,1920]{1,0:T(8,128)(2,1)}, f32[4,768]{1,0:T(4,128)S(1)}, f32[4,256]{1,0:T(4,128)S(1)}, f32[8,128]{1,0:T(8,128)S(1)}, f32[1,768]{1,0:T(1,128)S(1)}) custom-call(s32[2048,1]{1,0:T(8,128)S(1)} %copy-done.1, s32[16,1,128]{2,1,0:T(1,128)S(1)} %bitcast.114, f32[2048,8]{1,0:T(8,128)S(1)} %convert_element_type.419.mask_ref, ...), custom_call_target="tpu_custom_call" | custom-call | flops 4718592000 | bytes 44040192 | tf_op jit(solution)/shard_map/mix_bwd/pallas_call | solution.py:537
  423.8 4.0 fusion.66
  427.8 3.6 fusion.43
  431.4 3.7 fusion.40
  442.0 4.8 fusion.17
  449.4 6.1 %fusion.19 = f32[1024,1024]{1,0:T(8,128)} fusion(bf16[1024,1920]{1,0:T(8,128)(2,1)S(1)} %copy-done.13, bf16[2048,1920]{1,0:T(8,128)(2,1)S(1)} %copy-done.58, s32[]{:T(128)S(6)} %select_n.259), kind=kOutput, calls=%fused_computation.46 | convolution fusion | flops 4026531840 | bytes 12058628 | tf_op jit(solution)/shard_map/dot_general | solution.py:29
  458.7 3.0 collective-permute-done.45
  466.5 6.4 %collective-permute-done.42 = bf16[2,2,1,2,64,384]{5,4,3,2,1,0:T(8,128)(2,1)S(1)} collective-permute-done((bf16[2,2,1,2,64,384]{5,4,3,2,1,0:T(8,128)(2,1)}, bf16[2,2,1,2,64,384]{5,4,3,2,1,0:T(8,128)(2,1)S(1)}, u32[]{:S(2)}, u32[]{:S(2)}) %collective-permute-start.42) | collective-permute-done | bytes 393248 | tf_op jit(solution)/shard_map/ppermute | solution.py:586
  474.1 6.6 %collective-permute-done.41 = bf16[2,2,1,2,64,384]{5,4,3,2,1,0:T(8,128)(2,1)S(1)} collective-permute-done((bf16[2,2,1,2,64,384]{5,4,3,2,1,0:T(8,128)(2,1)}, bf16[2,2,1,2,64,384]{5,4,3,2,1,0:T(8,128)(2,1)S(1)}, u32[]{:S(2)}, u32[]{:S(2)}) %collective-permute-start.41) | collective-permute-done | bytes 393248 | tf_op jit(solution)/shard_map/ppermute | solution.py:586
  487.2 5.0 fusion.16
  502.1 5.5 fusion.13
  513.5 3.5 collective-permute-done.47
  531.9 4.5 collective-permute-done.54
  543.6 3.9 collective-permute-done.62
  (426 shorter events, 162.1 us)
Async XLA Ops:
  7.2 200.7 %all-gather.2.cloned.1.call-start = ((), (), s32[]{:S(2)}) async-start(), calls=%async_computation.1 | async-start | bytes 6684672 | tf_op jit(solution)/shard_map/all_gather | solution.py:783
  9.2 16.2 %collective-permute-start.10 = (bf16[1,64,384]{2,1,0:T(8,128)(2,1)S(1)}, bf16[1,64,384]{2,1,0:T(8,128)(2,1)S(1)}, u32[]{:S(2)}, u32[]{:S(2)}) collective-permute-start(bf16[1,64,384]{2,1,0:T(8,128)(2,1)S(1)} %maximum_bitcast_fusion.1), channel_id=1, source_target_pairs={{0,16},{2,18},{4,20},{6,22},{8,24},{10,26},{12,28},{14,30},{16,0},... | collective-permute-start | bytes 147464 | tf_op jit(solution)/shard_map/ppermute | solution.py:586
  13.2 15.5 %collective-permute-start.1 = (bf16[1,64,768]{2,1,0:T(8,128)(2,1)}, bf16[1,64,768]{2,1,0:T(8,128)(2,1)S(1)}, u32[]{:S(2)}, u32[]{:S(2)}) collective-permute-start(bf16[1,64,768]{2,1,0:T(8,128)(2,1)} %bitcast.122), channel_id=1, source_target_pairs={{0,16},{2,18},{4,20},{6,22},{8,24},{10,26},{12,28},{14,30},{16,0},... | collective-permute-start | bytes 294920 | tf_op jit(solution)/shard_map/ppermute | solution.py:586
  13.3 16.2 %collective-permute-start.4 = (bf16[1,64,768]{2,1,0:T(8,128)(2,1)}, bf16[1,64,768]{2,1,0:T(8,128)(2,1)S(1)}, u32[]{:S(2)}, u32[]{:S(2)}) collective-permute-start(bf16[1,64,768]{2,1,0:T(8,128)(2,1)} %bitcast.126), channel_id=1, source_target_pairs={{0,16},{2,18},{4,20},{6,22},{8,24},{10,26},{12,28},{14,30},{16,0},... | collective-permute-start | bytes 294920 | tf_op jit(solution)/shard_map/ppermute | solution.py:586
  17.7 9.5 %collective-permute-start.7 = (bf16[1,64,384]{2,1,0:T(8,128)(2,1)S(1)}, bf16[1,64,384]{2,1,0:T(8,128)(2,1)S(1)}, u32[]{:S(2)}, u32[]{:S(2)}) collective-permute-start(bf16[1,64,384]{2,1,0:T(8,128)(2,1)S(1)} %fusion.83), channel_id=1, source_target_pairs={{0,16},{2,18},{4,20},{6,22},{8,24},{10,26},{12,28},{14,30},{16,0},... | collective-permute-start | bytes 147464 | tf_op jit(solution)/shard_map/ppermute | solution.py:586
  23.9 63.7 %collective-permute-start = (bf16[1024,1024]{1,0:T(8,128)(2,1)}, bf16[1024,1024]{1,0:T(8,128)(2,1)}, u32[]{:S(2)}, u32[]{:S(2)}) collective-permute-start(bf16[1024,1024]{1,0:T(8,128)(2,1)} %fusion.10), channel_id=1, source_target_pairs={{0,1},{1,0},{2,3},{3,2},{4,5},{5,4},{6,7},{7,6},{8,9},{9,8},{10,11... | collective-permute-start | bytes 6291464 | tf_op jit(solution)/shard_map/ppermute | solution.py:586
  31.8 9.7 %collective-permute-start.12 = (bf16[4,64,384]{2,1,0:T(8,128)(2,1)}, bf16[4,64,384]{2,1,0:T(8,128)(2,1)}, u32[]{:S(2)}, u32[]{:S(2)}) collective-permute-start(bf16[4,64,384]{2,1,0:T(8,128)(2,1)} %pad_maximum_fusion.18), channel_id=1, source_target_pairs={{0,8},{2,10},{4,12},{6,14},{8,0},{10,2},{12,4},{14,6},{16,24},{18,... | collective-permute-start | bytes 589832 | tf_op jit(solution)/shard_map/ppermute | solution.py:586
  34.3 9.0 %collective-permute-start.9 = (bf16[4,64,384]{2,1,0:T(8,128)(2,1)}, bf16[4,64,384]{2,1,0:T(8,128)(2,1)}, u32[]{:S(2)}, u32[]{:S(2)}) collective-permute-start(bf16[4,64,384]{2,1,0:T(8,128)(2,1)} %pad_maximum_fusion.17), channel_id=1, source_target_pairs={{0,8},{2,10},{4,12},{6,14},{8,0},{10,2},{12,4},{14,6},{16,24},{18,... | collective-permute-start | bytes 589832 | tf_op jit(solution)/shard_map/ppermute | solution.py:586
  36.1 10.8 %collective-permute-start.3 = (bf16[4,64,768]{2,1,0:T(8,128)(2,1)}, bf16[4,64,768]{2,1,0:T(8,128)(2,1)}, u32[]{:S(2)}, u32[]{:S(2)}) collective-permute-start(bf16[4,64,768]{2,1,0:T(8,128)(2,1)} %pad_maximum_fusion.8), channel_id=1, source_target_pairs={{0,4},{2,6},{4,0},{6,2},{8,12},{10,14},{12,8},{14,10},{16,20},{18,... | collective-permute-start | bytes 1179656 | tf_op jit(solution)/shard_map/ppermute | solution.py:586
  38.4 10.5 %collective-permute-start.6 = (bf16[4,64,768]{2,1,0:T(8,128)(2,1)}, bf16[4,64,768]{2,1,0:T(8,128)(2,1)}, u32[]{:S(2)}, u32[]{:S(2)}) collective-permute-start(bf16[4,64,768]{2,1,0:T(8,128)(2,1)} %pad_maximum_fusion.9), channel_id=1, source_target_pairs={{0,2},{2,0},{4,6},{6,4},{8,10},{10,8},{12,14},{14,12},{16,18},{18,... | collective-permute-start | bytes 1179656 | tf_op jit(solution)/shard_map/ppermute | solution.py:586
  50.8 22.5 %collective-permute-start.13 = (bf16[8,64,768]{2,1,0:T(8,128)(2,1)}, bf16[8,64,768]{2,1,0:T(8,128)(2,1)}, u32[]{:S(2)}, u32[]{:S(2)}) collective-permute-start(bf16[8,64,768]{2,1,0:T(8,128)(2,1)} %pad_maximum_fusion.5.refs_0_), channel_id=1, source_target_pairs={{0,2},{2,0},{4,6},{6,4},{8,10},{10,8},{12,14},{14,12},{16,18},{18,... | collective-permute-start | bytes 2359304 | tf_op jit(solution)/shard_map/ppermute | solution.py:586
  52.3 26.1 %collective-permute-start.14 = (bf16[8,64,768]{2,1,0:T(8,128)(2,1)}, bf16[8,64,768]{2,1,0:T(8,128)(2,1)}, u32[]{:S(2)}, u32[]{:S(2)}) collective-permute-start(bf16[8,64,768]{2,1,0:T(8,128)(2,1)} %pad_maximum_fusion.6.refs_2_), channel_id=1, source_target_pairs={{0,8},{2,10},{4,12},{6,14},{8,0},{10,2},{12,4},{14,6},{16,24},{18,... | collective-permute-start | bytes 2359304 | tf_op jit(solution)/shard_map/ppermute | solution.py:586
  53.1 12.4 %collective-permute-start.15 = (bf16[8,64,384]{2,1,0:T(8,128)(2,1)}, bf16[8,64,384]{2,1,0:T(8,128)(2,1)}, u32[]{:S(2)}, u32[]{:S(2)}) collective-permute-start(bf16[8,64,384]{2,1,0:T(8,128)(2,1)} %pad_maximum_fusion.10.refs_4_), channel_id=1, source_target_pairs={{0,4},{2,6},{4,0},{6,2},{8,12},{10,14},{12,8},{14,10},{16,20},{18,... | collective-permute-start | bytes 1179656 | tf_op jit(solution)/shard_map/ppermute | solution.py:586
  54.6 18.7 %collective-permute-start.16 = (bf16[8,64,384]{2,1,0:T(8,128)(2,1)}, bf16[8,64,384]{2,1,0:T(8,128)(2,1)}, u32[]{:S(2)}, u32[]{:S(2)}) collective-permute-start(bf16[8,64,384]{2,1,0:T(8,128)(2,1)} %pad_maximum_fusion.11.refs_6_), channel_id=1, source_target_pairs={{0,4},{2,6},{4,0},{6,2},{8,12},{10,14},{12,8},{14,10},{16,20},{18,... | collective-permute-start | bytes 1179656 | tf_op jit(solution)/shard_map/ppermute | solution.py:586
  55.2 502.9 %reduce-scatter.2.cloned.1.call-start = ((), (), s32[]{:S(2)}) async-start(), calls=%async_computation.2 | async-start | bytes 6684672 | tf_op jit(solution)/shard_map/reduce_scatter | solution.py:863
  78.5 8.2 %collective-permute-start.19 = (bf16[1,64,256]{2,1,0:T(8,128)(2,1)S(1)}, bf16[1,64,256]{2,1,0:T(8,128)(2,1)S(1)}, u32[]{:S(2)}, u32[]{:S(2)}) collective-permute-start(bf16[1,64,256]{2,1,0:T(8,128)(2,1)S(1)} %bitcast.140), channel_id=1, source_target_pairs={{0,16},{2,18},{4,20},{6,22},{8,24},{10,26},{12,28},{14,30},{16,0},... | collective-permute-start | bytes 98312 | tf_op jit(solution)/shard_map/ppermute | solution.py:586
  97.0 14.2 %collective-permute-start.22 = (bf16[2,64,256]{2,1,0:T(8,128)(2,1)S(1)}, bf16[2,64,256]{2,1,0:T(8,128)(2,1)S(1)}, u32[]{:S(2)}, u32[]{:S(2)}) collective-permute-start(bf16[2,64,256]{2,1,0:T(8,128)(2,1)S(1)} %pad_maximum_fusion.26), channel_id=1, source_target_pairs={{0,2},{2,0},{4,6},{6,4},{8,10},{10,8},{12,14},{14,12},{16,18},{18,... | collective-permute-start | bytes 196616 | tf_op jit(solution)/shard_map/ppermute | solution.py:586
  97.0 14.2 %collective-permute-start.21 = (bf16[2,32,768]{2,1,0:T(8,128)(2,1)S(1)}, bf16[2,32,768]{2,1,0:T(8,128)(2,1)S(1)}, u32[]{:S(2)}, u32[]{:S(2)}) collective-permute-start(bf16[2,32,768]{2,1,0:T(8,128)(2,1)S(1)} %pad_maximum_fusion.25), channel_id=1, source_target_pairs={{0,4},{2,6},{4,0},{6,2},{8,12},{10,14},{12,8},{14,10},{16,20},{18,... | collective-permute-start | bytes 294920 | tf_op jit(solution)/shard_map/ppermute | solution.py:586
  98.4 12.8 %collective-permute-start.20 = (bf16[2,32,768]{2,1,0:T(8,128)(2,1)S(1)}, bf16[2,32,768]{2,1,0:T(8,128)(2,1)S(1)}, u32[]{:S(2)}, u32[]{:S(2)}) collective-permute-start(bf16[2,32,768]{2,1,0:T(8,128)(2,1)S(1)} %pad_maximum_fusion.24), channel_id=1, source_target_pairs={{0,8},{2,10},{4,12},{6,14},{8,0},{10,2},{12,4},{14,6},{16,24},{18,... | collective-permute-start | bytes 294920 | tf_op jit(solution)/shard_map/ppermute | solution.py:586
  111.3 28.2 %collective-permute-start.25 = (bf16[4,64,256]{2,1,0:T(8,128)(2,1)S(1)}, bf16[4,64,256]{2,1,0:T(8,128)(2,1)S(1)}, u32[]{:S(2)}, u32[]{:S(2)}) collective-permute-start(bf16[4,64,256]{2,1,0:T(8,128)(2,1)S(1)} %pad_maximum_fusion.21), channel_id=1, source_target_pairs={{0,8},{2,10},{4,12},{6,14},{8,0},{10,2},{12,4},{14,6},{16,24},{18,... | collective-permute-start | bytes 393224 | tf_op jit(solution)/shard_map/ppermute | solution.py:586
  112.2 28.1 %collective-permute-start.24 = (bf16[4,32,768]{2,1,0:T(8,128)(2,1)S(1)}, bf16[4,32,768]{2,1,0:T(8,128)(2,1)S(1)}, u32[]{:S(2)}, u32[]{:S(2)}) collective-permute-start(bf16[4,32,768]{2,1,0:T(8,128)(2,1)S(1)} %pad_maximum_fusion.20), channel_id=1, source_target_pairs={{0,2},{2,0},{4,6},{6,4},{8,10},{10,8},{12,14},{14,12},{16,18},{18,... | collective-permute-start | bytes 589832 | tf_op jit(solution)/shard_map/ppermute | solution.py:586
  114.2 26.9 %collective-permute-start.23 = (bf16[4,32,768]{2,1,0:T(8,128)(2,1)S(1)}, bf16[4,32,768]{2,1,0:T(8,128)(2,1)S(1)}, u32[]{:S(2)}, u32[]{:S(2)}) collective-permute-start(bf16[4,32,768]{2,1,0:T(8,128)(2,1)S(1)} %pad_maximum_fusion.19), channel_id=1, source_target_pairs={{0,4},{2,6},{4,0},{6,2},{8,12},{10,14},{12,8},{14,10},{16,20},{18,... | collective-permute-start | bytes 589832 | tf_op jit(solution)/shard_map/ppermute | solution.py:586
  141.9 39.3 %collective-permute-start.26 = (bf16[8,32,768]{2,1,0:T(8,128)(2,1)}, bf16[8,32,768]{2,1,0:T(8,128)(2,1)}, u32[]{:S(2)}, u32[]{:S(2)}) collective-permute-start(bf16[8,32,768]{2,1,0:T(8,128)(2,1)} %pad_maximum_fusion.12.refs_0_), channel_id=1, source_target_pairs={{0,2},{2,0},{4,6},{6,4},{8,10},{10,8},{12,14},{14,12},{16,18},{18,... | collective-permute-start | bytes 1179656 | tf_op jit(solution)/shard_map/ppermute | solution.py:586
  142.1 39.0 %collective-permute-start.27 = (bf16[8,32,768]{2,1,0:T(8,128)(2,1)}, bf16[8,32,768]{2,1,0:T(8,128)(2,1)}, u32[]{:S(2)}, u32[]{:S(2)}) collective-permute-start(bf16[8,32,768]{2,1,0:T(8,128)(2,1)} %pad_maximum_fusion.13.refs_2_), channel_id=1, source_target_pairs={{0,8},{2,10},{4,12},{6,14},{8,0},{10,2},{12,4},{14,6},{16,24},{18,... | collective-permute-start | bytes 1179656 | tf_op jit(solution)/shard_map/ppermute | solution.py:586
  143.4 37.7 %collective-permute-start.28 = (bf16[8,64,256]{2,1,0:T(8,128)(2,1)}, bf16[8,64,256]{2,1,0:T(8,128)(2,1)}, u32[]{:S(2)}, u32[]{:S(2)}) collective-permute-start(bf16[8,64,256]{2,1,0:T(8,128)(2,1)} %pad_maximum_fusion.14.refs_4_), channel_id=1, source_target_pairs={{0,4},{2,6},{4,0},{6,2},{8,12},{10,14},{12,8},{14,10},{16,20},{18,... | collective-permute-start | bytes 786440 | tf_op jit(solution)/shard_map/ppermute | solution.py:586
  187.3 17.6 %collective-permute-start.32 = (bf16[1024,1024]{1,0:T(8,128)(2,1)}, bf16[1024,1024]{1,0:T(8,128)(2,1)}, u32[]{:S(2)}, u32[]{:S(2)}) collective-permute-start(bf16[1024,1024]{1,0:T(8,128)(2,1)} %param.24), channel_id=1, source_target_pairs={{0,1},{1,0},{2,3},{3,2},{4,5},{5,4},{6,7},{7,6},{8,9},{9,8},{10,11... | collective-permute-start | bytes 6291464 | tf_op jit(solution)/shard_map/ppermute | solution.py:586
  248.0 23.1 %collective-permute-start.33 = (bf16[1024,1024]{1,0:T(8,128)(2,1)S(1)}, bf16[1024,1024]{1,0:T(8,128)(2,1)S(1)}, u32[]{:S(2)}, u32[]{:S(2)}) collective-permute-start(bf16[1024,1024]{1,0:T(8,128)(2,1)S(1)} %add_convert_fusion.1), channel_id=1, source_target_pairs={{0,1},{1,0},{2,3},{3,2},{4,5},{5,4},{6,7},{7,6},{8,9},{9,8},{10,11... | collective-permute-start | bytes 6291464 | tf_op jit(solution)/shard_map/ppermute | solution.py:586
  252.3 43.2 %collective-permute-start.31 = (bf16[1024,1024]{1,0:T(8,128)(2,1)}, bf16[1024,1024]{1,0:T(8,128)(2,1)}, u32[]{:S(2)}, u32[]{:S(2)}) collective-permute-start(bf16[1024,1024]{1,0:T(8,128)(2,1)} %fusion.37), channel_id=1, source_target_pairs={{0,1},{1,0},{2,3},{3,2},{4,5},{5,4},{6,7},{7,6},{8,9},{9,8},{10,11... | collective-permute-start | bytes 6291464 | tf_op jit(solution)/shard_map/ppermute | solution.py:586
  281.5 21.8 %collective-permute-start.34 = (bf16[1024,1024]{1,0:T(8,128)(2,1)}, bf16[1024,1024]{1,0:T(8,128)(2,1)}, u32[]{:S(2)}, u32[]{:S(2)}) collective-permute-start(bf16[1024,1024]{1,0:T(8,128)(2,1)} %get-tuple-element.326), channel_id=1, source_target_pairs={{0,1},{1,0},{2,3},{3,2},{4,5},{5,4},{6,7},{7,6},{8,9},{9,8},{10,11... | collective-permute-start | bytes 6291464 | tf_op jit(solution)/shard_map/ppermute | solution.py:586
  320.2 46.7 %collective-permute-start.37 = (bf16[2,2,1,2,64,256]{5,4,3,2,1,0:T(8,128)(2,1)S(1)}, bf16[2,2,1,2,64,256]{5,4,3,2,1,0:T(8,128)(2,1)S(1)}, u32[]{:S(2)}, u32[]{:S(2)}) collective-permute-start(bf16[2,2,1,2,64,256]{5,4,3,2,1,0:T(8,128)(2,1)S(1)} %get-tuple-element.166), channel_id=1, source_target_pairs={{0,4},{2,6},{4,0},{6,2},{8,12},{10,14},{12,8},{14,10},{16,20},{18,... | collective-permute-start | bytes 786440 | tf_op jit(solution)/shard_map/ppermute | solution.py:586
  320.2 46.7 %collective-permute-start.36 = (bf16[2,1,2,2,32,768]{5,4,3,2,1,0:T(8,128)(2,1)S(1)}, bf16[2,1,2,2,32,768]{5,4,3,2,1,0:T(8,128)(2,1)S(1)}, u32[]{:S(2)}, u32[]{:S(2)}) collective-permute-start(bf16[2,1,2,2,32,768]{5,4,3,2,1,0:T(8,128)(2,1)S(1)} %get-tuple-element.164), channel_id=1, source_target_pairs={{0,8},{2,10},{4,12},{6,14},{8,0},{10,2},{12,4},{14,6},{16,24},{18,... | collective-permute-start | bytes 1179656 | tf_op jit(solution)/shard_map/ppermute | solution.py:586
  320.3 46.8 %collective-permute-start.35 = (bf16[2,2,2,1,32,768]{5,4,3,2,1,0:T(8,128)(2,1)S(1)}, bf16[2,2,2,1,32,768]{5,4,3,2,1,0:T(8,128)(2,1)S(1)}, u32[]{:S(2)}, u32[]{:S(2)}) collective-permute-start(bf16[2,2,2,1,32,768]{5,4,3,2,1,0:T(8,128)(2,1)S(1)} %get-tuple-element.162), channel_id=1, source_target_pairs={{0,2},{2,0},{4,6},{6,4},{8,10},{10,8},{12,14},{14,12},{16,18},{18,... | collective-permute-start | bytes 1179656 | tf_op jit(solution)/shard_map/ppermute | solution.py:586
  449.4 37.7 %collective-permute-start.38 = (bf16[1024,1024]{1,0:T(8,128)(2,1)}, bf16[1024,1024]{1,0:T(8,128)(2,1)}, u32[]{:S(2)}, u32[]{:S(2)}) collective-permute-start(bf16[1024,1024]{1,0:T(8,128)(2,1)} %add_convert_fusion), channel_id=1, source_target_pairs={{0,1},{1,0},{2,3},{3,2},{4,5},{5,4},{6,7},{7,6},{8,9},{9,8},{10,11... | collective-permute-start | bytes 6291464 | tf_op jit(solution)/shard_map/ppermute | solution.py:586
  455.9 9.0 %collective-permute-start.43 = (bf16[2,2,1,1,32,768]{5,4,3,2,1,0:T(8,128)(2,1)}, bf16[2,2,1,1,32,768]{5,4,3,2,1,0:T(8,128)(2,1)S(1)}, u32[]{:S(2)}, u32[]{:S(2)}) collective-permute-start(bf16[2,2,1,1,32,768]{5,4,3,2,1,0:T(8,128)(2,1)} %get-tuple-element.182), channel_id=1, source_target_pairs={{0,4},{2,6},{4,0},{6,2},{8,12},{10,14},{12,8},{14,10},{16,20},{18,... | collective-permute-start | bytes 589832 | tf_op jit(solution)/shard_map/ppermute | solution.py:586
  458.6 14.4 %collective-permute-start.42 = (bf16[2,2,1,2,64,384]{5,4,3,2,1,0:T(8,128)(2,1)}, bf16[2,2,1,2,64,384]{5,4,3,2,1,0:T(8,128)(2,1)S(1)}, u32[]{:S(2)}, u32[]{:S(2)}) collective-permute-start(bf16[2,2,1,2,64,384]{5,4,3,2,1,0:T(8,128)(2,1)} %get-tuple-element.180), channel_id=1, source_target_pairs={{0,4},{2,6},{4,0},{6,2},{8,12},{10,14},{12,8},{14,10},{16,20},{18,... | collective-permute-start | bytes 1179656 | tf_op jit(solution)/shard_map/ppermute | solution.py:586
  461.7 19.0 %collective-permute-start.41 = (bf16[2,2,1,2,64,384]{5,4,3,2,1,0:T(8,128)(2,1)}, bf16[2,2,1,2,64,384]{5,4,3,2,1,0:T(8,128)(2,1)S(1)}, u32[]{:S(2)}, u32[]{:S(2)}) collective-permute-start(bf16[2,2,1,2,64,384]{5,4,3,2,1,0:T(8,128)(2,1)} %get-tuple-element.178), channel_id=1, source_target_pairs={{0,4},{2,6},{4,0},{6,2},{8,12},{10,14},{12,8},{14,10},{16,20},{18,... | collective-permute-start | bytes 1179656 | tf_op jit(solution)/shard_map/ppermute | solution.py:586
  463.2 19.4 %collective-permute-start.40 = (bf16[2,1,2,2,64,768]{5,4,3,2,1,0:T(8,128)(2,1)}, bf16[2,1,2,2,64,768]{5,4,3,2,1,0:T(8,128)(2,1)S(1)}, u32[]{:S(2)}, u32[]{:S(2)}) collective-permute-start(bf16[2,1,2,2,64,768]{5,4,3,2,1,0:T(8,128)(2,1)} %get-tuple-element.176), channel_id=1, source_target_pairs={{0,8},{2,10},{4,12},{6,14},{8,0},{10,2},{12,4},{14,6},{16,24},{18,... | collective-permute-start | bytes 2359304 | tf_op jit(solution)/shard_map/ppermute | solution.py:586
  464.9 19.9 %collective-permute-start.39 = (bf16[2,2,2,1,64,768]{5,4,3,2,1,0:T(8,128)(2,1)}, bf16[2,2,2,1,64,768]{5,4,3,2,1,0:T(8,128)(2,1)S(1)}, u32[]{:S(2)}, u32[]{:S(2)}) collective-permute-start(bf16[2,2,2,1,64,768]{5,4,3,2,1,0:T(8,128)(2,1)} %get-tuple-element.174), channel_id=1, source_target_pairs={{0,2},{2,0},{4,6},{6,4},{8,10},{10,8},{12,14},{14,12},{16,18},{18,... | collective-permute-start | bytes 2359304 | tf_op jit(solution)/shard_map/ppermute | solution.py:586
  492.3 15.4 %collective-permute-start.53 = (f32[6180]{0:T(1024)S(1)}, f32[6180]{0:T(1024)S(1)}, u32[]{:S(2)}, u32[]{:S(2)}) collective-permute-start(f32[6180]{0:T(1024)S(1)} %concatenate.139), channel_id=1, source_target_pairs={{0,2},{2,0},{4,6},{6,4},{8,10},{10,8},{12,14},{14,12},{16,18},{18,... | collective-permute-start | bytes 74168 | tf_op jit(solution)/shard_map/ppermute | solution.py:586
  494.4 13.7 %collective-permute-start.52 = (bf16[2,1,1,1,64,256]{5,4,3,2,1,0:T(8,128)(2,1)S(1)}, bf16[2,1,1,1,64,256]{5,4,3,2,1,0:T(8,128)(2,1)S(1)}, u32[]{:S(2)}, u32[]{:S(2)}) collective-permute-start(bf16[2,1,1,1,64,256]{5,4,3,2,1,0:T(8,128)(2,1)S(1)} %constant_dynamic-slice_fusion.11), channel_id=1, source_target_pairs={{0,2},{2,0},{4,6},{6,4},{8,10},{10,8},{12,14},{14,12},{16,18},{18,... | collective-permute-start | bytes 196616 | tf_op jit(solution)/shard_map/ppermute | solution.py:586
  495.2 14.2 %collective-permute-start.51 = (bf16[2,1,1,1,32,768]{5,4,3,2,1,0:T(8,128)(2,1)S(1)}, bf16[2,1,1,1,32,768]{5,4,3,2,1,0:T(8,128)(2,1)S(1)}, u32[]{:S(2)}, u32[]{:S(2)}) collective-permute-start(bf16[2,1,1,1,32,768]{5,4,3,2,1,0:T(8,128)(2,1)S(1)} %constant_dynamic-slice_fusion.12), channel_id=1, source_target_pairs={{0,4},{2,6},{4,0},{6,2},{8,12},{10,14},{12,8},{14,10},{16,20},{18,... | collective-permute-start | bytes 294920 | tf_op jit(solution)/shard_map/ppermute | solution.py:586
  497.9 13.3 %collective-permute-start.50 = (bf16[2,1,1,1,32,768]{5,4,3,2,1,0:T(8,128)(2,1)S(1)}, bf16[2,1,1,1,32,768]{5,4,3,2,1,0:T(8,128)(2,1)S(1)}, u32[]{:S(2)}, u32[]{:S(2)}) collective-permute-start(bf16[2,1,1,1,32,768]{5,4,3,2,1,0:T(8,128)(2,1)S(1)} %constant_dynamic-slice_fusion.13), channel_id=1, source_target_pairs={{0,8},{2,10},{4,12},{6,14},{8,0},{10,2},{12,4},{14,6},{16,24},{18,... | collective-permute-start | bytes 294920 | tf_op jit(solution)/shard_map/ppermute | solution.py:586
  498.3 13.0 %collective-permute-start.49 = (bf16[2,1,1,2,64,384]{5,4,3,2,1,0:T(8,128)(2,1)S(1)}, bf16[2,1,1,2,64,384]{5,4,3,2,1,0:T(8,128)(2,1)S(1)}, u32[]{:S(2)}, u32[]{:S(2)}) collective-permute-start(bf16[2,1,1,2,64,384]{5,4,3,2,1,0:T(8,128)(2,1)S(1)} %constant_dynamic-slice_fusion.14), channel_id=1, source_target_pairs={{0,8},{2,10},{4,12},{6,14},{8,0},{10,2},{12,4},{14,6},{16,24},{18,... | collective-permute-start | bytes 589832 | tf_op jit(solution)/shard_map/ppermute | solution.py:586
  508.1 8.8 %collective-permute-start.47 = (bf16[2,1,2,1,64,768]{5,4,3,2,1,0:T(8,128)(2,1)S(1)}, bf16[2,1,2,1,64,768]{5,4,3,2,1,0:T(8,128)(2,1)S(1)}, u32[]{:S(2)}, u32[]{:S(2)}) collective-permute-start(bf16[2,1,2,1,64,768]{5,4,3,2,1,0:T(8,128)(2,1)S(1)} %constant_dynamic-slice_fusion.16), channel_id=1, source_target_pairs={{0,2},{2,0},{4,6},{6,4},{8,10},{10,8},{12,14},{14,12},{16,18},{18,... | collective-permute-start | bytes 1179656 | tf_op jit(solution)/shard_map/ppermute | solution.py:586
  509.4 8.8 %collective-permute-start.46 = (bf16[2,2,1,1,64,768]{5,4,3,2,1,0:T(8,128)(2,1)S(1)}, bf16[2,2,1,1,64,768]{5,4,3,2,1,0:T(8,128)(2,1)S(1)}, u32[]{:S(2)}, u32[]{:S(2)}) collective-permute-start(bf16[2,2,1,1,64,768]{5,4,3,2,1,0:T(8,128)(2,1)S(1)} %constant_dynamic-slice_fusion.17), channel_id=1, source_target_pairs={{0,4},{2,6},{4,0},{6,2},{8,12},{10,14},{12,8},{14,10},{16,20},{18,... | collective-permute-start | bytes 1179656 | tf_op jit(solution)/shard_map/ppermute | solution.py:586
  536.5 18.9 %collective-permute-start.69 = (bf16[1,1,1,1,64,768]{5,4,3,2,1,0:T(8,128)(2,1)S(1)}, bf16[1,1,1,1,64,768]{5,4,3,2,1,0:T(8,128)(2,1)S(1)}, u32[]{:S(2)}, u32[]{:S(2)}) collective-permute-start(bf16[1,1,1,1,64,768]{5,4,3,2,1,0:T(8,128)(2,1)S(1)} %constant_dynamic-slice_fusion), channel_id=1, source_target_pairs={{0,16},{2,18},{4,20},{6,22},{8,24},{10,26},{12,28},{14,30},{16,0},... | collective-permute-start | bytes 294920 | tf_op jit(solution)/shard_map/ppermute | solution.py:586
  536.8 19.3 %collective-permute-start.68 = (bf16[1,1,1,1,64,768]{5,4,3,2,1,0:T(8,128)(2,1)S(1)}, bf16[1,1,1,1,64,768]{5,4,3,2,1,0:T(8,128)(2,1)S(1)}, u32[]{:S(2)}, u32[]{:S(2)}) collective-permute-start(bf16[1,1,1,1,64,768]{5,4,3,2,1,0:T(8,128)(2,1)S(1)} %constant_dynamic-slice_fusion.1), channel_id=1, source_target_pairs={{0,16},{2,18},{4,20},{6,22},{8,24},{10,26},{12,28},{14,30},{16,0},... | collective-permute-start | bytes 294920 | tf_op jit(solution)/shard_map/ppermute | solution.py:586
  548.0 8.8 %collective-permute-start.67 = (bf16[64,512]{1,0:T(8,128)(2,1)S(1)}, bf16[64,512]{1,0:T(8,128)(2,1)S(1)}, u32[]{:S(2)}, u32[]{:S(2)}) collective-permute-start(bf16[64,512]{1,0:T(8,128)(2,1)S(1)} %pad_maximum_fusion.27), channel_id=1, source_target_pairs={{0,1},{1,0},{2,3},{3,2},{4,5},{5,4},{6,7},{7,6},{8,9},{9,8},{10,11... | collective-permute-start | bytes 196616 | tf_op jit(solution)/shard_map/ppermute | solution.py:586
  (90 other events, 1463.5 us)
Sparse Core Ops, SparseCore 0:
  55.4 106.6 all-gather.1
  295.6 149.0 reduce-scatter.1

commit v2 on v1

--- a/solution.py
+++ b/solution.py
@@ -685,6 +685,13 @@
     return x
 
 
+def sum_bits(x, axis, bits):
+    total = x
+    for bit in bits + ([bits[0] | bits[1]] if len(bits) == 2 else []):
+        total = total + permute_bit(x, axis, bit)
+    return total
+
+
 def tensor_gather(x, natural):
     n = lax.axis_size("tensor")
     rank = lax.axis_index("tensor")
@@ -700,7 +707,7 @@
     return x
 
 
-def tensor_scatter(product, arrays, natural):
+def tensor_scatter(product, arrays, natural, late=lambda arrays: arrays):
     n = lax.axis_size("tensor")
     rank = lax.axis_index("tensor")
     if n == 2:
@@ -710,8 +717,9 @@
         mine, other = (rank, 1 - rank) if natural else (0, 1)
         send = product(*[cut(a, other) for a in arrays]).astype(BF16)
         arrived = permute_bit(send, "tensor", 1)
+        arrays = late(arrays)
         return product(*[cut(a, mine) for a in arrays]) + arrived.astype(F32)
-    x = product(*arrays)
+    x = product(*late(arrays))
     bit = n // 2
     while bit >= 1:
         half = x.shape[0] // 2
@@ -894,8 +902,27 @@
     halves1 = [reduce_halves(reduce_open(p, "dp", 0, block_rows), "dp", orders[j][-1]) for p, j in pieces1]
     mix_grad_late, halves1 = lax.optimization_barrier((mix_grad, halves1))
     held1 = [reduce_step(h, "dp", orders[p[1]][-1], False) for h, p in zip(halves1, pieces1)]
+    cur = held1 + held2
+    bits_left = [list(reversed(orders[p[1]][:-1])) for p in pieces1]
+    bits_left += [list(reversed(orders[p[3]][:-2])) for p in pieces2]
+
+    def late(arrays):
+        nonlocal cur
+        arrays, cur = lax.optimization_barrier((arrays, cur))
+        cur = tail_step(cur)
+        return arrays
+
+    def tail_step(cur):
+        out = []
+        for c, bits in zip(cur, bits_left):
+            if bits:
+                bit = bits.pop(0)
+                c = reduce_step(reduce_halves(c, "dp", bit), "dp", bit, not bits)
+            out.append(c)
+        return out
+
     normed_grad = tensor_scatter(
-        lambda a, b: dot_nt(a, qkv_w) + dot_nt(b, mix_w), (qkv_grad, mix_grad_late), True)
+        lambda a, b: dot_nt(a, qkv_w) + dot_nt(b, mix_w), (qkv_grad, mix_grad_late), True, late)
     norm_into, norm_gain_part = norm_back(tokens, inverse, norm_gain, normed_grad)
     input_grad = middle_grad + norm_into
 
@@ -906,18 +933,11 @@
         conv_part.reshape(-1), heads_part, state_conv_part.reshape(-1), ffn_gain_part,
         norm_gain_part])
     small_bits = list(bit_orders("dp")[0])
-    tail = [(c, list(reversed(orders[p[1]][:-1]))) for c, p in zip(held1, pieces1)]
-    tail += [(c, list(reversed(orders[p[3]][:-2]))) for c, p in zip(held2, pieces2)]
-    cur = [c for c, _ in tail]
-    for k in range(steps - 1):
+    for _ in range(steps - 2):
         cur, small = lax.optimization_barrier((cur, small))
-        bit = small_bits.pop()
-        small = small + permute_bit(small, "dp", bit)
-        cur = [
-            reduce_step(reduce_halves(c, "dp", bits[k]), "dp", bits[k], k == len(bits) - 1)
-            if k < len(bits) else c for c, (_, bits) in zip(cur, tail)]
-    while small_bits:
-        small = small + permute_bit(small, "dp", small_bits.pop())
+        if small_bits:
+            small = sum_bits(small, "dp", [small_bits.pop() for _ in range(min(2, len(small_bits)))])
+        cur = tail_step(cur)
     sums = [c.reshape(c.shape[-2:]) for c in cur]
     mix_sum = jnp.concatenate(sums[:len(mix_cols)], axis=1)
     qkv_sum = sums[len(mix_cols)]

time: 572 us -> 566 us (0.990)
  starting transfers between devices: 73.2 us -> 88.4 us
  Pallas kernels: 162 us -> 150 us
  waiting for transfers between devices: 57.9 us -> 46.9 us
    ppermute x70 -> x72, starting transfers between devices: 72.9 us -> 88.1 us  [permute_bit(): return lax.ppermute(x, axis, [(i, i ^ bit) for i in range(n)])]
    ppermute x70 -> x72, waiting for transfers between devices: 57.8 us -> 46.9 us  [permute_bit(): return lax.ppermute(x, axis, [(i, i ^ bit) for i in range(n)])]
    pallas_call x1, Pallas kernels: 43 us -> 36.1 us  [attend_bwd(): pl.pallas_call(functools.partial(attend_bwd_kernel, heads), grid_spec=plt...]
    unnamed x136 -> x134, local copies, waits for them, and re-layouts: 13.5 us -> 14 us
  transfers between devices with their start and end apart: 72 -> 74, of which waited for: 18 -> 16; matrix products, arithmetic and copies ran while one was open for 36% -> 37% of each run, Pallas kernels for 29% -> 27%
where the time goes in v2:
time: 566 us; the launch traced here: 562 us
  matrix products  153 us (27%)
  Pallas kernels  150 us (27%)
  starting transfers between devices  88.4 us (16%)
  other arithmetic  71 us (13%)
  waiting for transfers between devices  46.9 us (8%)
  local copies, waits for them, and re-layouts  36.9 us (7%)
  between operations  16.1 us (3%)
    ppermute x72, starting transfers between devices, permute_bit(): return lax.ppermute(x, axis, [(i, i ^ bit) for i in range(n)])  88.1 us
    dot_general x14, matrix products, dot_nt(): lax.dot_general(left, right, (((1,), (1,)), ((), ())), preferred_element_...  56.8 us
    dot_general x7, matrix products, dot_nn(): lax.dot_general(left, right, (((1,), (0,)), ((), ())), preferred_element_...  56 us
    pallas_call x1, Pallas kernels, mix_bwd(): pl.pallas_call(functools.partial(mix_bwd_kernel, heads), grid=(seqs, per)...  55.7 us
    ppermute x72, waiting for transfers between devices, permute_bit(): return lax.ppermute(x, axis, [(i, i ^ bit) for i in range(n)])  46.9 us
    dot_general x9, matrix products, dot_tn(): lax.dot_general(left, right, (((0,), (0,)), ((), ())), preferred_element_...  40 us
    pallas_call x1, Pallas kernels, attend_bwd(): pl.pallas_call(functools.partial(attend_bwd_kernel, heads), grid_spec=plt...  36.1 us
    pallas_call x1, Pallas kernels, attend_fwd(): pl.pallas_call(functools.partial(attend_fwd_kernel, heads), grid_spec=plt...  24.4 us
  transfers between devices with their start and end apart: 74, of which 16 were waited for; matrix products, arithmetic and copies ran while one was open for 37% of the time, Pallas kernels for 27%

profile of v2, /device:TPU:0, one launch (start us, length us, event | category | flops | bytes accessed | tf_op | source)
XLA Modules:
  0.0 562.1 jit_solution(15967486613314444797)
XLA Ops:
  9.2 4.0 collective-permute-start.10
  20.4 3.5 fusion.10
  55.5 5.3 multiply_sine_fusion
  60.9 4.7 collective-permute-done.15.refs_5_
  65.6 7.8 %collective-permute-done.16.refs_7_ = bf16[8,64,384]{2,1,0:T(8,128)(2,1)} collective-permute-done((bf16[8,64,384]{2,1,0:T(8,128)(2,1)}, bf16[8,64,384]{2,1,0:T(8,128)(2,1)}, u32[]{:S(2)}, u32[]{:S(2)}) %collective-permute-start.16) | collective-permute-done | bytes 393248 | tf_op jit(solution)/shard_map/ppermute | solution.py:586
  73.3 5.5 collective-permute-done.14.refs_3_
  83.8 2.9 assemble.2
  87.7 3.2 broadcast_select_fusion.3
  92.9 4.1 fusion.97.qkv_ref
  99.6 11.5 %fusion.107.pre_ref.pre_prev_ref = f32[2048,1920]{1,0:T(8,128)} fusion(bf16[2048,1024]{1,0:T(8,128)(2,1)S(1)} %pad_maximum_fusion.1, bf16[1024,1920]{1,0:T(8,128)(2,1)S(1)} %get-tuple-element.136), kind=kOutput, calls=%fused_computation.265 | convolution fusion | flops 8053063680 | bytes 23855104 | tf_op jit(solution)/shard_map/dot_general | solution.py:25
  114.8 23.1 %mix_fwd.1 = (bf16[2048,768]{1,0:T(8,128)(2,1)S(1)}, f32[2048,768]{1,0:T(8,128)}, f32[16,128,768]{2,1,0:T(8,128)}) custom-call(s32[2048,1]{1,0:T(8,128)S(1)} %copy.103.seg_ref, s32[16,1,128]{2,1,0:T(1,128)S(1)} %bitcast.111, f32[2048,8]{1,0:T(8,128)S(1)} %convert_element_type.419.mask_ref, f32[2048,1920]{1,0:T(8,128)} %fusion.107.pre_ref.pre_prev_ref, ...), custom_call_target="tpu_custom_call" | custom-call | flops 1887436800 | bytes 34603008 | tf_op jit(solution)/shard_map/mix_fwd/pallas_call | solution.py:377
  145.9 5.6 rope.1
  151.6 24.4 %attend_fwd.1 = (bf16[2048,256]{1,0:T(8,128)(2,1)S(1)}, f32[4,4,512]{2,1,0:T(4,128)S(1)}) custom-call(s32[4]{0:T(128)S(1)} %and_select_fusion.1.first_ref, bf16[2048,256]{1,0:T(8,128)(2,1)S(1)} %get-tuple-element.146.q_ref, bf16[2048,64]{1,0:T(8,128)(2,1)S(1)} %get-tuple-element.147.k_ref, bf16[2048,128]{1,0:T(8,128)(2,1)S(1)} %get-tuple-element.148.v_ref, ...), custom_call_target="tpu_custom_call" | custom-call | flops 2147483648 | bytes 2097152 | tf_op jit(solution)/shard_map/attend_fwd/pallas_call | solution.py:121
  185.1 3.8 fusion.64
  188.9 4.0 multiply_reduce_fusion.2
  196.7 3.1 constant_dynamic-update-slice_fusion.1
  199.8 3.1 constant_dynamic-update-slice_fusion
  202.9 9.5 %convolution_convert_fusion.1 = bf16[2048,1024]{1,0:T(8,128)(2,1)} fusion(bf16[1024,3072]{1,0:T(8,128)(2,1)} %all-gather.2.cloned.1.call-done, bf16[1024,1024]{1,0:T(8,128)(2,1)} %collective-permute-done.30, bf16[1024,1024]{1,0:T(8,128)(2,1)} %multiply_convert_fusion.1), kind=kOutput, calls=%fused_computation.49 | convolution fusion | flops 4305453056 | bytes 10485760 | tf_op jit(solution)/shard_map/dot_general | solution.py:25
  212.4 8.8 %convolution_convert_fusion = bf16[2048,1024]{1,0:T(8,128)(2,1)} fusion(bf16[1024,3072]{1,0:T(8,128)(2,1)S(1)} %copy-done.58, bf16[1024,1024]{1,0:T(8,128)(2,1)} %collective-permute-done.30, bf16[1024,1024]{1,0:T(8,128)(2,1)} %multiply_convert_fusion.1), kind=kOutput, calls=%fused_computation.48 | convolution fusion | flops 4305453056 | bytes 10485760 | tf_op jit(solution)/shard_map/dot_general | solution.py:25
  221.2 13.8 %fusion.2 = (bf16[2048,1024]{1,0:T(8,128)(2,1)S(1)}, bf16[2048,1024]{1,0:T(8,128)(2,1)}, bf16[2048,1024]{1,0:T(8,128)(2,1)S(1)}) fusion(bf16[2048,1024]{1,0:T(8,128)(2,1)} %convolution_convert_fusion, bf16[2048,1024]{1,0:T(8,128)(2,1)} %convolution_convert_fusion.1, bf16[2048,1024]{1,0:T(8,128)(2,1)} %constant_dynamic-update-slice_fusion, ...), kind=kOutput, calls=%fused_computation.13 | convolution fusion | flops 4330618880 | bytes 27262976 | tf_op jit(solution)/shard_map/dot_general | solution.py:25
  235.0 5.5 fusion.25
  243.5 3.7 fusion.37
  247.3 4.4 fusion.29
  251.6 7.2 %convolution_convert_fusion.5 = bf16[1024,1024]{1,0:T(8,128)(2,1)S(1)} fusion(bf16[2048,1024]{1,0:T(8,128)(2,1)S(1)} %get-tuple-element.332, bf16[1024,1024]{1,0:T(8,128)(2,1)} %collective-permute-done.30, bf16[1024,1024]{1,0:T(8,128)(2,1)} %multiply_convert_fusion.1), kind=kOutput, calls=%fused_computation.74 | convolution fusion | flops 4304404480 | bytes 10485760 | tf_op jit(solution)/shard_map/dot_general | solution.py:33
  258.8 7.2 %convolution_convert_fusion.3 = bf16[1024,1024]{1,0:T(8,128)(2,1)S(1)} fusion(bf16[2048,1024]{1,0:T(8,128)(2,1)} %constant_dynamic-update-slice_fusion, bf16[2048,1024]{1,0:T(8,128)(2,1)S(1)} %copy-done.62), kind=kOutput, calls=%fused_computation.72 | convolution fusion | flops 4296015872 | bytes 10485760 | tf_op jit(solution)/shard_map/dot_general | solution.py:33
  266.0 6.2 %multiply_reduce_fusion = (f32[1024]{0:T(1024)}, f32[1024]{0:T(1024)S(1)}, f32[1024,1024]{1,0:T(8,128)S(1)}) fusion(f32[1024,1024]{1,0:T(8,128)S(1)} %copy-done.32, f32[1024]{0:T(1024)S(1)} %get-tuple-element.393, f32[1024]{0:T(1024)S(1)} %copy-done.54, bf16[1024,1024]{1,0:T(8,128)(2,1)S(1)} %collective-permute-done.33, f32[1024,1024]{1,0:T(8,128)} %fusion.29, ...), kind=kOutput, calls=%fused_computation.33 | convolution fusion | flops 2156918784 | bytes 18890752 | tf_op jit(solution)/shard_map/dot_general | solution.py:29
  272.3 4.7 fusion.99
  277.4 7.0 %convolution_convert_fusion.4 = bf16[1024,1024]{1,0:T(8,128)(2,1)S(1)} fusion(bf16[2048,1024]{1,0:T(8,128)(2,1)S(1)} %copy-done.64, bf16[1024,1024]{1,0:T(8,128)(2,1)} %collective-permute-done.30, bf16[1024,1024]{1,0:T(8,128)(2,1)} %multiply_convert_fusion.1), kind=kOutput, calls=%fused_computation.73 | convolution fusion | flops 4304404480 | bytes 10485760 | tf_op jit(solution)/shard_map/dot_general | solution.py:33
  284.5 6.4 %pad_maximum_fusion = bf16[16,192,1024]{2,1,0:T(8,128)(2,1)} fusion(bf16[16,64,1024]{2,1,0:T(8,128)(2,1)S(1)} %bitcast.117, bf16[16,64,1024]{2,1,0:T(8,128)(2,1)S(1)} %bitcast.118, bf16[16,64,1024]{2,1,0:T(8,128)(2,1)S(1)} %bitcast.116), kind=kLoop, calls=%fused_computation.20 | loop fusion | flops 18874368 | bytes 12582912 | tf_op jit(solution)/shard_map/concatenate | solution.py:872
  290.9 7.8 %add_convert_fusion.2 = bf16[1024,1024]{1,0:T(8,128)(2,1)} fusion(f32[1024,1024]{1,0:T(8,128)} %copy-done.31, bf16[1024,1024]{1,0:T(8,128)(2,1)} %collective-permute-done.31, bf16[1024,3072]{1,0:T(8,128)(2,1)} %all-gather.2.cloned.1.call-done, bf16[2048,1024]{1,0:T(8,128)(2,1)} %copy-done.61), kind=kOutput, calls=%fused_computation.40 | convolution fusion | flops 2151677952 | bytes 12582912 | tf_op jit(solution)/shard_map/dot_general | solution.py:29
  303.1 3.7 convolution_convert_fusion.6
  308.2 7.0 %fusion.96.dout_ref = f32[2048,768]{1,0:T(8,128)} fusion(bf16[1024,768]{1,0:T(8,128)(2,1)S(1)} %copy-done.21, bf16[1024,1024]{1,0:T(8,128)(2,1)S(1)} %get-tuple-element.336, bf16[1024,1024]{1,0:T(8,128)(2,1)S(1)} %get-tuple-element.335), kind=kOutput, calls=%fused_computation.254 | convolution fusion | flops 3229614080 | bytes 12058624 | tf_op jit(solution)/shard_map/dot_general | solution.py:25
  317.0 6.4 %collective-permute-start.35 = (bf16[2,2,2,1,32,768]{5,4,3,2,1,0:T(8,128)(2,1)S(1)}, bf16[2,2,2,1,32,768]{5,4,3,2,1,0:T(8,128)(2,1)S(1)}, u32[]{:S(2)}, u32[]{:S(2)}) collective-permute-start(bf16[2,2,2,1,32,768]{5,4,3,2,1,0:T(8,128)(2,1)S(1)} %get-tuple-element.163), channel_id=1, source_target_pairs={{0,2},{2,0},{4,6},{6,4},{8,10},{10,8},{12,14},{14,12},{16,18},{18,... | collective-permute-start | bytes 1179656 | tf_op jit(solution)/shard_map/ppermute | solution.py:586
  323.4 36.1 %attend_bwd.1 = (bf16[2048,256]{1,0:T(8,128)(2,1)S(1)}, bf16[2048,64]{1,0:T(8,128)(2,1)S(1)}, bf16[2048,64]{1,0:T(8,128)(2,1)S(1)}) custom-call(s32[4]{0:T(128)S(1)} %and_select_fusion.1.first_ref, bf16[2048,256]{1,0:T(8,128)(2,1)S(1)} %copy-done.23, bf16[2048,64]{1,0:T(8,128)(2,1)S(1)} %copy-done.25, bf16[2048,128]{1,0:T(8,128)(2,1)S(1)} %copy-done.27, ...), custom_call_target="tpu_custom_call" | custom-call | flops 5368709120 | bytes 4194304 | tf_op jit(solution)/shard_map/attend_bwd/pallas_call | solution.py:220
  362.7 55.7 %mix_bwd.1 = (bf16[2048,1920]{1,0:T(8,128)(2,1)}, f32[4,768]{1,0:T(4,128)S(1)}, f32[4,256]{1,0:T(4,128)S(1)}, f32[8,128]{1,0:T(8,128)S(1)}, f32[1,768]{1,0:T(1,128)S(1)}) custom-call(s32[2048,1]{1,0:T(8,128)S(1)} %copy-done.1, s32[16,1,128]{2,1,0:T(1,128)S(1)} %bitcast.114, f32[2048,8]{1,0:T(8,128)S(1)} %convert_element_type.419.mask_ref, ...), custom_call_target="tpu_custom_call" | custom-call | flops 4718592000 | bytes 44040192 | tf_op jit(solution)/shard_map/mix_bwd/pallas_call | solution.py:537
  418.4 4.0 fusion.66
  422.4 3.6 fusion.43
  426.0 3.6 fusion.40
  431.6 6.8 %collective-permute-start.43 = (bf16[2,1,2,1,32,768]{5,4,3,2,1,0:T(8,128)(2,1)}, bf16[2,1,2,1,32,768]{5,4,3,2,1,0:T(8,128)(2,1)}, u32[]{:S(2)}, u32[]{:S(2)}) collective-permute-start(bf16[2,1,2,1,32,768]{5,4,3,2,1,0:T(8,128)(2,1)} %get-tuple-element.185), channel_id=1, source_target_pairs={{0,2},{2,0},{4,6},{6,4},{8,10},{10,8},{12,14},{14,12},{16,18},{18,... | collective-permute-start | bytes 589832 | tf_op jit(solution)/shard_map/ppermute | solution.py:586
  446.8 4.8 fusion.17
  464.6 10.1 %collective-permute-done.39 = bf16[2,1,2,2,64,768]{5,4,3,2,1,0:T(8,128)(2,1)S(1)} collective-permute-done((bf16[2,1,2,2,64,768]{5,4,3,2,1,0:T(8,128)(2,1)}, bf16[2,1,2,2,64,768]{5,4,3,2,1,0:T(8,128)(2,1)S(1)}, u32[]{:S(2)}, u32[]{:S(2)}) %collective-permute-start.39) | collective-permute-done | bytes 786464 | tf_op jit(solution)/shard_map/ppermute | solution.py:586
  479.9 6.6 %fusion.19 = f32[1024,1024]{1,0:T(8,128)S(1)} fusion(bf16[1024,1920]{1,0:T(8,128)(2,1)S(1)} %copy-done.14, bf16[2048,1920]{1,0:T(8,128)(2,1)} %get-tuple-element.189, s32[]{:T(128)S(6)} %select_n.259), kind=kOutput, calls=%fused_computation.46 | convolution fusion | flops 4026531840 | bytes 12058628 | tf_op jit(solution)/shard_map/dot_general | solution.py:29
  499.4 4.3 fusion.16
  505.3 2.9 collective-permute-start.62
  513.9 5.5 fusion.13
  528.5 4.9 collective-permute-done.53
  538.0 3.0 collective-permute-start.70
  541.8 2.9 collective-permute-start.67
  (426 shorter events, 162.4 us)
Async XLA Ops:
  7.2 195.6 %all-gather.2.cloned.1.call-start = ((), (), s32[]{:S(2)}) async-start(), calls=%async_computation.1 | async-start | bytes 6684672 | tf_op jit(solution)/shard_map/all_gather | solution.py:791
  9.2 16.2 %collective-permute-start.10 = (bf16[1,64,384]{2,1,0:T(8,128)(2,1)S(1)}, bf16[1,64,384]{2,1,0:T(8,128)(2,1)S(1)}, u32[]{:S(2)}, u32[]{:S(2)}) collective-permute-start(bf16[1,64,384]{2,1,0:T(8,128)(2,1)S(1)} %maximum_bitcast_fusion.1), channel_id=1, source_target_pairs={{0,16},{2,18},{4,20},{6,22},{8,24},{10,26},{12,28},{14,30},{16,0},... | collective-permute-start | bytes 147464 | tf_op jit(solution)/shard_map/ppermute | solution.py:586
  13.2 15.5 %collective-permute-start.1 = (bf16[1,64,768]{2,1,0:T(8,128)(2,1)}, bf16[1,64,768]{2,1,0:T(8,128)(2,1)S(1)}, u32[]{:S(2)}, u32[]{:S(2)}) collective-permute-start(bf16[1,64,768]{2,1,0:T(8,128)(2,1)} %bitcast.122), channel_id=1, source_target_pairs={{0,16},{2,18},{4,20},{6,22},{8,24},{10,26},{12,28},{14,30},{16,0},... | collective-permute-start | bytes 294920 | tf_op jit(solution)/shard_map/ppermute | solution.py:586
  13.3 16.2 %collective-permute-start.4 = (bf16[1,64,768]{2,1,0:T(8,128)(2,1)}, bf16[1,64,768]{2,1,0:T(8,128)(2,1)S(1)}, u32[]{:S(2)}, u32[]{:S(2)}) collective-permute-start(bf16[1,64,768]{2,1,0:T(8,128)(2,1)} %bitcast.126), channel_id=1, source_target_pairs={{0,16},{2,18},{4,20},{6,22},{8,24},{10,26},{12,28},{14,30},{16,0},... | collective-permute-start | bytes 294920 | tf_op jit(solution)/shard_map/ppermute | solution.py:586
  17.7 9.5 %collective-permute-start.7 = (bf16[1,64,384]{2,1,0:T(8,128)(2,1)S(1)}, bf16[1,64,384]{2,1,0:T(8,128)(2,1)S(1)}, u32[]{:S(2)}, u32[]{:S(2)}) collective-permute-start(bf16[1,64,384]{2,1,0:T(8,128)(2,1)S(1)} %fusion.83), channel_id=1, source_target_pairs={{0,16},{2,18},{4,20},{6,22},{8,24},{10,26},{12,28},{14,30},{16,0},... | collective-permute-start | bytes 147464 | tf_op jit(solution)/shard_map/ppermute | solution.py:586
  23.9 63.8 %collective-permute-start = (bf16[1024,1024]{1,0:T(8,128)(2,1)}, bf16[1024,1024]{1,0:T(8,128)(2,1)}, u32[]{:S(2)}, u32[]{:S(2)}) collective-permute-start(bf16[1024,1024]{1,0:T(8,128)(2,1)} %fusion.10), channel_id=1, source_target_pairs={{0,1},{1,0},{2,3},{3,2},{4,5},{5,4},{6,7},{7,6},{8,9},{9,8},{10,11... | collective-permute-start | bytes 6291464 | tf_op jit(solution)/shard_map/ppermute | solution.py:586
  31.8 9.7 %collective-permute-start.12 = (bf16[4,64,384]{2,1,0:T(8,128)(2,1)}, bf16[4,64,384]{2,1,0:T(8,128)(2,1)}, u32[]{:S(2)}, u32[]{:S(2)}) collective-permute-start(bf16[4,64,384]{2,1,0:T(8,128)(2,1)} %pad_maximum_fusion.18), channel_id=1, source_target_pairs={{0,8},{2,10},{4,12},{6,14},{8,0},{10,2},{12,4},{14,6},{16,24},{18,... | collective-permute-start | bytes 589832 | tf_op jit(solution)/shard_map/ppermute | solution.py:586
  36.1 10.8 %collective-permute-start.3 = (bf16[4,64,768]{2,1,0:T(8,128)(2,1)}, bf16[4,64,768]{2,1,0:T(8,128)(2,1)}, u32[]{:S(2)}, u32[]{:S(2)}) collective-permute-start(bf16[4,64,768]{2,1,0:T(8,128)(2,1)} %pad_maximum_fusion.8), channel_id=1, source_target_pairs={{0,4},{2,6},{4,0},{6,2},{8,12},{10,14},{12,8},{14,10},{16,20},{18,... | collective-permute-start | bytes 1179656 | tf_op jit(solution)/shard_map/ppermute | solution.py:586
  38.4 10.5 %collective-permute-start.6 = (bf16[4,64,768]{2,1,0:T(8,128)(2,1)}, bf16[4,64,768]{2,1,0:T(8,128)(2,1)}, u32[]{:S(2)}, u32[]{:S(2)}) collective-permute-start(bf16[4,64,768]{2,1,0:T(8,128)(2,1)} %pad_maximum_fusion.9), channel_id=1, source_target_pairs={{0,2},{2,0},{4,6},{6,4},{8,10},{10,8},{12,14},{14,12},{16,18},{18,... | collective-permute-start | bytes 1179656 | tf_op jit(solution)/shard_map/ppermute | solution.py:586
  50.8 22.5 %collective-permute-start.13 = (bf16[8,64,768]{2,1,0:T(8,128)(2,1)}, bf16[8,64,768]{2,1,0:T(8,128)(2,1)}, u32[]{:S(2)}, u32[]{:S(2)}) collective-permute-start(bf16[8,64,768]{2,1,0:T(8,128)(2,1)} %pad_maximum_fusion.5.refs_0_), channel_id=1, source_target_pairs={{0,2},{2,0},{4,6},{6,4},{8,10},{10,8},{12,14},{14,12},{16,18},{18,... | collective-permute-start | bytes 2359304 | tf_op jit(solution)/shard_map/ppermute | solution.py:586
  52.3 26.5 %collective-permute-start.14 = (bf16[8,64,768]{2,1,0:T(8,128)(2,1)}, bf16[8,64,768]{2,1,0:T(8,128)(2,1)}, u32[]{:S(2)}, u32[]{:S(2)}) collective-permute-start(bf16[8,64,768]{2,1,0:T(8,128)(2,1)} %pad_maximum_fusion.6.refs_2_), channel_id=1, source_target_pairs={{0,8},{2,10},{4,12},{6,14},{8,0},{10,2},{12,4},{14,6},{16,24},{18,... | collective-permute-start | bytes 2359304 | tf_op jit(solution)/shard_map/ppermute | solution.py:586
  53.1 12.4 %collective-permute-start.15 = (bf16[8,64,384]{2,1,0:T(8,128)(2,1)}, bf16[8,64,384]{2,1,0:T(8,128)(2,1)}, u32[]{:S(2)}, u32[]{:S(2)}) collective-permute-start(bf16[8,64,384]{2,1,0:T(8,128)(2,1)} %pad_maximum_fusion.10.refs_4_), channel_id=1, source_target_pairs={{0,4},{2,6},{4,0},{6,2},{8,12},{10,14},{12,8},{14,10},{16,20},{18,... | collective-permute-start | bytes 1179656 | tf_op jit(solution)/shard_map/ppermute | solution.py:586
  54.6 18.7 %collective-permute-start.16 = (bf16[8,64,384]{2,1,0:T(8,128)(2,1)}, bf16[8,64,384]{2,1,0:T(8,128)(2,1)}, u32[]{:S(2)}, u32[]{:S(2)}) collective-permute-start(bf16[8,64,384]{2,1,0:T(8,128)(2,1)} %pad_maximum_fusion.11.refs_6_), channel_id=1, source_target_pairs={{0,4},{2,6},{4,0},{6,2},{8,12},{10,14},{12,8},{14,10},{16,20},{18,... | collective-permute-start | bytes 1179656 | tf_op jit(solution)/shard_map/ppermute | solution.py:586
  55.2 497.7 %reduce-scatter.2.cloned.1.call-start = ((), (), s32[]{:S(2)}) async-start(), calls=%async_computation.2 | async-start | bytes 6684672 | tf_op jit(solution)/shard_map/reduce_scatter | solution.py:871
  97.0 14.2 %collective-permute-start.22 = (bf16[2,64,256]{2,1,0:T(8,128)(2,1)S(1)}, bf16[2,64,256]{2,1,0:T(8,128)(2,1)S(1)}, u32[]{:S(2)}, u32[]{:S(2)}) collective-permute-start(bf16[2,64,256]{2,1,0:T(8,128)(2,1)S(1)} %pad_maximum_fusion.26), channel_id=1, source_target_pairs={{0,2},{2,0},{4,6},{6,4},{8,10},{10,8},{12,14},{14,12},{16,18},{18,... | collective-permute-start | bytes 196616 | tf_op jit(solution)/shard_map/ppermute | solution.py:586
  97.0 14.2 %collective-permute-start.21 = (bf16[2,32,768]{2,1,0:T(8,128)(2,1)S(1)}, bf16[2,32,768]{2,1,0:T(8,128)(2,1)S(1)}, u32[]{:S(2)}, u32[]{:S(2)}) collective-permute-start(bf16[2,32,768]{2,1,0:T(8,128)(2,1)S(1)} %pad_maximum_fusion.25), channel_id=1, source_target_pairs={{0,4},{2,6},{4,0},{6,2},{8,12},{10,14},{12,8},{14,10},{16,20},{18,... | collective-permute-start | bytes 294920 | tf_op jit(solution)/shard_map/ppermute | solution.py:586
  98.4 12.8 %collective-permute-start.20 = (bf16[2,32,768]{2,1,0:T(8,128)(2,1)S(1)}, bf16[2,32,768]{2,1,0:T(8,128)(2,1)S(1)}, u32[]{:S(2)}, u32[]{:S(2)}) collective-permute-start(bf16[2,32,768]{2,1,0:T(8,128)(2,1)S(1)} %pad_maximum_fusion.24), channel_id=1, source_target_pairs={{0,8},{2,10},{4,12},{6,14},{8,0},{10,2},{12,4},{14,6},{16,24},{18,... | collective-permute-start | bytes 294920 | tf_op jit(solution)/shard_map/ppermute | solution.py:586
  111.3 28.2 %collective-permute-start.25 = (bf16[4,64,256]{2,1,0:T(8,128)(2,1)S(1)}, bf16[4,64,256]{2,1,0:T(8,128)(2,1)S(1)}, u32[]{:S(2)}, u32[]{:S(2)}) collective-permute-start(bf16[4,64,256]{2,1,0:T(8,128)(2,1)S(1)} %pad_maximum_fusion.21), channel_id=1, source_target_pairs={{0,8},{2,10},{4,12},{6,14},{8,0},{10,2},{12,4},{14,6},{16,24},{18,... | collective-permute-start | bytes 393224 | tf_op jit(solution)/shard_map/ppermute | solution.py:586
  112.2 28.1 %collective-permute-start.24 = (bf16[4,32,768]{2,1,0:T(8,128)(2,1)S(1)}, bf16[4,32,768]{2,1,0:T(8,128)(2,1)S(1)}, u32[]{:S(2)}, u32[]{:S(2)}) collective-permute-start(bf16[4,32,768]{2,1,0:T(8,128)(2,1)S(1)} %pad_maximum_fusion.20), channel_id=1, source_target_pairs={{0,2},{2,0},{4,6},{6,4},{8,10},{10,8},{12,14},{14,12},{16,18},{18,... | collective-permute-start | bytes 589832 | tf_op jit(solution)/shard_map/ppermute | solution.py:586
  114.2 26.9 %collective-permute-start.23 = (bf16[4,32,768]{2,1,0:T(8,128)(2,1)S(1)}, bf16[4,32,768]{2,1,0:T(8,128)(2,1)S(1)}, u32[]{:S(2)}, u32[]{:S(2)}) collective-permute-start(bf16[4,32,768]{2,1,0:T(8,128)(2,1)S(1)} %pad_maximum_fusion.19), channel_id=1, source_target_pairs={{0,4},{2,6},{4,0},{6,2},{8,12},{10,14},{12,8},{14,10},{16,20},{18,... | collective-permute-start | bytes 589832 | tf_op jit(solution)/shard_map/ppermute | solution.py:586
  141.9 34.2 %collective-permute-start.26 = (bf16[8,32,768]{2,1,0:T(8,128)(2,1)}, bf16[8,32,768]{2,1,0:T(8,128)(2,1)}, u32[]{:S(2)}, u32[]{:S(2)}) collective-permute-start(bf16[8,32,768]{2,1,0:T(8,128)(2,1)} %pad_maximum_fusion.12.refs_0_), channel_id=1, source_target_pairs={{0,2},{2,0},{4,6},{6,4},{8,10},{10,8},{12,14},{14,12},{16,18},{18,... | collective-permute-start | bytes 1179656 | tf_op jit(solution)/shard_map/ppermute | solution.py:586
  142.1 34.0 %collective-permute-start.27 = (bf16[8,32,768]{2,1,0:T(8,128)(2,1)}, bf16[8,32,768]{2,1,0:T(8,128)(2,1)}, u32[]{:S(2)}, u32[]{:S(2)}) collective-permute-start(bf16[8,32,768]{2,1,0:T(8,128)(2,1)} %pad_maximum_fusion.13.refs_2_), channel_id=1, source_target_pairs={{0,8},{2,10},{4,12},{6,14},{8,0},{10,2},{12,4},{14,6},{16,24},{18,... | collective-permute-start | bytes 1179656 | tf_op jit(solution)/shard_map/ppermute | solution.py:586
  143.4 32.6 %collective-permute-start.28 = (bf16[8,64,256]{2,1,0:T(8,128)(2,1)}, bf16[8,64,256]{2,1,0:T(8,128)(2,1)}, u32[]{:S(2)}, u32[]{:S(2)}) collective-permute-start(bf16[8,64,256]{2,1,0:T(8,128)(2,1)} %pad_maximum_fusion.14.refs_4_), channel_id=1, source_target_pairs={{0,4},{2,6},{4,0},{6,2},{8,12},{10,14},{12,8},{14,10},{16,20},{18,... | collective-permute-start | bytes 786440 | tf_op jit(solution)/shard_map/ppermute | solution.py:586
  182.2 17.6 %collective-permute-start.32 = (bf16[1024,1024]{1,0:T(8,128)(2,1)}, bf16[1024,1024]{1,0:T(8,128)(2,1)}, u32[]{:S(2)}, u32[]{:S(2)}) collective-permute-start(bf16[1024,1024]{1,0:T(8,128)(2,1)} %param.24), channel_id=1, source_target_pairs={{0,1},{1,0},{2,3},{3,2},{4,5},{5,4},{6,7},{7,6},{8,9},{9,8},{10,11... | collective-permute-start | bytes 6291464 | tf_op jit(solution)/shard_map/ppermute | solution.py:586
  242.9 23.1 %collective-permute-start.33 = (bf16[1024,1024]{1,0:T(8,128)(2,1)S(1)}, bf16[1024,1024]{1,0:T(8,128)(2,1)S(1)}, u32[]{:S(2)}, u32[]{:S(2)}) collective-permute-start(bf16[1024,1024]{1,0:T(8,128)(2,1)S(1)} %add_convert_fusion.1), channel_id=1, source_target_pairs={{0,1},{1,0},{2,3},{3,2},{4,5},{5,4},{6,7},{7,6},{8,9},{9,8},{10,11... | collective-permute-start | bytes 6291464 | tf_op jit(solution)/shard_map/ppermute | solution.py:586
  247.2 43.7 %collective-permute-start.31 = (bf16[1024,1024]{1,0:T(8,128)(2,1)}, bf16[1024,1024]{1,0:T(8,128)(2,1)}, u32[]{:S(2)}, u32[]{:S(2)}) collective-permute-start(bf16[1024,1024]{1,0:T(8,128)(2,1)} %fusion.37), channel_id=1, source_target_pairs={{0,1},{1,0},{2,3},{3,2},{4,5},{5,4},{6,7},{7,6},{8,9},{9,8},{10,11... | collective-permute-start | bytes 6291464 | tf_op jit(solution)/shard_map/ppermute | solution.py:586
  276.9 21.8 %collective-permute-start.34 = (bf16[1024,1024]{1,0:T(8,128)(2,1)}, bf16[1024,1024]{1,0:T(8,128)(2,1)}, u32[]{:S(2)}, u32[]{:S(2)}) collective-permute-start(bf16[1024,1024]{1,0:T(8,128)(2,1)} %get-tuple-element.328), channel_id=1, source_target_pairs={{0,1},{1,0},{2,3},{3,2},{4,5},{5,4},{6,7},{7,6},{8,9},{9,8},{10,11... | collective-permute-start | bytes 6291464 | tf_op jit(solution)/shard_map/ppermute | solution.py:586
  315.5 44.4 %collective-permute-start.37 = (bf16[2,2,1,2,64,256]{5,4,3,2,1,0:T(8,128)(2,1)S(1)}, bf16[2,2,1,2,64,256]{5,4,3,2,1,0:T(8,128)(2,1)S(1)}, u32[]{:S(2)}, u32[]{:S(2)}) collective-permute-start(bf16[2,2,1,2,64,256]{5,4,3,2,1,0:T(8,128)(2,1)S(1)} %get-tuple-element.167), channel_id=1, source_target_pairs={{0,4},{2,6},{4,0},{6,2},{8,12},{10,14},{12,8},{14,10},{16,20},{18,... | collective-permute-start | bytes 786440 | tf_op jit(solution)/shard_map/ppermute | solution.py:586
  316.4 44.5 %collective-permute-start.36 = (bf16[2,1,2,2,32,768]{5,4,3,2,1,0:T(8,128)(2,1)S(1)}, bf16[2,1,2,2,32,768]{5,4,3,2,1,0:T(8,128)(2,1)S(1)}, u32[]{:S(2)}, u32[]{:S(2)}) collective-permute-start(bf16[2,1,2,2,32,768]{5,4,3,2,1,0:T(8,128)(2,1)S(1)} %get-tuple-element.165), channel_id=1, source_target_pairs={{0,8},{2,10},{4,12},{6,14},{8,0},{10,2},{12,4},{14,6},{16,24},{18,... | collective-permute-start | bytes 1179656 | tf_op jit(solution)/shard_map/ppermute | solution.py:586
  317.0 44.7 %collective-permute-start.35 = (bf16[2,2,2,1,32,768]{5,4,3,2,1,0:T(8,128)(2,1)S(1)}, bf16[2,2,2,1,32,768]{5,4,3,2,1,0:T(8,128)(2,1)S(1)}, u32[]{:S(2)}, u32[]{:S(2)}) collective-permute-start(bf16[2,2,2,1,32,768]{5,4,3,2,1,0:T(8,128)(2,1)S(1)} %get-tuple-element.163), channel_id=1, source_target_pairs={{0,2},{2,0},{4,6},{6,4},{8,10},{10,8},{12,14},{14,12},{16,18},{18,... | collective-permute-start | bytes 1179656 | tf_op jit(solution)/shard_map/ppermute | solution.py:586
  429.7 27.0 %collective-permute-start.44 = (bf16[2,1,1,2,64,256]{5,4,3,2,1,0:T(8,128)(2,1)}, bf16[2,1,1,2,64,256]{5,4,3,2,1,0:T(8,128)(2,1)}, u32[]{:S(2)}, u32[]{:S(2)}) collective-permute-start(bf16[2,1,1,2,64,256]{5,4,3,2,1,0:T(8,128)(2,1)} %get-tuple-element.187), channel_id=1, source_target_pairs={{0,8},{2,10},{4,12},{6,14},{8,0},{10,2},{12,4},{14,6},{16,24},{18,... | collective-permute-start | bytes 393224 | tf_op jit(solution)/shard_map/ppermute | solution.py:586
  431.6 28.0 %collective-permute-start.43 = (bf16[2,1,2,1,32,768]{5,4,3,2,1,0:T(8,128)(2,1)}, bf16[2,1,2,1,32,768]{5,4,3,2,1,0:T(8,128)(2,1)}, u32[]{:S(2)}, u32[]{:S(2)}) collective-permute-start(bf16[2,1,2,1,32,768]{5,4,3,2,1,0:T(8,128)(2,1)} %get-tuple-element.185), channel_id=1, source_target_pairs={{0,2},{2,0},{4,6},{6,4},{8,10},{10,8},{12,14},{14,12},{16,18},{18,... | collective-permute-start | bytes 589832 | tf_op jit(solution)/shard_map/ppermute | solution.py:586
  438.4 22.3 %collective-permute-start.42 = (bf16[2,2,1,1,32,768]{5,4,3,2,1,0:T(8,128)(2,1)}, bf16[2,2,1,1,32,768]{5,4,3,2,1,0:T(8,128)(2,1)}, u32[]{:S(2)}, u32[]{:S(2)}) collective-permute-start(bf16[2,2,1,1,32,768]{5,4,3,2,1,0:T(8,128)(2,1)} %get-tuple-element.183), channel_id=1, source_target_pairs={{0,4},{2,6},{4,0},{6,2},{8,12},{10,14},{12,8},{14,10},{16,20},{18,... | collective-permute-start | bytes 589832 | tf_op jit(solution)/shard_map/ppermute | solution.py:586
  444.7 17.3 %collective-permute-start.41 = (bf16[2,2,1,2,64,384]{5,4,3,2,1,0:T(8,128)(2,1)}, bf16[2,2,1,2,64,384]{5,4,3,2,1,0:T(8,128)(2,1)}, u32[]{:S(2)}, u32[]{:S(2)}) collective-permute-start(bf16[2,2,1,2,64,384]{5,4,3,2,1,0:T(8,128)(2,1)} %get-tuple-element.181), channel_id=1, source_target_pairs={{0,4},{2,6},{4,0},{6,2},{8,12},{10,14},{12,8},{14,10},{16,20},{18,... | collective-permute-start | bytes 1179656 | tf_op jit(solution)/shard_map/ppermute | solution.py:586
  446.6 16.8 %collective-permute-start.40 = (bf16[2,2,1,2,64,384]{5,4,3,2,1,0:T(8,128)(2,1)}, bf16[2,2,1,2,64,384]{5,4,3,2,1,0:T(8,128)(2,1)}, u32[]{:S(2)}, u32[]{:S(2)}) collective-permute-start(bf16[2,2,1,2,64,384]{5,4,3,2,1,0:T(8,128)(2,1)} %get-tuple-element.179), channel_id=1, source_target_pairs={{0,4},{2,6},{4,0},{6,2},{8,12},{10,14},{12,8},{14,10},{16,20},{18,... | collective-permute-start | bytes 1179656 | tf_op jit(solution)/shard_map/ppermute | solution.py:586
  456.6 18.1 %collective-permute-start.39 = (bf16[2,1,2,2,64,768]{5,4,3,2,1,0:T(8,128)(2,1)}, bf16[2,1,2,2,64,768]{5,4,3,2,1,0:T(8,128)(2,1)S(1)}, u32[]{:S(2)}, u32[]{:S(2)}) collective-permute-start(bf16[2,1,2,2,64,768]{5,4,3,2,1,0:T(8,128)(2,1)} %get-tuple-element.177), channel_id=1, source_target_pairs={{0,8},{2,10},{4,12},{6,14},{8,0},{10,2},{12,4},{14,6},{16,24},{18,... | collective-permute-start | bytes 2359304 | tf_op jit(solution)/shard_map/ppermute | solution.py:586
  459.6 17.7 %collective-permute-start.38 = (bf16[2,2,2,1,64,768]{5,4,3,2,1,0:T(8,128)(2,1)}, bf16[2,2,2,1,64,768]{5,4,3,2,1,0:T(8,128)(2,1)S(1)}, u32[]{:S(2)}, u32[]{:S(2)}) collective-permute-start(bf16[2,2,2,1,64,768]{5,4,3,2,1,0:T(8,128)(2,1)} %get-tuple-element.175), channel_id=1, source_target_pairs={{0,2},{2,0},{4,6},{6,4},{8,10},{10,8},{12,14},{14,12},{16,18},{18,... | collective-permute-start | bytes 2359304 | tf_op jit(solution)/shard_map/ppermute | solution.py:586
  460.7 38.7 %collective-permute-start.45 = (bf16[1024,1024]{1,0:T(8,128)(2,1)}, bf16[1024,1024]{1,0:T(8,128)(2,1)S(1)}, u32[]{:S(2)}, u32[]{:S(2)}) collective-permute-start(bf16[1024,1024]{1,0:T(8,128)(2,1)} %add_convert_fusion), channel_id=1, source_target_pairs={{0,1},{1,0},{2,3},{3,2},{4,5},{5,4},{6,7},{7,6},{8,9},{9,8},{10,11... | collective-permute-start | bytes 6291464 | tf_op jit(solution)/shard_map/ppermute | solution.py:586
  477.5 9.7 %collective-permute-start.52 = (bf16[2,1,1,1,64,256]{5,4,3,2,1,0:T(8,128)(2,1)S(1)}, bf16[2,1,1,1,64,256]{5,4,3,2,1,0:T(8,128)(2,1)S(1)}, u32[]{:S(2)}, u32[]{:S(2)}) collective-permute-start(bf16[2,1,1,1,64,256]{5,4,3,2,1,0:T(8,128)(2,1)S(1)} %constant_dynamic-slice_fusion.11), channel_id=1, source_target_pairs={{0,2},{2,0},{4,6},{6,4},{8,10},{10,8},{12,14},{14,12},{16,18},{18,... | collective-permute-start | bytes 196616 | tf_op jit(solution)/shard_map/ppermute | solution.py:586
  477.8 11.1 %collective-permute-start.51 = (bf16[2,1,1,1,32,768]{5,4,3,2,1,0:T(8,128)(2,1)S(1)}, bf16[2,1,1,1,32,768]{5,4,3,2,1,0:T(8,128)(2,1)S(1)}, u32[]{:S(2)}, u32[]{:S(2)}) collective-permute-start(bf16[2,1,1,1,32,768]{5,4,3,2,1,0:T(8,128)(2,1)S(1)} %constant_dynamic-slice_fusion.12), channel_id=1, source_target_pairs={{0,4},{2,6},{4,0},{6,2},{8,12},{10,14},{12,8},{14,10},{16,20},{18,... | collective-permute-start | bytes 294920 | tf_op jit(solution)/shard_map/ppermute | solution.py:586
  478.2 13.3 %collective-permute-start.50 = (bf16[2,1,1,1,32,768]{5,4,3,2,1,0:T(8,128)(2,1)S(1)}, bf16[2,1,1,1,32,768]{5,4,3,2,1,0:T(8,128)(2,1)S(1)}, u32[]{:S(2)}, u32[]{:S(2)}) collective-permute-start(bf16[2,1,1,1,32,768]{5,4,3,2,1,0:T(8,128)(2,1)S(1)} %constant_dynamic-slice_fusion.13), channel_id=1, source_target_pairs={{0,8},{2,10},{4,12},{6,14},{8,0},{10,2},{12,4},{14,6},{16,24},{18,... | collective-permute-start | bytes 294920 | tf_op jit(solution)/shard_map/ppermute | solution.py:586
  504.6 14.7 %collective-permute-start.60 = (f32[6180]{0:T(1024)S(1)}, f32[6180]{0:T(1024)S(1)}, u32[]{:S(2)}, u32[]{:S(2)}) collective-permute-start(f32[6180]{0:T(1024)S(1)} %concatenate.139), channel_id=1, source_target_pairs={{0,2},{2,0},{4,6},{6,4},{8,10},{10,8},{12,14},{14,12},{16,18},{18,... | collective-permute-start | bytes 74168 | tf_op jit(solution)/shard_map/ppermute | solution.py:586
  504.9 15.8 %collective-permute-start.61 = (f32[6180]{0:T(1024)S(1)}, f32[6180]{0:T(1024)S(1)}, u32[]{:S(2)}, u32[]{:S(2)}) collective-permute-start(f32[6180]{0:T(1024)S(1)} %concatenate.139), channel_id=1, source_target_pairs={{0,4},{2,6},{4,0},{6,2},{8,12},{10,14},{12,8},{14,10},{16,20},{18,... | collective-permute-start | bytes 74168 | tf_op jit(solution)/shard_map/ppermute | solution.py:586
  505.3 17.2 %collective-permute-start.62 = (f32[6180]{0:T(1024)S(1)}, f32[6180]{0:T(1024)S(1)}, u32[]{:S(2)}, u32[]{:S(2)}) collective-permute-start(f32[6180]{0:T(1024)S(1)} %concatenate.139), channel_id=1, source_target_pairs={{0,6},{2,4},{4,2},{6,0},{8,14},{10,12},{12,10},{14,8},{16,22},{18,... | collective-permute-start | bytes 74168 | tf_op jit(solution)/shard_map/ppermute | solution.py:586
  508.2 14.6 %collective-permute-start.59 = (bf16[1,1,1,1,64,256]{5,4,3,2,1,0:T(8,128)(2,1)S(1)}, bf16[1,1,1,1,64,256]{5,4,3,2,1,0:T(8,128)(2,1)S(1)}, u32[]{:S(2)}, u32[]{:S(2)}) collective-permute-start(bf16[1,1,1,1,64,256]{5,4,3,2,1,0:T(8,128)(2,1)S(1)} %constant_dynamic-slice_fusion.4), channel_id=1, source_target_pairs={{0,16},{2,18},{4,20},{6,22},{8,24},{10,26},{12,28},{14,30},{16,0},... | collective-permute-start | bytes 98312 | tf_op jit(solution)/shard_map/ppermute | solution.py:586
  510.2 14.8 %collective-permute-start.58 = (bf16[1,1,1,1,32,768]{5,4,3,2,1,0:T(8,128)(2,1)S(1)}, bf16[1,1,1,1,32,768]{5,4,3,2,1,0:T(8,128)(2,1)S(1)}, u32[]{:S(2)}, u32[]{:S(2)}) collective-permute-start(bf16[1,1,1,1,32,768]{5,4,3,2,1,0:T(8,128)(2,1)S(1)} %constant_dynamic-slice_fusion.5), channel_id=1, source_target_pairs={{0,16},{2,18},{4,20},{6,22},{8,24},{10,26},{12,28},{14,30},{16,0},... | collective-permute-start | bytes 147464 | tf_op jit(solution)/shard_map/ppermute | solution.py:586
  537.9 12.3 %collective-permute-start.71 = (bf16[1,1,1,1,64,768]{5,4,3,2,1,0:T(8,128)(2,1)S(1)}, bf16[1,1,1,1,64,768]{5,4,3,2,1,0:T(8,128)(2,1)S(1)}, u32[]{:S(2)}, u32[]{:S(2)}) collective-permute-start(bf16[1,1,1,1,64,768]{5,4,3,2,1,0:T(8,128)(2,1)S(1)} %constant_dynamic-slice_fusion), channel_id=1, source_target_pairs={{0,16},{2,18},{4,20},{6,22},{8,24},{10,26},{12,28},{14,30},{16,0},... | collective-permute-start | bytes 294920 | tf_op jit(solution)/shard_map/ppermute | solution.py:586
  538.0 12.9 %collective-permute-start.70 = (bf16[1,1,1,1,64,768]{5,4,3,2,1,0:T(8,128)(2,1)S(1)}, bf16[1,1,1,1,64,768]{5,4,3,2,1,0:T(8,128)(2,1)S(1)}, u32[]{:S(2)}, u32[]{:S(2)}) collective-permute-start(bf16[1,1,1,1,64,768]{5,4,3,2,1,0:T(8,128)(2,1)S(1)} %constant_dynamic-slice_fusion.1), channel_id=1, source_target_pairs={{0,16},{2,18},{4,20},{6,22},{8,24},{10,26},{12,28},{14,30},{16,0},... | collective-permute-start | bytes 294920 | tf_op jit(solution)/shard_map/ppermute | solution.py:586
  (91 other events, 1435.0 us)
Sparse Core Ops, SparseCore 0:
  55.4 106.5 all-gather.1
  291.1 155.6 reduce-scatter.1
